TPU v7x, 32 devices: a whole 2x2x4 slice. The times are simulated.
32 devices in a mesh: groups: 2 (over x), dev: 16 (over z, y, core).
Axes of the slice: x: 2, y: 2, z: 4, core: 2. Of those that a mesh axis runs over, the one named last changes fastest.
Arguments:
- queries: bfloat16 [2, 32, 128, 1024], P(None, ('groups', 'dev')), parts along dimension 1, may hold values from -180 to 180
- keys_values: bfloat16 [2, 32, 2, 1664, 128], P(None, ('groups', 'dev')), parts along dimension 1, may hold values from -6 to 6
- residual: bfloat16 [2, 2048, 2048], P(None, ('groups', 'dev')), parts along dimension 1, may hold values from -6 to 6
- norm_gain: float32 [2048], replicated, may hold values from 0.1 to 1.9
- gate_up: bfloat16 [16, 2048, 1536], P('dev'), may hold values from -0.125 to 0.125
- down_proj: bfloat16 [16, 768, 2048], P('dev'), may hold values from -0.21875 to 0.21875
- expert_ids: int32 [2, 2048, 8], P(None, ('groups', 'dev')), parts along dimension 1, may hold values from 0 to 15, all different within a row; in each aligned block of 64 rows (0 to 63, 64 to 127, ..., all dimensions but the last counted through in order) at most 40 rows name the same one
- expert_gates: int32 [2, 2048, 8], P(None, ('groups', 'dev')), parts along dimension 1, may hold values from 1 to 1023
Outputs:
- layer_out: bfloat16 [2, 2048, 2048], P(None, ('groups', 'dev')), parts along dimension 1
There are 2 independent parts, one for each index of `groups`. A program takes and returns all parts, laid end to end along the dimension named above; an argument that names none is the same for every part. Nothing has to cross between parts.
Inputs may be any that keep to these rules, and one draw needn't show every extreme that they name: `expert_ids`: in each micro-batch and each aligned block of 64 rows (the tokens of one device), no expert is named by more than 40 rows, a bound that some block reaches; the 8 experts of a row differ.
All inputs are finite; a program needn't handle non-finite values.
Results may differ from a plain program's by a relative error of at most 0.0039.
Values may be sent and summed in bfloat16 or wider, within the bound.
No kernel may reach another device: no remote copies, remote signals or barrier semaphores. Data moves between devices by JAX's collectives and lax.ppermute only.
A program may use at most 128 MiB of HBM per device.

v0:
```python
import math

import jax
import jax.numpy as jnp
from jax import lax
from jax.sharding import PartitionSpec as P


def attend(query_rows, cached_pairs):
    batches, length, feat_width = query_rows.shape
    context = cached_pairs.shape[2]
    head_size = cached_pairs.shape[3]
    groups = feat_width // head_size
    head_rows = query_rows.reshape(batches, length, groups, head_size)
    scores = jnp.einsum(
        "mqgd,mkd->mgqk", head_rows, cached_pairs[:, 0], preferred_element_type=jnp.float32
    ) / math.sqrt(head_size)
    query_pos = context - length + lax.broadcasted_iota(jnp.int32, (length, context), 0)
    key_pos = lax.broadcasted_iota(jnp.int32, (length, context), 1)
    allowed = key_pos <= query_pos
    scores = jnp.where(allowed, scores, -1e30)
    highest = jnp.max(scores, axis=-1, keepdims=True)
    scaled_exp = jnp.where(allowed, jnp.exp(scores - highest), 0.0)
    totals = jnp.sum(scaled_exp, axis=-1, keepdims=True)
    weights = (scaled_exp / totals).astype(jnp.bfloat16)
    blended = jnp.einsum(
        "mgqk,mkd->mqgd", weights, cached_pairs[:, 1], preferred_element_type=jnp.float32
    )
    return blended.astype(jnp.bfloat16).reshape(batches, length, feat_width)


def to_owners(exchanged, kv_heads):
    batches, sources, positions, feat_width = exchanged.shape
    grouped = exchanged.reshape(batches, sources // kv_heads, kv_heads, positions, feat_width)
    grouped = jnp.transpose(grouped, (0, 1, 3, 2, 4))
    return grouped.reshape(batches, sources // kv_heads * positions, kv_heads * feat_width)


def prepare(attn_rows, residual, norm_gain, expert_ids, expert_gates, experts, capacity):
    stream = residual.astype(jnp.float32) + attn_rows.astype(jnp.float32)
    meansq = jnp.mean(stream * stream, axis=-1, keepdims=True)
    normed = (stream * lax.rsqrt(meansq + 1e-06) * norm_gain).astype(jnp.bfloat16)
    batches, rows_count, top_count = expert_ids.shape
    flat_ids = expert_ids.reshape(batches, rows_count * top_count)
    one_hot = (flat_ids[:, :, None] == jnp.arange(experts, dtype=jnp.int32)).astype(jnp.int32)
    ranking = jnp.sum((jnp.cumsum(one_hot, axis=1) - one_hot) * one_hot, axis=-1)
    target = flat_ids * capacity + ranking
    buffer_rows = jnp.arange(experts * capacity, dtype=jnp.int32)
    chosen = target.reshape(batches, 1, rows_count, top_count) == buffer_rows[None, :, None, None]
    selector = jnp.any(chosen, axis=-1).astype(jnp.bfloat16)
    outgoing = jnp.einsum(
        "mrt,mtd->mrd", selector, normed, preferred_element_type=jnp.float32
    ).astype(jnp.bfloat16)
    shares = expert_gates.astype(jnp.float32)
    shares = shares / jnp.sum(shares, axis=-1, keepdims=True)
    return (stream, outgoing, target, shares)


def run_experts(arrived, gate_up, down_proj):
    batches, sources, slot_count, model_width = arrived.shape
    local_count = gate_up.shape[0]
    hidden_width = down_proj.shape[1]
    per_expert = arrived.reshape(
        batches, sources, local_count, slot_count // local_count, model_width
    )
    rows_in = per_expert[:, :, 0].reshape(-1, model_width)
    projected = jnp.dot(rows_in, gate_up[0], preferred_element_type=jnp.float32)
    hidden = (jax.nn.silu(projected[:, :hidden_width]) * projected[:, hidden_width:]).astype(
        jnp.bfloat16
    )
    output = jnp.dot(hidden, down_proj[0], preferred_element_type=jnp.float32).astype(jnp.bfloat16)
    results = output.reshape(batches, sources, 1, slot_count // local_count, model_width)
    finished = results.reshape(batches, sources, slot_count, model_width)
    return lax.all_to_all(finished, "dev", split_axis=1, concat_axis=1, tiled=True)


def combine(came_back, target, shares, stream):
    batches, sources, slot_count, model_width = came_back.shape
    flat_back = came_back.reshape(batches, sources * slot_count, model_width)
    picked = jnp.take_along_axis(flat_back, target[:, :, None], axis=1)
    picked = picked.reshape(batches, shares.shape[1], shares.shape[2], model_width)
    summed = jnp.sum(shares[..., None] * picked.astype(jnp.float32), axis=2)
    return (stream + summed).astype(jnp.bfloat16)


def body(queries, keys_values, residual, norm_gain, gate_up, down_proj, expert_ids, expert_gates):
    devices = lax.axis_size("dev")
    model_width = residual.shape[2]
    kv_heads = model_width // queries.shape[3]
    experts = devices * gate_up.shape[0]
    capacity = 5 * residual.shape[1] * expert_ids.shape[2] // (4 * experts)
    own_query = queries[:, 0]
    own_pairs = keys_values[:, 0]
    batches, length, feat_width = own_query.shape
    positions = length // devices
    pieces = []
    for batch_index in range(batches):
        window = slice(batch_index, batch_index + 1)
        blended_heads = attend(own_query[window], own_pairs[window])
        outgoing_rows = blended_heads.reshape(1, devices, positions, feat_width)
        arrived_rows = lax.all_to_all(outgoing_rows, "dev", split_axis=1, concat_axis=1, tiled=True)
        attn_rows = to_owners(arrived_rows, kv_heads)
        stream, dispatched, target, shares = prepare(
            attn_rows,
            residual[window],
            norm_gain,
            expert_ids[window],
            expert_gates[window],
            experts,
            capacity,
        )
        shaped = dispatched.reshape(1, devices, -1, model_width)
        came_back = run_experts(
            lax.all_to_all(shaped, "dev", split_axis=1, concat_axis=1, tiled=True),
            gate_up,
            down_proj,
        )
        pieces.append(combine(came_back, target, shares, stream))
    return jnp.concatenate(pieces, axis=0)


def solution(mesh):
    in_specs = (
        P(None, ("groups", "dev"), None, None),
        P(None, ("groups", "dev"), None, None, None),
        P(None, ("groups", "dev"), None),
        P(),
        P("dev", None, None),
        P("dev", None, None),
        P(None, ("groups", "dev"), None),
        P(None, ("groups", "dev"), None),
    )
    out_specs = P(None, ("groups", "dev"), None)
    return jax.shard_map(body, mesh=mesh, in_specs=in_specs, out_specs=out_specs, check_vma=False)
```

profile of v0, /device:TPU:15, one launch (start us, length us, event | category | flops | bytes accessed | tf_op | source)
XLA Modules:
  0.0 325.3 jit_solution(3495001670778187816)
XLA Ops:
  0.2 2.9 slice_bitcast_fusion
  9.7 2.8 fusion.6
  14.2 2.6 fusion.26
  19.4 6.6 %all-to-all-start.3 = ((bf16[1,16,8,1024]{3,2,0,1:T(8,128)(2,1)}), bf16[1,16,8,1024]{3,2,0,1:T(8,128)(2,1)}, u32[]{:S(2)}, u32[]{:S(2)}) async-start(bf16[1,16,8,1024]{3,2,0,1:T(8,128)(2,1)} %bitcast.227), calls=%async_computation.3 | async-start | bytes 524288 | tf_op jit(solution)/shard_map/all_to_all | solution.py:101
  26.0 5.5 %fusion.29 = bf16[1,128,8,128]{3,1,2,0:T(8,128)(2,1)S(1)} fusion(f32[8,128]{1,0:T(8,128)S(1)} %get-tuple-element.8, f32[8,128]{1,0:T(8,128)S(1)} %get-tuple-element.26, f32[1664,128,8]{1,0,2:T(8,128)} %copy-done.1, pred[128,1664]{0,1:T(8,128)(4,1)S(1)} %iota_compare_fusion.2, bf16[1,2,1664,128]{3,2,1,0:T(8,128)(2,1)} %get-tuple-element.17), kind=kOutput, calls=%fused_computation.43 | convolution fusion | flops 446562304 | bytes 7725056 | tf_op jit(solution)/shard_map/mgqk,mkd->mqgd/dot_general | solution.py:26
  34.1 6.0 %all-to-all-start = ((bf16[1,16,8,1024]{3,2,0,1:T(8,128)(2,1)}), bf16[1,16,8,1024]{3,2,0,1:T(8,128)(2,1)S(1)}, u32[]{:S(2)}, u32[]{:S(2)}) async-start(bf16[1,16,8,1024]{3,2,0,1:T(8,128)(2,1)} %bitcast.226), calls=%async_computation | async-start | bytes 524288 | tf_op jit(solution)/shard_map/all_to_all | solution.py:101
  42.8 5.3 %all-to-all-done = bf16[1,16,8,1024]{3,2,0,1:T(8,128)(2,1)S(1)} async-done(((bf16[1,16,8,1024]{3,2,0,1:T(8,128)(2,1)}), bf16[1,16,8,1024]{3,2,0,1:T(8,128)(2,1)S(1)}, u32[]{:S(2)}, u32[]{:S(2)}) %all-to-all-start) | async-done | bytes 262176 | tf_op jit(solution)/shard_map/all_to_all | solution.py:101
  50.5 3.6 %convolution_convert_fusion.2 = bf16[640,2048]{1,0:T(8,128)(2,1)} fusion(pred[640,64]{0,1:T(8,128)(4,1)S(1)} %fusion.19, f32[64]{0:T(128)S(1)} %get-tuple-element.29, f32[2048]{0:T(1024)S(1)} %copy-done.10, f32[1,64,2048]{2,1,0:T(8,128)} %bitcast.217, bf16[2,64,2048]{2,1,0:T(8,128)(2,1)} %param.12), kind=kOutput, calls=%fused_computation.26 | convolution fusion | flops 169738240 | bytes 3457280 | tf_op jit(solution)/shard_map/mrt,mtd->mrd/dot_general | solution.py:51
  54.0 6.4 %all-to-all-start.4 = ((bf16[1,16,40,2048]{3,2,0,1:T(8,128)(2,1)}), bf16[1,16,40,2048]{3,2,0,1:T(8,128)(2,1)}, u32[]{:S(2)}, u32[]{:S(2)}) async-start(bf16[1,16,40,2048]{3,2,0,1:T(8,128)(2,1)} %bitcast.214), calls=%async_computation.4 | async-start | bytes 5242880 | tf_op jit(solution)/shard_map/all_to_all | solution.py:114
  62.9 3.5 %convolution_convert_fusion.3 = bf16[640,2048]{1,0:T(8,128)(2,1)} fusion(pred[640,64]{0,1:T(8,128)(4,1)S(1)} %fusion.18, f32[2048]{0:T(1024)S(1)} %copy-done.10, f32[64]{0:T(128)S(1)} %get-tuple-element.30, f32[1,64,2048]{2,1,0:T(8,128)} %bitcast.220, bf16[2,64,2048]{2,1,0:T(8,128)(2,1)} %param.12), kind=kOutput, calls=%fused_computation.27 | convolution fusion | flops 169738240 | bytes 3457280 | tf_op jit(solution)/shard_map/mrt,mtd->mrd/dot_general | solution.py:51
  66.4 52.8 %all-to-all-done.4 = bf16[1,16,40,2048]{3,2,0,1:T(8,128)(2,1)} async-done(((bf16[1,16,40,2048]{3,2,0,1:T(8,128)(2,1)}), bf16[1,16,40,2048]{3,2,0,1:T(8,128)(2,1)}, u32[]{:S(2)}, u32[]{:S(2)}) %all-to-all-start.4) | async-done | bytes 2621472 | tf_op jit(solution)/shard_map/all_to_all | solution.py:114
  119.2 4.9 %all-to-all-start.1 = ((bf16[1,16,40,2048]{3,2,0,1:T(8,128)(2,1)}), bf16[1,16,40,2048]{3,2,0,1:T(8,128)(2,1)}, u32[]{:S(2)}, u32[]{:S(2)}) async-start(bf16[1,16,40,2048]{3,2,0,1:T(8,128)(2,1)} %bitcast.215), calls=%async_computation.1 | async-start | bytes 5242880 | tf_op jit(solution)/shard_map/all_to_all | solution.py:114
  124.1 7.1 %fusion = f32[640,1536]{1,0:T(8,128)S(1)} fusion(bf16[640,2048]{1,0:T(8,128)(2,1)} %bitcast.67, bf16[1,2048,1536]{2,1,0:T(8,128)(2,1)} %param.14), kind=kOutput, calls=%fused_computation.8 | convolution fusion | flops 4026531840 | bytes 12845056 | tf_op jit(solution)/shard_map/dot_general | solution.py:67
  131.2 3.8 %convolution_convert_fusion = bf16[640,2048]{1,0:T(8,128)(2,1)} fusion(bf16[1,768,2048]{2,1,0:T(8,128)(2,1)S(1)} %copy-done, f32[640,1536]{1,0:T(8,128)S(1)} %fusion), kind=kOutput, calls=%fused_computation.24 | convolution fusion | flops 2017525760 | bytes 9699328 | tf_op jit(solution)/shard_map/dot_general | solution.py:71
  135.0 47.8 %all-to-all-done.1 = bf16[1,16,40,2048]{3,2,0,1:T(8,128)(2,1)} async-done(((bf16[1,16,40,2048]{3,2,0,1:T(8,128)(2,1)}), bf16[1,16,40,2048]{3,2,0,1:T(8,128)(2,1)}, u32[]{:S(2)}, u32[]{:S(2)}) %all-to-all-start.1) | async-done | bytes 2621472 | tf_op jit(solution)/shard_map/all_to_all | solution.py:114
  182.8 4.9 %all-to-all-start.5 = ((bf16[1,16,40,2048]{3,2,0,1:T(8,128)(2,1)}), bf16[1,16,40,2048]{3,2,0,1:T(8,128)(2,1)}, u32[]{:S(2)}, u32[]{:S(2)}) async-start(bf16[1,16,40,2048]{3,2,0,1:T(8,128)(2,1)} %bitcast.223), calls=%async_computation.5 | async-start | bytes 5242880 | tf_op jit(solution)/shard_map/all_to_all | solution.py:74
  187.7 7.1 %fusion.2 = f32[640,1536]{1,0:T(8,128)S(1)} fusion(bf16[640,2048]{1,0:T(8,128)(2,1)} %bitcast.28, bf16[1,2048,1536]{2,1,0:T(8,128)(2,1)} %param.14), kind=kOutput, calls=%fused_computation.10 | convolution fusion | flops 4026531840 | bytes 12845056 | tf_op jit(solution)/shard_map/dot_general | solution.py:67
  194.9 3.8 %convolution_convert_fusion.1 = bf16[640,2048]{1,0:T(8,128)(2,1)} fusion(bf16[1,768,2048]{2,1,0:T(8,128)(2,1)S(1)} %copy-done, f32[640,1536]{1,0:T(8,128)S(1)} %fusion.2), kind=kOutput, calls=%fused_computation.25 | convolution fusion | flops 2017525760 | bytes 9699328 | tf_op jit(solution)/shard_map/dot_general | solution.py:71
  198.6 47.9 %all-to-all-done.5 = bf16[1,16,40,2048]{3,2,0,1:T(8,128)(2,1)} async-done(((bf16[1,16,40,2048]{3,2,0,1:T(8,128)(2,1)}), bf16[1,16,40,2048]{3,2,0,1:T(8,128)(2,1)}, u32[]{:S(2)}, u32[]{:S(2)}) %all-to-all-start.5) | async-done | bytes 2621472 | tf_op jit(solution)/shard_map/all_to_all | solution.py:74
  246.5 4.9 %all-to-all-start.2 = ((bf16[1,16,40,2048]{3,2,0,1:T(8,128)(2,1)}), bf16[1,16,40,2048]{3,2,0,1:T(8,128)(2,1)}, u32[]{:S(2)}, u32[]{:S(2)}) async-start(bf16[1,16,40,2048]{3,2,0,1:T(8,128)(2,1)} %bitcast.222), calls=%async_computation.2 | async-start | bytes 5242880 | tf_op jit(solution)/shard_map/all_to_all | solution.py:74
  251.9 7.4 %gather_fusion.1 = bf16[512,2048]{1,0:T(8,128)(2,1)} fusion(bf16[640,2048]{1,0:T(8,128)(2,1)} %bitcast.71, s32[1024]{0:T(1024)S(1)} %pad_clamp_fusion), kind=kCustom, calls=%fused_computation.1.clone | custom fusion | bytes 4196352 | tf_op jit(solution)/shard_map/jit(take_along_axis)/gather | solution.py:80
  259.3 50.9 %all-to-all-done.2 = bf16[1,16,40,2048]{3,2,0,1:T(8,128)(2,1)} async-done(((bf16[1,16,40,2048]{3,2,0,1:T(8,128)(2,1)}), bf16[1,16,40,2048]{3,2,0,1:T(8,128)(2,1)}, u32[]{:S(2)}, u32[]{:S(2)}) %all-to-all-start.2) | async-done | bytes 2621472 | tf_op jit(solution)/shard_map/all_to_all | solution.py:74
  310.2 7.4 %gather_fusion = bf16[512,2048]{1,0:T(8,128)(2,1)} fusion(bf16[640,2048]{1,0:T(8,128)(2,1)} %bitcast.34, s32[1024]{0:T(1024)S(1)} %pad_clamp_fusion.1), kind=kCustom, calls=%fused_computation.clone | custom fusion | bytes 4196352 | tf_op jit(solution)/shard_map/jit(take_along_axis)/gather | solution.py:80
  317.6 4.2 %fusion.8 = f32[64,2048]{1,0:T(8,128)S(1)} fusion(bf16[512,2048]{1,0:T(8,128)(2,1)} %gather_fusion.1, f32[64,8]{1,0:T(8,128)S(1)} %copy.74, pred[512]{0:T(512)(128)(4,1)S(1)} %get-tuple-element.14), kind=kLoop, calls=%fused_computation.17 | loop fusion | flops 4063232 | bytes 2624000 | tf_op jit(solution)/shard_map/reduce_sum | solution.py:82
  (92 shorter events, 25.0 us)
Async XLA Ops:
  0.0 131.2 %copy-start = (bf16[1,768,2048]{2,1,0:T(8,128)(2,1)S(1)}, bf16[1,768,2048]{2,1,0:T(8,128)(2,1)}, u32[]{:S(2)}) copy-start(bf16[1,768,2048]{2,1,0:T(8,128)(2,1)} %param.15) | copy-start | bytes 9437188
  0.0 3.0 copy-start.8
  7.4 2.3 copy-start.7
  7.5 2.3 copy-start.9
  9.7 2.8 copy-start.1
  19.4 14.7 %all-to-all-start.3 = ((bf16[1,16,8,1024]{3,2,0,1:T(8,128)(2,1)}), bf16[1,16,8,1024]{3,2,0,1:T(8,128)(2,1)}, u32[]{:S(2)}, u32[]{:S(2)}) async-start(bf16[1,16,8,1024]{3,2,0,1:T(8,128)(2,1)} %bitcast.227), calls=%async_computation.3 | async-start | bytes 524288 | tf_op jit(solution)/shard_map/all_to_all | solution.py:101
  26.0 6.5 %copy-start.12 = (s32[2,64,8]{1,2,0:T(8,128)S(1)}, s32[2,64,8]{1,2,0:T(8,128)}, u32[]{:S(2)}) copy-start(s32[2,64,8]{1,2,0:T(8,128)} %param.16) | copy-start | bytes 12292
  31.5 19.0 %copy-start.10 = (f32[2048]{0:T(1024)S(1)}, f32[2048]{0:T(1024)}, u32[]{:S(2)}) copy-start(f32[2048]{0:T(1024)} %param.13) | copy-start | bytes 24580
  34.1 14.0 %all-to-all-start = ((bf16[1,16,8,1024]{3,2,0,1:T(8,128)(2,1)}), bf16[1,16,8,1024]{3,2,0,1:T(8,128)(2,1)S(1)}, u32[]{:S(2)}, u32[]{:S(2)}) async-start(bf16[1,16,8,1024]{3,2,0,1:T(8,128)(2,1)} %bitcast.226), calls=%async_computation | async-start | bytes 524288 | tf_op jit(solution)/shard_map/all_to_all | solution.py:101
  48.2 0.8 copy-start.4
  54.0 65.2 %all-to-all-start.4 = ((bf16[1,16,40,2048]{3,2,0,1:T(8,128)(2,1)}), bf16[1,16,40,2048]{3,2,0,1:T(8,128)(2,1)}, u32[]{:S(2)}, u32[]{:S(2)}) async-start(bf16[1,16,40,2048]{3,2,0,1:T(8,128)(2,1)} %bitcast.214), calls=%async_computation.4 | async-start | bytes 5242880 | tf_op jit(solution)/shard_map/all_to_all | solution.py:114
  119.2 63.6 %all-to-all-start.1 = ((bf16[1,16,40,2048]{3,2,0,1:T(8,128)(2,1)}), bf16[1,16,40,2048]{3,2,0,1:T(8,128)(2,1)}, u32[]{:S(2)}, u32[]{:S(2)}) async-start(bf16[1,16,40,2048]{3,2,0,1:T(8,128)(2,1)} %bitcast.215), calls=%async_computation.1 | async-start | bytes 5242880 | tf_op jit(solution)/shard_map/all_to_all | solution.py:114
  182.8 63.7 %all-to-all-start.5 = ((bf16[1,16,40,2048]{3,2,0,1:T(8,128)(2,1)}), bf16[1,16,40,2048]{3,2,0,1:T(8,128)(2,1)}, u32[]{:S(2)}, u32[]{:S(2)}) async-start(bf16[1,16,40,2048]{3,2,0,1:T(8,128)(2,1)} %bitcast.223), calls=%async_computation.5 | async-start | bytes 5242880 | tf_op jit(solution)/shard_map/all_to_all | solution.py:74
  198.6 52.9 %copy-start.11 = (s32[2,64,8]{1,2,0:T(8,128)S(1)}, s32[2,64,8]{1,2,0:T(8,128)}, u32[]{:S(2)}) copy-start(s32[2,64,8]{1,2,0:T(8,128)} %param.17) | copy-start | bytes 12292
  246.5 63.7 %all-to-all-start.2 = ((bf16[1,16,40,2048]{3,2,0,1:T(8,128)(2,1)}), bf16[1,16,40,2048]{3,2,0,1:T(8,128)(2,1)}, u32[]{:S(2)}, u32[]{:S(2)}) async-start(bf16[1,16,40,2048]{3,2,0,1:T(8,128)(2,1)} %bitcast.222), calls=%async_computation.2 | async-start | bytes 5242880 | tf_op jit(solution)/shard_map/all_to_all | solution.py:74
  317.5 4.2 %copy-start.2 = (bf16[512,2048]{1,0:T(8,128)(2,1)S(1)}, bf16[512,2048]{1,0:T(8,128)(2,1)}, u32[]{:S(2)}) copy-start(bf16[512,2048]{1,0:T(8,128)(2,1)} %gather_fusion) | copy-start | bytes 6291460
  317.5 6.8 %copy-start.3 = (f32[1,8,2,8,1024]{4,3,2,1,0:T(8,128)S(1)}, f32[1,8,2,8,1024]{4,3,2,1,0:T(8,128)}, u32[]{:S(2)}) copy-start(f32[1,8,2,8,1024]{4,3,2,1,0:T(8,128)} %convert.10) | copy-start | bytes 1572868
  317.5 6.8 %copy-start.5 = (f32[1,8,2,8,1024]{4,3,2,1,0:T(8,128)S(1)}, f32[1,8,2,8,1024]{4,3,2,1,0:T(8,128)}, u32[]{:S(2)}) copy-start(f32[1,8,2,8,1024]{4,3,2,1,0:T(8,128)} %copy-done.4) | copy-start | bytes 1572868
  317.5 6.8 %copy-start.6 = (bf16[2,64,2048]{2,1,0:T(8,128)(2,1)S(1)}, bf16[2,64,2048]{2,1,0:T(8,128)(2,1)}, u32[]{:S(2)}) copy-start(bf16[2,64,2048]{2,1,0:T(8,128)(2,1)} %param.12) | copy-start | bytes 1572868
  317.5 6.8 %copy-start.13 = (bf16[2,64,2048]{2,1,0:T(8,128)(2,1)S(1)}, bf16[2,64,2048]{2,1,0:T(8,128)(2,1)}, u32[]{:S(2)}) copy-start(bf16[2,64,2048]{2,1,0:T(8,128)(2,1)} %custom-call.4) | copy-start | bytes 1572868
  324.5 0.8 copy-start.14
where the time goes:
time: 326 us; the launch traced here: 325 us
  waiting for transfers between devices  205 us (63%)
  matrix products  42 us (13%)
  starting transfers between devices  33.7 us (10%)
  local copies, waits for them, and re-layouts  29 us (9%)
  other arithmetic  15.6 us (5%)
    all_to_all x2, waiting for transfers between devices, body(): lax.all_to_all(shaped, 'dev', split_axis=1, concat_axis=1, tiled=True)  101 us
    all_to_all x2, waiting for transfers between devices, run_experts(): lax.all_to_all(finished, 'dev', split_axis=1, concat_axis=1, tiled=True)  98.8 us
    gather x2, local copies, waits for them, and re-layouts, combine(): picked = jnp.take_along_axis(flat_back, target[:, :, None], axis=1)  14.7 us
    dot_general x2, matrix products, run_experts(): projected = jnp.dot(rows_in, gate_up[0], preferred_element_type=jnp.float32)  14.3 us
    all_to_all x2, starting transfers between devices, body(): lax.all_to_all(outgoing_rows, 'dev', split_axis=1, concat_axis=1, tiled=T...  12.6 us
    all_to_all x2, starting transfers between devices, body(): lax.all_to_all(shaped, 'dev', split_axis=1, concat_axis=1, tiled=True)  11.3 us
    all_to_all x2, starting transfers between devices, run_experts(): lax.all_to_all(finished, 'dev', split_axis=1, concat_axis=1, tiled=True)  9.82 us
    dot_general x2, matrix products, attend(): jnp.einsum('mgqk,mkd->mqgd', weights, cached_pairs[:, 1], preferred_eleme...  8.07 us
  transfers between devices with their start and end apart: 6, of which 5 were waited for; matrix products, arithmetic and copies ran while one was open for 14% of the time, Pallas kernels for 0%

commit v1 on v0

v1 whole, which is shorter than its diff:
```python
import functools
import math

import jax
import jax.numpy as jnp
from jax import lax
from jax.experimental import pallas as pl
from jax.experimental.pallas import tpu as pltpu
from jax.sharding import PartitionSpec as P

F32 = jnp.float32
BF16 = jnp.bfloat16


def attend_kernel(q_ref, kv_ref, out_ref):
    length, feat_width = q_ref.shape
    context, head_size = kv_ref.shape[1:]
    scale = math.log2(math.e) / math.sqrt(head_size)
    keys, values = kv_ref[0], kv_ref[1]
    row = lax.broadcasted_iota(jnp.int32, (length, length), 0)
    col = lax.broadcasted_iota(jnp.int32, (length, length), 1)
    allowed = col <= row
    for head in range(feat_width // head_size):
        cols = slice(head * head_size, (head + 1) * head_size)
        scores = lax.dot_general(
            q_ref[:, cols], keys, (((1,), (1,)), ((), ())), preferred_element_type=F32
        )
        cached = scores[:, : context - length]
        fresh = jnp.where(allowed, scores[:, context - length :], -1e30)
        highest = jnp.maximum(
            jnp.max(cached, axis=-1, keepdims=True), jnp.max(fresh, axis=-1, keepdims=True)
        )
        grown = jnp.concatenate(
            [jnp.exp2((cached - highest) * scale), jnp.exp2((fresh - highest) * scale)], axis=1
        )
        total = jnp.sum(grown, axis=-1, keepdims=True)
        blended = jnp.dot(grown.astype(BF16), values, preferred_element_type=F32)
        out_ref[:, cols] = (blended / total).astype(BF16)


def attend(queries, keys_values, batch):
    length, feat_width = queries.shape[2:]
    context, head_size = keys_values.shape[3:]
    pairs = length * (feat_width // head_size) * context
    return pl.pallas_call(
        attend_kernel,
        out_shape=jax.ShapeDtypeStruct((length, feat_width), BF16),
        grid=(1,),
        in_specs=[
            pl.BlockSpec((None, None, length, feat_width), lambda i: (batch, 0, 0, 0)),
            pl.BlockSpec((None, None, 2, context, head_size), lambda i: (batch, 0, 0, 0, 0)),
        ],
        out_specs=pl.BlockSpec((length, feat_width), lambda i: (0, 0)),
        compiler_params=pltpu.CompilerParams(vmem_limit_bytes=32 << 20),
        cost_estimate=pl.CostEstimate(
            flops=4 * pairs * head_size,
            bytes_accessed=2 * (2 * length * feat_width + 2 * context * head_size),
            transcendentals=pairs,
        ),
        name="attend",
    )(queries, keys_values)


def expert_kernel(me_ref, x_ref, share_ref, gate_ref, up_ref, down_ref, mine_ref, other_ref, hidden_ref, *, steps, offset):
    step = pl.program_id(0)
    rows = x_ref.shape[0]
    tokens = rows // share_ref.shape[0]
    lanes = share_ref.shape[2]

    @pl.when(step < steps)
    def _():
        x = x_ref[...]
        gate = jnp.dot(x, gate_ref[...], preferred_element_type=F32)
        up = jnp.dot(x, up_ref[...], preferred_element_type=F32)
        hidden_ref[step] = (gate / (1.0 + jnp.exp(-gate)) * up).astype(BF16)

    @pl.when(step >= steps)
    def _():
        width = hidden_ref.shape[2]
        total = jnp.dot(hidden_ref[0], down_ref[:width], preferred_element_type=F32)
        for part in range(1, steps):
            total += jnp.dot(
                hidden_ref[part],
                down_ref[part * width : (part + 1) * width],
                preferred_element_type=F32,
            )
        token = lax.broadcasted_iota(jnp.int32, (tokens, lanes), 0)
        lane = lax.broadcasted_iota(jnp.int32, (tokens, lanes), 1)
        diagonal = lane == token + offset
        shares = []
        for block in range(rows // tokens):
            line = share_ref[block, pl.ds(me_ref[0], 1), :]
            shares.append(
                jnp.sum(
                    jnp.where(diagonal, jnp.broadcast_to(line, (tokens, lanes)), 0.0),
                    axis=-1,
                    keepdims=True,
                )
            )
        weighted = (total * jnp.concatenate(shares, axis=0)).astype(BF16)
        mine_ref[...] = weighted[: rows // 2]
        other_ref[...] = weighted[rows // 2 :]


def run_expert(me, x, shares, gate_up, down_proj, batch):
    rows, model_width = x.shape
    hidden_width = down_proj.shape[1]
    blocks, experts, lanes = shares.shape
    tokens = rows // blocks
    part = 256
    steps = hidden_width // part
    chunk = 512
    chunks = model_width // chunk
    clamp = lambda i: jnp.minimum(i, steps - 1)
    late = lambda i: jnp.maximum(i - steps, 0)
    half = jax.ShapeDtypeStruct((rows // 2, model_width), BF16)
    flops = 2 * rows * model_width * hidden_width * 3
    return pl.pallas_call(
        functools.partial(expert_kernel, steps=steps, offset=batch * tokens),
        out_shape=(half, half),
        grid_spec=pltpu.PrefetchScalarGridSpec(
            num_scalar_prefetch=1,
            grid=(steps + chunks,),
            in_specs=[
                pl.BlockSpec((rows, model_width), lambda i, me: (0, 0)),
                pl.BlockSpec((blocks, experts, lanes), lambda i, me: (0, 0, 0)),
                pl.BlockSpec((None, model_width, part), lambda i, me: (0, 0, clamp(i))),
                pl.BlockSpec((None, model_width, part), lambda i, me: (0, 0, steps + clamp(i))),
                pl.BlockSpec((None, hidden_width, chunk), lambda i, me: (0, 0, late(i))),
            ],
            out_specs=(
                pl.BlockSpec((rows // 2, chunk), lambda i, me: (0, late(i))),
                pl.BlockSpec((rows // 2, chunk), lambda i, me: (0, late(i))),
            ),
            scratch_shapes=[pltpu.VMEM((steps, rows, part), BF16)],
        ),
        compiler_params=pltpu.CompilerParams(vmem_limit_bytes=56 << 20),
        cost_estimate=pl.CostEstimate(
            flops=flops,
            bytes_accessed=2 * (3 * hidden_width * model_width + 2 * rows * model_width),
            transcendentals=rows * hidden_width,
        ),
        name="expert",
    )(me, x, shares, gate_up, gate_up, down_proj)


def ring_orders(devices):
    chips = devices // 2
    order = [2 * r if r < chips // 2 else 2 * (chips - 1 - r) + 1 for r in range(chips)]
    forward = [
        (2 * order[r] + core, 2 * order[(r + 1) % chips] + core)
        for r in range(chips)
        for core in range(2)
    ]
    backward = [(b, a) for a, b in forward]
    swap = [(i, i ^ 1) for i in range(devices)]
    return forward, backward, swap


def gather_ring(block, forward, backward, reach):
    width = block.shape[-1] // 2
    ahead = behind = block
    pairs = []
    for _ in range(reach - 1):
        ahead = lax.ppermute(ahead, "dev", forward)
        behind = lax.ppermute(behind, "dev", backward)
        pairs.append((behind, ahead))
    left = lax.ppermute(ahead[..., :width], "dev", forward)
    right = lax.ppermute(behind[..., width:], "dev", backward)
    return pairs, jnp.concatenate([left, right], axis=-1)


def add(*terms):
    total = terms[0].astype(F32)
    for term in terms[1:]:
        total = total + term.astype(F32)
    return total


def scatter_ring(near, far, forward, backward):
    far = add(*far).astype(BF16)
    width = far.shape[-1] // 2
    ahead = lax.ppermute(far[:, :width], "dev", forward)
    behind = lax.ppermute(far[:, width:], "dev", backward)
    empty = jnp.zeros_like(ahead)
    ahead = jnp.concatenate([ahead, empty], axis=-1)
    behind = jnp.concatenate([empty, behind], axis=-1)
    for up, down in reversed(near):
        ahead = lax.ppermute(add(ahead, *up).astype(BF16), "dev", forward)
        behind = lax.ppermute(add(behind, *down).astype(BF16), "dev", backward)
    return ahead, behind


def share_table(expert_ids, expert_gates, experts):
    shares = expert_gates.astype(F32)
    shares = shares / jnp.sum(shares, axis=-1, keepdims=True)
    named = lax.broadcasted_iota(jnp.int32, (experts, 1, 1, 1), 0) == expert_ids[None]
    table = jnp.sum(jnp.where(named, shares[None], 0.0), axis=-1)
    return table.reshape(experts, -1)


def to_owners(arrived, kv_heads):
    sources, positions, feat_width = arrived.shape
    grouped = arrived.reshape(sources // kv_heads, kv_heads, positions, feat_width)
    grouped = jnp.transpose(grouped, (0, 2, 1, 3))
    return grouped.reshape(sources // kv_heads * positions, kv_heads * feat_width)


def body(queries, keys_values, residual, norm_gain, gate_up, down_proj, expert_ids, expert_gates):
    devices = lax.axis_size("dev")
    batches, tokens, model_width = residual.shape
    length, feat_width = queries.shape[2:]
    kv_heads = model_width // feat_width
    experts = devices * gate_up.shape[0]
    forward, backward, swap = ring_orders(devices)
    reach = devices // 4
    split = reach // 2
    me = lax.axis_index("dev").astype(jnp.int32).reshape(1)

    table = share_table(expert_ids, expert_gates, experts)
    streams, rows_all = [], []
    for batch in range(batches):
        heads = attend(queries, keys_values, batch)
        arrived = lax.all_to_all(
            heads.reshape(devices, length // devices, feat_width),
            "dev",
            split_axis=0,
            concat_axis=0,
            tiled=True,
        )
        stream = residual[batch].astype(F32) + to_owners(arrived, kv_heads).astype(F32)
        meansq = jnp.mean(stream * stream, axis=-1, keepdims=True)
        streams.append(stream)
        rows_all.append((stream * lax.rsqrt(meansq + 1e-06) * norm_gain).astype(BF16))

    table_pairs, table_far = gather_ring(table, forward, backward, reach)
    near_tables = jnp.stack([table] + [t for pair in table_pairs[:split] for t in pair])
    far_tables = jnp.stack([t for pair in table_pairs[split:] for t in pair] + [table_far])
    near_tables = jnp.concatenate([near_tables, lax.ppermute(near_tables, "dev", swap)])
    far_tables = jnp.concatenate([far_tables, lax.ppermute(far_tables, "dev", swap)])

    pieces = []
    for batch in range(batches):
        own = rows_all[batch]
        pairs, far = gather_ring(own, forward, backward, reach)
        outs = []
        for blocks, tables in (
            ([own] + [b for pair in pairs[:split] for b in pair], near_tables),
            ([b for pair in pairs[split:] for b in pair] + [far], far_tables),
        ):
            held = jnp.concatenate(blocks, axis=0)
            swapped = lax.ppermute(held, "dev", swap)
            mine, other = run_expert(
                me, jnp.concatenate([held, swapped], axis=0), tables, gate_up, down_proj, batch
            )
            theirs = lax.ppermute(other, "dev", swap)
            for k in range(len(blocks)):
                cut = slice(k * tokens, (k + 1) * tokens)
                outs.append((mine[cut], theirs[cut]))
        near = [(outs[1 + 2 * d], outs[2 + 2 * d]) for d in range(reach - 1)]
        ahead, behind = scatter_ring(near, outs[-1], forward, backward)
        pieces.append(add(streams[batch], *outs[0], ahead, behind).astype(BF16))
    return jnp.stack(pieces, axis=0)


def solution(mesh):
    in_specs = (
        P(None, ("groups", "dev"), None, None),
        P(None, ("groups", "dev"), None, None, None),
        P(None, ("groups", "dev"), None),
        P(),
        P("dev", None, None),
        P("dev", None, None),
        P(None, ("groups", "dev"), None),
        P(None, ("groups", "dev"), None),
    )
    out_specs = P(None, ("groups", "dev"), None)
    return jax.shard_map(body, mesh=mesh, in_specs=in_specs, out_specs=out_specs, check_vma=False)
```

time: 326 us -> 200 us (0.61)
  the two profiles are of different devices: /device:TPU:15 before, /device:TPU:0 now
where the time goes in v1:
time: 200 us; the launch traced here: 199 us
  waiting for transfers between devices  67.4 us (34%)
  Pallas kernels  55.9 us (28%)
  starting transfers between devices  53.3 us (27%)
  local copies, waits for them, and re-layouts  13 us (6%)
  other arithmetic  9.08 us (5%)
    pallas_call x4, Pallas kernels, run_expert(): pl.pallas_call(functools.partial(expert_kernel, steps=steps, offset=batch...  46.9 us
    ppermute x6, waiting for transfers between devices, scatter_ring(): behind = lax.ppermute(add(behind, *down).astype(BF16), 'dev', backward)  15.2 us
    ppermute x9, starting transfers between devices, gather_ring(): ahead = lax.ppermute(ahead, 'dev', forward)  12.8 us
    ppermute x9, waiting for transfers between devices, gather_ring(): behind = lax.ppermute(behind, 'dev', backward)  11.9 us
    all_to_all x2, starting transfers between devices, body(): lax.all_to_all(heads.reshape(devices, length // devices, feat_width), 'de...  11.1 us
    ppermute x9, waiting for transfers between devices, gather_ring(): ahead = lax.ppermute(ahead, 'dev', forward)  9.31 us
    pallas_call x2, Pallas kernels, attend(): pl.pallas_call(attend_kernel, out_shape=jax.ShapeDtypeStruct((length, fea...  9 us
    all_to_all x2, waiting for transfers between devices, body(): lax.all_to_all(heads.reshape(devices, length // devices, feat_width), 'de...  8.64 us
  transfers between devices with their start and end apart: 52, of which 28 were waited for; matrix products, arithmetic and copies ran while one was open for 7% of the time, Pallas kernels for 28%

profile of v1, /device:TPU:0, one launch (start us, length us, event | category | flops | bytes accessed | tf_op | source)
XLA Modules:
  0.0 199.0 jit_solution(8549453550723094206)
XLA Ops:
  1.6 3.0 %collective-permute-start.5 = (f32[16,128]{1,0:T(8,128)S(1)}, f32[16,128]{1,0:T(8,128)S(1)}, u32[]{:S(2)}, u32[]{:S(2)}) collective-permute-start(f32[16,128]{1,0:T(8,128)S(1)} %reshape.50), channel_id=1, source_target_pairs={{4,0},{5,1},{8,4},{9,5},{12,8},{13,9},{14,12},{15,13},{10,14},{11,... | collective-permute-start | bytes 24584 | tf_op jit(solution)/shard_map/ppermute | solution.py:166
  7.2 4.5 %attend.3 = bf16[128,1024]{1,0:T(8,128)(2,1)} custom-call(bf16[2,1,128,1024]{3,2,1,0:T(8,128)(2,1)S(1)} %copy-done.2, bf16[2,1,2,1664,128]{4,3,2,1,0:T(8,128)(2,1)S(1)} %copy-done), custom_call_target="tpu_custom_call" | custom-call | flops 872415232 | bytes 1376256 | tf_op jit(solution)/shard_map/attend/pallas_call | solution.py:45
  11.7 6.3 %all-to-all-start.1 = ((bf16[16,8,1024]{2,1,0:T(8,128)(2,1)}), bf16[16,8,1024]{2,1,0:T(8,128)(2,1)S(1)}, u32[]{:S(2)}, u32[]{:S(2)}) async-start(bf16[16,8,1024]{2,1,0:T(8,128)(2,1)} %bitcast.15), calls=%async_computation.1 | async-start | bytes 524288 | tf_op jit(solution)/shard_map/all_to_all | solution.py:224
  18.1 4.5 %attend.2 = bf16[128,1024]{1,0:T(8,128)(2,1)} custom-call(bf16[2,1,128,1024]{3,2,1,0:T(8,128)(2,1)S(1)} %copy-done.3, bf16[2,1,2,1664,128]{4,3,2,1,0:T(8,128)(2,1)S(1)} %copy-done.1), custom_call_target="tpu_custom_call" | custom-call | flops 872415232 | bytes 1376256 | tf_op jit(solution)/shard_map/attend/pallas_call | solution.py:45
  35.7 4.7 %all-to-all-start = ((bf16[16,8,1024]{2,1,0:T(8,128)(2,1)}), bf16[16,8,1024]{2,1,0:T(8,128)(2,1)S(1)}, u32[]{:S(2)}, u32[]{:S(2)}) async-start(bf16[16,8,1024]{2,1,0:T(8,128)(2,1)} %bitcast.1), calls=%async_computation | async-start | bytes 524288 | tf_op jit(solution)/shard_map/all_to_all | solution.py:224
  41.9 8.6 %all-to-all-done = bf16[16,8,1024]{2,1,0:T(8,128)(2,1)S(1)} async-done(((bf16[16,8,1024]{2,1,0:T(8,128)(2,1)}), bf16[16,8,1024]{2,1,0:T(8,128)(2,1)S(1)}, u32[]{:S(2)}, u32[]{:S(2)}) %all-to-all-start) | async-done | bytes 262176 | tf_op jit(solution)/shard_map/all_to_all | solution.py:224
  56.0 5.1 %collective-permute-done.30 = bf16[64,2048]{1,0:T(8,128)(2,1)S(1)} collective-permute-done((bf16[64,2048]{1,0:T(8,128)(2,1)S(1)}, bf16[64,2048]{1,0:T(8,128)(2,1)S(1)}, u32[]{:S(2)}, u32[]{:S(2)}) %collective-permute-start.30) | collective-permute-done | bytes 262176 | tf_op jit(solution)/shard_map/ppermute | solution.py:166
  63.1 3.5 %collective-permute-done = bf16[64,2048]{1,0:T(8,128)(2,1)S(1)} collective-permute-done((bf16[64,2048]{1,0:T(8,128)(2,1)S(1)}, bf16[64,2048]{1,0:T(8,128)(2,1)S(1)}, u32[]{:S(2)}, u32[]{:S(2)}) %collective-permute-start) | collective-permute-done | bytes 262176 | tf_op jit(solution)/shard_map/ppermute | solution.py:166
  72.2 2.1 %collective-permute-start.37 = (bf16[64,2048]{1,0:T(8,128)(2,1)S(1)}, bf16[64,2048]{1,0:T(8,128)(2,1)S(1)}, u32[]{:S(2)}, u32[]{:S(2)}) collective-permute-start(bf16[64,2048]{1,0:T(8,128)(2,1)S(1)} %collective-permute-done.33), channel_id=1, source_target_pairs={{0,4},{1,5},{4,8},{5,9},{8,12},{9,13},{12,14},{13,15},{14,10},{15,... | collective-permute-start | bytes 786440 | tf_op jit(solution)/shard_map/ppermute | solution.py:165
  75.1 2.7 %collective-permute-done.3 = bf16[64,2048]{1,0:T(8,128)(2,1)S(1)} collective-permute-done((bf16[64,2048]{1,0:T(8,128)(2,1)S(1)}, bf16[64,2048]{1,0:T(8,128)(2,1)S(1)}, u32[]{:S(2)}, u32[]{:S(2)}) %collective-permute-start.3) | collective-permute-done | bytes 262176 | tf_op jit(solution)/shard_map/ppermute | solution.py:165
  80.7 2.7 %collective-permute-done.37 = bf16[64,2048]{1,0:T(8,128)(2,1)S(1)} collective-permute-done((bf16[64,2048]{1,0:T(8,128)(2,1)S(1)}, bf16[64,2048]{1,0:T(8,128)(2,1)S(1)}, u32[]{:S(2)}, u32[]{:S(2)}) %collective-permute-start.37) | collective-permute-done | bytes 262176 | tf_op jit(solution)/shard_map/ppermute | solution.py:165
  83.5 2.2 %collective-permute-start.38 = (bf16[64,1024]{1,0:T(8,128)(2,1)S(1)}, bf16[64,1024]{1,0:T(8,128)(2,1)S(1)}, u32[]{:S(2)}, u32[]{:S(2)}) collective-permute-start(bf16[64,1024]{1,0:T(8,128)(2,1)S(1)} %slice.191), channel_id=1, source_target_pairs={{0,4},{1,5},{4,8},{5,9},{8,12},{9,13},{12,14},{13,15},{14,10},{15,... | collective-permute-start | bytes 393224 | tf_op jit(solution)/shard_map/ppermute | solution.py:168
  86.5 2.6 %collective-permute-done.12 = bf16[64,2048]{1,0:T(8,128)(2,1)S(1)} collective-permute-done((bf16[64,2048]{1,0:T(8,128)(2,1)S(1)}, bf16[64,2048]{1,0:T(8,128)(2,1)S(1)}, u32[]{:S(2)}, u32[]{:S(2)}) %collective-permute-start.12) | collective-permute-done | bytes 262176 | tf_op jit(solution)/shard_map/ppermute | solution.py:165
  89.1 2.1 %collective-permute-start.13 = (bf16[64,1024]{1,0:T(8,128)(2,1)S(1)}, bf16[64,1024]{1,0:T(8,128)(2,1)S(1)}, u32[]{:S(2)}, u32[]{:S(2)}) collective-permute-start(bf16[64,1024]{1,0:T(8,128)(2,1)S(1)} %slice.177), channel_id=1, source_target_pairs={{0,4},{1,5},{4,8},{5,9},{8,12},{9,13},{12,14},{13,15},{14,10},{15,... | collective-permute-start | bytes 393224 | tf_op jit(solution)/shard_map/ppermute | solution.py:168
  94.1 2.3 %collective-permute-done.14 = bf16[64,1024]{1,0:T(8,128)(2,1)S(1)} collective-permute-done((bf16[64,1024]{1,0:T(8,128)(2,1)S(1)}, bf16[64,1024]{1,0:T(8,128)(2,1)S(1)}, u32[]{:S(2)}, u32[]{:S(2)}) %collective-permute-start.14) | collective-permute-done | bytes 131104 | tf_op jit(solution)/shard_map/ppermute | solution.py:169
  100.7 10.6 %expert.7 = (bf16[192,2048]{1,0:T(8,128)(2,1)}, bf16[192,2048]{1,0:T(8,128)(2,1)}) custom-call(s32[1]{0:T(128)} %bitcast.5.me_ref, bf16[384,2048]{1,0:T(8,128)(2,1)} %pad_maximum_fusion.1.x_ref, f32[6,16,128]{2,1,0:T(8,128)} %pad_maximum_fusion.5.share_ref, bf16[1,2048,1536]{2,1,0:T(8,128)(2,1)} %up_ref.7, bf16[1,2048,1536]{2,1,0:T(8,128)(2,1)} %up_ref.7, ...), custom_call_target="tpu_custom_call" | custom-call | flops 3623878656 | bytes 12582912 | tf_op jit(solution)/shard_map/expert/pallas_call | solution.py:118
  112.7 10.6 %expert.5 = (bf16[192,2048]{1,0:T(8,128)(2,1)}, bf16[192,2048]{1,0:T(8,128)(2,1)}) custom-call(s32[1]{0:T(128)} %bitcast.5.me_ref, bf16[384,2048]{1,0:T(8,128)(2,1)} %pad_maximum_fusion.x_ref, f32[6,16,128]{2,1,0:T(8,128)} %pad_maximum_fusion.5.share_ref, bf16[1,2048,1536]{2,1,0:T(8,128)(2,1)} %up_ref.7, bf16[1,2048,1536]{2,1,0:T(8,128)(2,1)} %up_ref.7, ...), custom_call_target="tpu_custom_call" | custom-call | flops 3623878656 | bytes 12582912 | tf_op jit(solution)/shard_map/expert/pallas_call | solution.py:118
  125.0 12.8 %expert.6 = (bf16[320,2048]{1,0:T(8,128)(2,1)}, bf16[320,2048]{1,0:T(8,128)(2,1)}) custom-call(s32[1]{0:T(128)} %bitcast.5.me_ref, bf16[640,2048]{1,0:T(8,128)(2,1)} %constant_dynamic-update-slice_fusion.29.x_ref, f32[10,16,128]{2,1,0:T(8,128)} %copy-done.12, bf16[1,2048,1536]{2,1,0:T(8,128)(2,1)} %up_ref.7, bf16[1,2048,1536]{2,1,0:T(8,128)(2,1)} %up_ref.7, ...), custom_call_target="tpu_custom_call" | custom-call | flops 6039797760 | bytes 14680064 | tf_op jit(solution)/shard_map/expert/pallas_call | solution.py:118
  139.1 12.9 %expert.4 = (bf16[320,2048]{1,0:T(8,128)(2,1)}, bf16[320,2048]{1,0:T(8,128)(2,1)}) custom-call(s32[1]{0:T(128)} %bitcast.5.me_ref, bf16[640,2048]{1,0:T(8,128)(2,1)} %constant_dynamic-update-slice_fusion.5.x_ref, f32[10,16,128]{2,1,0:T(8,128)} %copy-done.12, bf16[1,2048,1536]{2,1,0:T(8,128)(2,1)} %up_ref.7, bf16[1,2048,1536]{2,1,0:T(8,128)(2,1)} %up_ref.7, ...), custom_call_target="tpu_custom_call" | custom-call | flops 6039797760 | bytes 14680064 | tf_op jit(solution)/shard_map/expert/pallas_call | solution.py:118
  154.8 4.1 %collective-permute-done.42 = bf16[64,1024]{1,0:T(8,128)(2,1)S(1)} collective-permute-done((bf16[64,1024]{1,0:T(8,128)(2,1)S(1)}, bf16[64,1024]{1,0:T(8,128)(2,1)S(1)}, u32[]{:S(2)}, u32[]{:S(2)}) %collective-permute-start.42) | collective-permute-done | bytes 131104 | tf_op jit(solution)/shard_map/ppermute | solution.py:183
  161.5 3.7 %collective-permute-done.26 = bf16[64,1024]{1,0:T(8,128)(2,1)S(1)} collective-permute-done((bf16[64,1024]{1,0:T(8,128)(2,1)S(1)}, bf16[64,1024]{1,0:T(8,128)(2,1)S(1)}, u32[]{:S(2)}, u32[]{:S(2)}) %collective-permute-start.26) | collective-permute-done | bytes 131104 | tf_op jit(solution)/shard_map/ppermute | solution.py:184
  165.5 2.9 %collective-permute-done.43 = bf16[64,2048]{1,0:T(8,128)(2,1)S(1)} collective-permute-done((bf16[64,2048]{1,0:T(8,128)(2,1)S(1)}, bf16[64,2048]{1,0:T(8,128)(2,1)S(1)}, u32[]{:S(2)}, u32[]{:S(2)}) %collective-permute-start.43) | collective-permute-done | bytes 262176 | tf_op jit(solution)/shard_map/ppermute | solution.py:189
  173.2 4.5 %collective-permute-done.27 = bf16[64,2048]{1,0:T(8,128)(2,1)S(1)} collective-permute-done((bf16[64,2048]{1,0:T(8,128)(2,1)S(1)}, bf16[64,2048]{1,0:T(8,128)(2,1)S(1)}, u32[]{:S(2)}, u32[]{:S(2)}) %collective-permute-start.27) | collective-permute-done | bytes 262176 | tf_op jit(solution)/shard_map/ppermute | solution.py:190
  180.0 3.3 %collective-permute-done.48 = bf16[64,2048]{1,0:T(8,128)(2,1)S(1)} collective-permute-done((bf16[64,2048]{1,0:T(8,128)(2,1)S(1)}, bf16[64,2048]{1,0:T(8,128)(2,1)S(1)}, u32[]{:S(2)}, u32[]{:S(2)}) %collective-permute-start.48) | collective-permute-done | bytes 262176 | tf_op jit(solution)/shard_map/ppermute | solution.py:190
  (167 shorter events, 76.0 us)
Async XLA Ops:
  1.6 21.0 %collective-permute-start.5 = (f32[16,128]{1,0:T(8,128)S(1)}, f32[16,128]{1,0:T(8,128)S(1)}, u32[]{:S(2)}, u32[]{:S(2)}) collective-permute-start(f32[16,128]{1,0:T(8,128)S(1)} %reshape.50), channel_id=1, source_target_pairs={{4,0},{5,1},{8,4},{9,5},{12,8},{13,9},{14,12},{15,13},{10,14},{11,... | collective-permute-start | bytes 24584 | tf_op jit(solution)/shard_map/ppermute | solution.py:166
  4.6 20.0 %collective-permute-start.6 = (f32[16,128]{1,0:T(8,128)S(1)}, f32[16,128]{1,0:T(8,128)S(1)}, u32[]{:S(2)}, u32[]{:S(2)}) collective-permute-start(f32[16,128]{1,0:T(8,128)S(1)} %reshape.50), channel_id=1, source_target_pairs={{0,4},{1,5},{4,8},{5,9},{8,12},{9,13},{12,14},{13,15},{14,10},{15,... | collective-permute-start | bytes 24584 | tf_op jit(solution)/shard_map/ppermute | solution.py:165
  11.7 24.0 %all-to-all-start.1 = ((bf16[16,8,1024]{2,1,0:T(8,128)(2,1)}), bf16[16,8,1024]{2,1,0:T(8,128)(2,1)S(1)}, u32[]{:S(2)}, u32[]{:S(2)}) async-start(bf16[16,8,1024]{2,1,0:T(8,128)(2,1)} %bitcast.15), calls=%async_computation.1 | async-start | bytes 524288 | tf_op jit(solution)/shard_map/all_to_all | solution.py:224
  35.7 14.8 %all-to-all-start = ((bf16[16,8,1024]{2,1,0:T(8,128)(2,1)}), bf16[16,8,1024]{2,1,0:T(8,128)(2,1)S(1)}, u32[]{:S(2)}, u32[]{:S(2)}) async-start(bf16[16,8,1024]{2,1,0:T(8,128)(2,1)} %bitcast.1), calls=%async_computation | async-start | bytes 524288 | tf_op jit(solution)/shard_map/all_to_all | solution.py:224
  53.9 12.8 %collective-permute-start = (bf16[64,2048]{1,0:T(8,128)(2,1)S(1)}, bf16[64,2048]{1,0:T(8,128)(2,1)S(1)}, u32[]{:S(2)}, u32[]{:S(2)}) collective-permute-start(bf16[64,2048]{1,0:T(8,128)(2,1)S(1)} %get-tuple-element.24), channel_id=1, source_target_pairs={{4,0},{5,1},{8,4},{9,5},{12,8},{13,9},{14,12},{15,13},{10,14},{11,... | collective-permute-start | bytes 786440 | tf_op jit(solution)/shard_map/ppermute | solution.py:166
  53.9 12.8 %collective-permute-start.1 = (bf16[64,2048]{1,0:T(8,128)(2,1)S(1)}, bf16[64,2048]{1,0:T(8,128)(2,1)S(1)}, u32[]{:S(2)}, u32[]{:S(2)}) collective-permute-start(bf16[64,2048]{1,0:T(8,128)(2,1)S(1)} %get-tuple-element.24), channel_id=1, source_target_pairs={{0,4},{1,5},{4,8},{5,9},{8,12},{9,13},{12,14},{13,15},{14,10},{15,... | collective-permute-start | bytes 786440 | tf_op jit(solution)/shard_map/ppermute | solution.py:165
  61.0 13.3 %collective-permute-start.32 = (bf16[64,2048]{1,0:T(8,128)(2,1)S(1)}, bf16[64,2048]{1,0:T(8,128)(2,1)S(1)}, u32[]{:S(2)}, u32[]{:S(2)}) collective-permute-start(bf16[64,2048]{1,0:T(8,128)(2,1)S(1)} %collective-permute-done.30), channel_id=1, source_target_pairs={{4,0},{5,1},{8,4},{9,5},{12,8},{13,9},{14,12},{15,13},{10,14},{11,... | collective-permute-start | bytes 786440 | tf_op jit(solution)/shard_map/ppermute | solution.py:166
  61.0 11.2 %collective-permute-start.33 = (bf16[64,2048]{1,0:T(8,128)(2,1)S(1)}, bf16[64,2048]{1,0:T(8,128)(2,1)S(1)}, u32[]{:S(2)}, u32[]{:S(2)}) collective-permute-start(bf16[64,2048]{1,0:T(8,128)(2,1)S(1)} %collective-permute-done.31), channel_id=1, source_target_pairs={{0,4},{1,5},{4,8},{5,9},{8,12},{9,13},{12,14},{13,15},{14,10},{15,... | collective-permute-start | bytes 786440 | tf_op jit(solution)/shard_map/ppermute | solution.py:165
  66.7 13.3 %collective-permute-start.2 = (bf16[64,2048]{1,0:T(8,128)(2,1)S(1)}, bf16[64,2048]{1,0:T(8,128)(2,1)S(1)}, u32[]{:S(2)}, u32[]{:S(2)}) collective-permute-start(bf16[64,2048]{1,0:T(8,128)(2,1)S(1)} %collective-permute-done), channel_id=1, source_target_pairs={{4,0},{5,1},{8,4},{9,5},{12,8},{13,9},{14,12},{15,13},{10,14},{11,... | collective-permute-start | bytes 786440 | tf_op jit(solution)/shard_map/ppermute | solution.py:166
  66.7 11.2 %collective-permute-start.3 = (bf16[64,2048]{1,0:T(8,128)(2,1)S(1)}, bf16[64,2048]{1,0:T(8,128)(2,1)S(1)}, u32[]{:S(2)}, u32[]{:S(2)}) collective-permute-start(bf16[64,2048]{1,0:T(8,128)(2,1)S(1)} %collective-permute-done.1), channel_id=1, source_target_pairs={{0,4},{1,5},{4,8},{5,9},{8,12},{9,13},{12,14},{13,15},{14,10},{15,... | collective-permute-start | bytes 786440 | tf_op jit(solution)/shard_map/ppermute | solution.py:165
  72.2 11.2 %collective-permute-start.37 = (bf16[64,2048]{1,0:T(8,128)(2,1)S(1)}, bf16[64,2048]{1,0:T(8,128)(2,1)S(1)}, u32[]{:S(2)}, u32[]{:S(2)}) collective-permute-start(bf16[64,2048]{1,0:T(8,128)(2,1)S(1)} %collective-permute-done.33), channel_id=1, source_target_pairs={{0,4},{1,5},{4,8},{5,9},{8,12},{9,13},{12,14},{13,15},{14,10},{15,... | collective-permute-start | bytes 786440 | tf_op jit(solution)/shard_map/ppermute | solution.py:165
  74.3 11.3 %collective-permute-start.36 = (bf16[64,2048]{1,0:T(8,128)(2,1)S(1)}, bf16[64,2048]{1,0:T(8,128)(2,1)S(1)}, u32[]{:S(2)}, u32[]{:S(2)}) collective-permute-start(bf16[64,2048]{1,0:T(8,128)(2,1)S(1)} %collective-permute-done.32), channel_id=1, source_target_pairs={{4,0},{5,1},{8,4},{9,5},{12,8},{13,9},{14,12},{15,13},{10,14},{11,... | collective-permute-start | bytes 786440 | tf_op jit(solution)/shard_map/ppermute | solution.py:166
  77.8 11.2 %collective-permute-start.12 = (bf16[64,2048]{1,0:T(8,128)(2,1)S(1)}, bf16[64,2048]{1,0:T(8,128)(2,1)S(1)}, u32[]{:S(2)}, u32[]{:S(2)}) collective-permute-start(bf16[64,2048]{1,0:T(8,128)(2,1)S(1)} %collective-permute-done.3), channel_id=1, source_target_pairs={{0,4},{1,5},{4,8},{5,9},{8,12},{9,13},{12,14},{13,15},{14,10},{15,... | collective-permute-start | bytes 786440 | tf_op jit(solution)/shard_map/ppermute | solution.py:165
  80.0 11.3 %collective-permute-start.11 = (bf16[64,2048]{1,0:T(8,128)(2,1)S(1)}, bf16[64,2048]{1,0:T(8,128)(2,1)S(1)}, u32[]{:S(2)}, u32[]{:S(2)}) collective-permute-start(bf16[64,2048]{1,0:T(8,128)(2,1)S(1)} %collective-permute-done.2), channel_id=1, source_target_pairs={{4,0},{5,1},{8,4},{9,5},{12,8},{13,9},{14,12},{15,13},{10,14},{11,... | collective-permute-start | bytes 786440 | tf_op jit(solution)/shard_map/ppermute | solution.py:166
  86.5 37.3 %collective-permute-start.34 = (bf16[320,2048]{1,0:T(8,128)(2,1)}, bf16[320,2048]{1,0:T(8,128)(2,1)S(1)}, u32[]{:S(2)}, u32[]{:S(2)}) collective-permute-start(bf16[320,2048]{1,0:T(8,128)(2,1)} %get-tuple-element.55), channel_id=1, source_target_pairs={{0,1},{1,0},{2,3},{3,2},{4,5},{5,4},{6,7},{7,6},{8,9},{9,8},{10,11... | collective-permute-start | bytes 3932168 | tf_op jit(solution)/shard_map/ppermute | solution.py:252
  96.5 14.8 %collective-permute-start.15 = (bf16[192,2048]{1,0:T(8,128)(2,1)S(1)}, bf16[192,2048]{1,0:T(8,128)(2,1)S(1)}, u32[]{:S(2)}, u32[]{:S(2)}) collective-permute-start(bf16[192,2048]{1,0:T(8,128)(2,1)S(1)} %pad_maximum_fusion.2), channel_id=1, source_target_pairs={{0,1},{1,0},{2,3},{3,2},{4,5},{5,4},{6,7},{7,6},{8,9},{9,8},{10,11... | collective-permute-start | bytes 2359304 | tf_op jit(solution)/shard_map/ppermute | solution.py:252
  98.9 38.9 %collective-permute-start.4 = (bf16[320,2048]{1,0:T(8,128)(2,1)}, bf16[320,2048]{1,0:T(8,128)(2,1)S(1)}, u32[]{:S(2)}, u32[]{:S(2)}) collective-permute-start(bf16[320,2048]{1,0:T(8,128)(2,1)} %get-tuple-element.45), channel_id=1, source_target_pairs={{0,1},{1,0},{2,3},{3,2},{4,5},{5,4},{6,7},{7,6},{8,9},{9,8},{10,11... | collective-permute-start | bytes 3932168 | tf_op jit(solution)/shard_map/ppermute | solution.py:252
  111.3 41.2 %collective-permute-start.41 = (bf16[192,2048]{1,0:T(8,128)(2,1)}, bf16[192,2048]{1,0:T(8,128)(2,1)S(1)}, u32[]{:S(2)}, u32[]{:S(2)}) collective-permute-start(bf16[192,2048]{1,0:T(8,128)(2,1)} %get-tuple-element.20), channel_id=1, source_target_pairs={{0,1},{1,0},{2,3},{3,2},{4,5},{5,4},{6,7},{7,6},{8,9},{9,8},{10,11... | collective-permute-start | bytes 2359304 | tf_op jit(solution)/shard_map/ppermute | solution.py:256
  123.3 31.4 %collective-permute-start.21 = (bf16[192,2048]{1,0:T(8,128)(2,1)}, bf16[192,2048]{1,0:T(8,128)(2,1)S(1)}, u32[]{:S(2)}, u32[]{:S(2)}) collective-permute-start(bf16[192,2048]{1,0:T(8,128)(2,1)} %get-tuple-element.16), channel_id=1, source_target_pairs={{0,1},{1,0},{2,3},{3,2},{4,5},{5,4},{6,7},{7,6},{8,9},{9,8},{10,11... | collective-permute-start | bytes 2359304 | tf_op jit(solution)/shard_map/ppermute | solution.py:256
  137.8 33.1 %collective-permute-start.35 = (bf16[320,2048]{1,0:T(8,128)(2,1)}, bf16[320,2048]{1,0:T(8,128)(2,1)S(1)}, u32[]{:S(2)}, u32[]{:S(2)}) collective-permute-start(bf16[320,2048]{1,0:T(8,128)(2,1)} %get-tuple-element.18), channel_id=1, source_target_pairs={{0,1},{1,0},{2,3},{3,2},{4,5},{5,4},{6,7},{7,6},{8,9},{9,8},{10,11... | collective-permute-start | bytes 3932168 | tf_op jit(solution)/shard_map/ppermute | solution.py:256
  152.0 25.7 %collective-permute-start.10 = (bf16[320,2048]{1,0:T(8,128)(2,1)}, bf16[320,2048]{1,0:T(8,128)(2,1)S(1)}, u32[]{:S(2)}, u32[]{:S(2)}) collective-permute-start(bf16[320,2048]{1,0:T(8,128)(2,1)} %get-tuple-element.14), channel_id=1, source_target_pairs={{0,1},{1,0},{2,3},{3,2},{4,5},{5,4},{6,7},{7,6},{8,9},{9,8},{10,11... | collective-permute-start | bytes 3932168 | tf_op jit(solution)/shard_map/ppermute | solution.py:256
  159.2 9.3 %collective-permute-start.43 = (bf16[64,2048]{1,0:T(8,128)(2,1)S(1)}, bf16[64,2048]{1,0:T(8,128)(2,1)S(1)}, u32[]{:S(2)}, u32[]{:S(2)}) collective-permute-start(bf16[64,2048]{1,0:T(8,128)(2,1)S(1)} %get-tuple-element.37), channel_id=1, source_target_pairs={{0,4},{1,5},{4,8},{5,9},{8,12},{9,13},{12,14},{13,15},{14,10},{15,... | collective-permute-start | bytes 786440 | tf_op jit(solution)/shard_map/ppermute | solution.py:189
  161.5 9.4 %collective-permute-start.47 = (bf16[64,2048]{1,0:T(8,128)(2,1)S(1)}, bf16[64,2048]{1,0:T(8,128)(2,1)S(1)}, u32[]{:S(2)}, u32[]{:S(2)}) collective-permute-start(bf16[64,2048]{1,0:T(8,128)(2,1)S(1)} %get-tuple-element.38), channel_id=1, source_target_pairs={{4,0},{5,1},{8,4},{9,5},{12,8},{13,9},{14,12},{15,13},{10,14},{11,... | collective-permute-start | bytes 786440 | tf_op jit(solution)/shard_map/ppermute | solution.py:190
  171.2 12.1 %collective-permute-start.48 = (bf16[64,2048]{1,0:T(8,128)(2,1)S(1)}, bf16[64,2048]{1,0:T(8,128)(2,1)S(1)}, u32[]{:S(2)}, u32[]{:S(2)}) collective-permute-start(bf16[64,2048]{1,0:T(8,128)(2,1)S(1)} %get-tuple-element.34), channel_id=1, source_target_pairs={{4,0},{5,1},{8,4},{9,5},{12,8},{13,9},{14,12},{15,13},{10,14},{11,... | collective-permute-start | bytes 786440 | tf_op jit(solution)/shard_map/ppermute | solution.py:190
  (41 other events, 311.9 us)

commit v2 on v1

v2 whole, which is shorter than its diff:
```python
import functools
import math

import jax
import jax.numpy as jnp
import numpy as np
from jax import lax
from jax.experimental import pallas as pl
from jax.experimental.pallas import tpu as pltpu
from jax.sharding import PartitionSpec as P

F32 = jnp.float32
BF16 = jnp.bfloat16


def attend_kernel(token_ref, q_ref, kv_ref, *refs, devices):
    out_ref, next_ref = refs[-2:]
    next_ref[...] = token_ref[...]
    length, feat_width = q_ref.shape
    context, head_size = kv_ref.shape[1:]
    scale = math.log2(math.e) / math.sqrt(head_size)
    keys, values = kv_ref[0], kv_ref[1]
    row = lax.broadcasted_iota(jnp.int32, (length, length), 0)
    col = lax.broadcasted_iota(jnp.int32, (length, length), 1)
    allowed = col <= row
    for head in range(feat_width // head_size):
        cols = slice(head * head_size, (head + 1) * head_size)
        scores = lax.dot_general(
            q_ref[:, cols], keys, (((1,), (1,)), ((), ())), preferred_element_type=F32
        )
        cached = scores[:, : context - length]
        fresh = jnp.where(allowed, scores[:, context - length :], -1e30)
        highest = jnp.maximum(
            jnp.max(cached, axis=-1, keepdims=True), jnp.max(fresh, axis=-1, keepdims=True)
        )
        grown = jnp.concatenate(
            [jnp.exp2((cached - highest) * scale), jnp.exp2((fresh - highest) * scale)], axis=1
        )
        total = jnp.sum(grown, axis=-1, keepdims=True)
        blended = jnp.dot(grown.astype(BF16), values, preferred_element_type=F32)
        out_ref[:, cols] = (blended / total).astype(BF16)
    if len(refs) == 4:
        ids_ref, gates_ref = refs[:2]
        batches, top, tokens = ids_ref.shape
        tables = []
        for batch in range(batches):
            shares = gates_ref[batch].astype(F32)
            shares = shares / jnp.sum(shares, axis=0, keepdims=True)
            expert = lax.broadcasted_iota(jnp.int32, (devices, tokens), 0)
            table = jnp.zeros((devices, tokens), F32)
            for k in range(top):
                named = expert == ids_ref[batch, k : k + 1]
                table += jnp.where(named, shares[k : k + 1], 0.0)
            tables.append(table)
        table = jnp.concatenate(tables, axis=1)
        rest = length // devices
        lines = batches * tokens
        high = table.astype(BF16).astype(F32)
        part = lax.broadcasted_iota(jnp.int32, (devices, rest, lines), 1)
        spread = [jnp.broadcast_to(x[:, None, :], part.shape) for x in (high, table - high)]
        both = jnp.where(part == 0, spread[0], jnp.where(part == 1, spread[1], 0.0))
        out_ref[:, feat_width:] = both.reshape(length, lines).astype(BF16)


def attend(token, queries, keys_values, batch, devices, *choices):
    length, feat_width = queries.shape[2:]
    context, head_size = keys_values.shape[3:]
    pairs = length * (feat_width // head_size) * context
    choices = [jnp.swapaxes(c, 1, 2) for c in choices]
    width = feat_width + (choices[0].shape[0] * choices[0].shape[2] if choices else 0)
    once = lambda shape: pl.BlockSpec(shape, lambda i: (0,) * len(shape))
    return pl.pallas_call(
        functools.partial(attend_kernel, devices=devices),
        out_shape=(
            jax.ShapeDtypeStruct((length, width), BF16),
            jax.ShapeDtypeStruct(token.shape, token.dtype),
        ),
        grid=(1,),
        in_specs=[
            once(token.shape),
            pl.BlockSpec((None, None, length, feat_width), lambda i: (batch, 0, 0, 0)),
            pl.BlockSpec((None, None, 2, context, head_size), lambda i: (batch, 0, 0, 0, 0)),
        ]
        + [once(c.shape) for c in choices],
        out_specs=(once((length, width)), once(token.shape)),
        compiler_params=pltpu.CompilerParams(vmem_limit_bytes=10 << 20),
        cost_estimate=pl.CostEstimate(
            flops=4 * pairs * head_size,
            bytes_accessed=2 * (2 * length * feat_width + 2 * context * head_size),
            transcendentals=pairs,
        ),
        name="attend",
    )(token, queries, keys_values, *choices)


def prepare_kernel(rows_ref, residual_ref, gain_ref, own_ref):
    stream = residual_ref[...].astype(F32) + rows_ref[...].astype(F32)
    meansq = jnp.mean(stream * stream, axis=-1, keepdims=True)
    own_ref[...] = (stream * lax.rsqrt(meansq + 1e-06) * gain_ref[...]).astype(BF16)


def prepare(rows, residual, norm_gain, batch):
    tokens, model_width = rows.shape
    return pl.pallas_call(
        prepare_kernel,
        out_shape=jax.ShapeDtypeStruct(rows.shape, BF16),
        grid=(1,),
        in_specs=[
            pl.BlockSpec((tokens, model_width), lambda i: (0, 0)),
            pl.BlockSpec((None, tokens, model_width), lambda i: (batch, 0, 0)),
            pl.BlockSpec((1, model_width), lambda i: (0, 0)),
        ],
        out_specs=pl.BlockSpec((tokens, model_width), lambda i: (0, 0)),
        compiler_params=pltpu.CompilerParams(vmem_limit_bytes=4 << 20),
        name="prepare",
    )(rows, residual, norm_gain.reshape(1, model_width))


def ring_place(device, step, devices):
    chips = devices // 2
    chip, core = device // 2, device % 2
    place = jnp.where(chip % 2 == 0, chip // 2, chips - 1 - chip // 2)
    place = (place + step) % chips
    chip = jnp.where(place < chips // 2, 2 * place, 2 * (chips - 1 - place) + 1)
    return 2 * chip + core


def expert_kernel(me_ref, token_ref, share_ref, gate_up_ref, down_ref, *refs, places, offset):
    blocks = len(places)
    x_refs = refs[: 2 * blocks]
    mine_ref, other_ref, next_ref, x_all, hidden_ref = refs[2 * blocks :]
    next_ref[...] = token_ref[...]
    tokens, model_width = x_refs[0].shape
    rows = blocks * tokens
    hidden_width = down_ref.shape[1]
    devices, lanes = share_ref.shape
    part = min(256, hidden_width)
    chunk = min(512, model_width)
    for block, x_ref in enumerate(x_refs):
        x_all[block * tokens : (block + 1) * tokens] = x_ref[...]
    for start in range(0, hidden_width, part):
        gate = jnp.dot(
            x_all[...], gate_up_ref[0, :, start : start + part], preferred_element_type=F32
        )
        up = jnp.dot(
            x_all[...],
            gate_up_ref[0, :, hidden_width + start : hidden_width + start + part],
            preferred_element_type=F32,
        )
        hidden_ref[:, start : start + part] = (gate / (1.0 + jnp.exp(-gate)) * up).astype(BF16)
    token = lax.broadcasted_iota(jnp.int32, (tokens, lanes), 0)
    lane = lax.broadcasted_iota(jnp.int32, (tokens, lanes), 1)
    diagonal = lane == token + offset
    shares = []
    for plane in range(2):
        for place in places:
            source = ring_place(me_ref[0], place, devices) ^ plane
            line = share_ref[pl.ds(source, 1), :]
            spread = jnp.where(diagonal, jnp.broadcast_to(line, (tokens, lanes)), 0.0)
            shares.append(jnp.sum(spread, axis=-1, keepdims=True))
    share = jnp.concatenate(shares, axis=0)
    for start in range(0, model_width, chunk):
        total = jnp.dot(
            hidden_ref[...], down_ref[0, :, start : start + chunk], preferred_element_type=F32
        )
        weighted = (total * share).astype(BF16)
        mine_ref[:, start : start + chunk] = weighted[:rows]
        other_ref[:, start : start + chunk] = weighted[rows:]


def run_expert(me, token, shares, gate_up, down_proj, held, swapped, places, batch):
    tokens, model_width = held[0].shape
    rows = len(held) * tokens
    hidden_width = down_proj.shape[1]
    whole = pl.BlockSpec(memory_space=pltpu.VMEM)
    half = jax.ShapeDtypeStruct((rows, model_width), BF16)
    gate_up = pltpu.with_memory_space_constraint(gate_up, pltpu.VMEM)
    down_proj = pltpu.with_memory_space_constraint(down_proj, pltpu.VMEM)
    return pl.pallas_call(
        functools.partial(expert_kernel, places=places, offset=batch * tokens),
        out_shape=[half, half, jax.ShapeDtypeStruct(token.shape, token.dtype)],
        in_specs=[pl.BlockSpec(memory_space=pltpu.SMEM)] + [whole] * (4 + 2 * len(held)),
        out_specs=[whole] * 3,
        scratch_shapes=[
            pltpu.VMEM((2 * rows, model_width), BF16),
            pltpu.VMEM((2 * rows, hidden_width), BF16),
        ],
        compiler_params=pltpu.CompilerParams(vmem_limit_bytes=5 << 20),
        cost_estimate=pl.CostEstimate(flops=1, bytes_accessed=1, transcendentals=0),
        name="expert",
    )(me, token, shares, gate_up, down_proj, *held, *swapped)


def load_kernel(token_ref, gate_up_ref, down_ref, next_ref, gate_up_out, down_out, sems):
    copies = [
        pltpu.make_async_copy(gate_up_ref, gate_up_out, sems.at[0]),
        pltpu.make_async_copy(down_ref, down_out, sems.at[1]),
    ]
    for copy in copies:
        copy.start()
    next_ref[...] = token_ref[...]
    for copy in copies:
        copy.wait()


def load(token, gate_up, down_proj):
    whole = pl.BlockSpec(memory_space=pltpu.VMEM)
    source = pl.BlockSpec(memory_space=pl.ANY)
    gate_up = pltpu.with_memory_space_constraint(gate_up, pltpu.HBM)
    down_proj = pltpu.with_memory_space_constraint(down_proj, pltpu.HBM)
    return pl.pallas_call(
        load_kernel,
        out_shape=[
            jax.ShapeDtypeStruct(token.shape, token.dtype),
            pltpu.VMEM(gate_up.shape, gate_up.dtype),
            pltpu.VMEM(down_proj.shape, down_proj.dtype),
        ],
        in_specs=[whole, source, source],
        out_specs=[whole, whole, whole],
        scratch_shapes=[pltpu.SemaphoreType.DMA((2,))],
        compiler_params=pltpu.CompilerParams(vmem_limit_bytes=1 << 20),
        name="load",
    )(token, gate_up, down_proj)


def ring_orders(devices):
    chips = devices // 2
    order = [2 * r if r < chips // 2 else 2 * (chips - 1 - r) + 1 for r in range(chips)]
    forward = [
        (2 * order[r] + core, 2 * order[(r + 1) % chips] + core)
        for r in range(chips)
        for core in range(2)
    ]
    backward = [(b, a) for a, b in forward]
    swap = [(i, i ^ 1) for i in range(devices)]
    return forward, backward, swap


def add(*terms):
    total = terms[0].astype(F32)
    for term in terms[1:]:
        total = total + term.astype(F32)
    return total


def to_owners(arrived, kv_heads):
    sources, positions, feat_width = arrived.shape
    grouped = arrived.reshape(sources // kv_heads, kv_heads, positions, feat_width)
    grouped = jnp.transpose(grouped, (0, 2, 1, 3))
    return grouped.reshape(sources // kv_heads * positions, kv_heads * feat_width)


class Line:
    def __init__(self):
        self.token = jnp.zeros((16, 128), F32)

    def hold(self, values):
        values, self.token = lax.optimization_barrier((values, self.token))
        return values


def body(queries, keys_values, residual, norm_gain, gate_up, down_proj, expert_ids, expert_gates):
    devices = lax.axis_size("dev")
    batches, tokens, model_width = residual.shape
    length, feat_width = queries.shape[2:]
    kv_heads = model_width // feat_width
    forward, backward, swap = ring_orders(devices)
    chips = devices // 2
    reach = chips // 2
    half = model_width // 2
    me = lax.axis_index("dev").astype(jnp.int32).reshape(1)
    send_ahead = lambda x: lax.ppermute(x, "dev", forward)
    send_behind = lambda x: lax.ppermute(x, "dev", backward)
    swapped = lambda x: lax.ppermute(x, "dev", swap)
    line = Line()

    queries = pltpu.with_memory_space_constraint(queries, pltpu.HBM)
    keys_values = pltpu.with_memory_space_constraint(keys_values, pltpu.HBM)

    def exchange(heads):
        return lax.all_to_all(
            heads.reshape(devices, length // devices, -1),
            "dev",
            split_axis=0,
            concat_axis=0,
            tiled=True,
        )

    class Chain:
        def __init__(self, batch):
            self.batch = batch
            self.held = {}
            self.others = {}
            self.outs = {}
            self.pending = []

        def prepare(self, arrived):
            arrived = line.hold(arrived)
            self.rows = to_owners(arrived[..., :feat_width], kv_heads)
            own = prepare(self.rows, residual, norm_gain, self.batch)
            self.held[0] = [own]
            self.moving = [own, own]
            return arrived

        def start(self, step):
            if step > reach:
                self.start_back(step - reach)
            elif step < reach:
                self.moving = [send_ahead(self.moving[0]), send_behind(self.moving[1])]
            else:
                self.moving = [
                    send_ahead(self.moving[0][:, :half]),
                    send_behind(self.moving[1][:, half:]),
                ]

        def land(self, step):
            self.moving = line.hold(self.moving)
            if step < reach:
                self.held[step] = [self.moving[1], self.moving[0]]
            elif step == reach:
                self.held[step] = [jnp.concatenate(self.moving, axis=1)]

        def swap(self, step):
            self.others[step] = [swapped(x) for x in self.held[step]]

        def expert(self, step):
            places = [step] if step in (0, reach) else [step, chips - step]
            mine, other, line.token = run_expert(
                me, line.token, shares, gate_up, down_proj, self.held[step], self.others[step],
                places, self.batch,
            )
            self.outs[step] = [mine, swapped(other)]

        def settle(self, step):
            self.outs[step] = line.hold(self.outs[step])

        def start_back(self, step):
            mine, other = self.outs[reach + 1 - step]
            if step == 1:
                total = add(mine, other).astype(BF16)
                sums = [total[:, :half], total[:, half:]]
            else:
                ahead, behind = self.moving
                if step == 2:
                    empty = jnp.zeros_like(ahead)
                    ahead = jnp.concatenate([ahead, empty], axis=1)
                    behind = jnp.concatenate([empty, behind], axis=1)
                sums = [
                    add(ahead, mine[:tokens], other[:tokens]).astype(BF16),
                    add(behind, mine[tokens:], other[tokens:]).astype(BF16),
                ]
            sums = line.hold(sums)
            self.moving = [send_ahead(sums[0]), send_behind(sums[1])]

        def finish(self):
            return add(
                residual[self.batch], self.rows, *self.outs[0], *self.moving
            ).astype(BF16)

    heads, line.token = attend(
        line.token, queries, keys_values, 0, devices, expert_ids, expert_gates
    )
    arrived = exchange(heads)
    later, line.token = attend(line.token, queries, keys_values, 1, devices)
    line.token, gate_up, down_proj = load(line.token, gate_up, down_proj)

    a, b = [Chain(batch) for batch in range(batches)]
    arrived = a.prepare(arrived)
    shares = arrived[:, 0, feat_width:].astype(F32) + arrived[:, 1, feat_width:].astype(F32)
    later, a.held[0][0] = lax.optimization_barrier((later, a.held[0][0]))
    a.moving = a.held[0] * 2
    arrived = exchange(later)
    a.start(1)
    a.swap(0)
    a.expert(0)
    a.land(1)
    a.swap(1)
    a.start(2)
    a.land(2)
    a.swap(2)
    a.start(3)
    b.prepare(arrived)
    b.start(1)
    b.swap(0)
    a.settle(0)
    for step in range(3, reach + 1):
        a.expert(step - 2)
        a.land(step)
        a.swap(step)
        if step < reach:
            a.start(step + 1)
        b.land(step - 2)
        b.swap(step - 2)
        b.start(step - 1)
        if step > 3:
            a.settle(step - 3)
    a.expert(reach - 1)
    a.expert(reach)
    b.land(reach - 1)
    b.swap(reach - 1)
    b.start(reach)
    a.settle(reach - 2)
    b.expert(0)
    a.settle(reach - 1)
    a.settle(reach)
    a.start(reach + 1)
    b.land(reach)
    b.swap(reach)
    b.expert(1)
    a.land(reach + 1)
    a.start(reach + 2)
    for step in range(2, reach):
        b.expert(step)
        b.settle(step - 2)
    b.expert(reach)
    a.land(reach + 2)
    a.start(reach + 3)
    b.settle(reach - 2)
    b.settle(reach - 1)
    b.settle(reach)
    b.start(reach + 1)
    for step in range(reach + 3, 2 * reach):
        a.land(step)
        a.start(step + 1)
        b.land(step - 2)
        b.start(step - 1)
    a.land(2 * reach)
    for step in range(2 * reach - 2, 2 * reach):
        b.land(step)
        b.start(step + 1)
    b.land(2 * reach)
    return jnp.stack([a.finish(), b.finish()], axis=0)


def solution(mesh):
    in_specs = (
        P(None, ("groups", "dev"), None, None),
        P(None, ("groups", "dev"), None, None, None),
        P(None, ("groups", "dev"), None),
        P(),
        P("dev", None, None),
        P("dev", None, None),
        P(None, ("groups", "dev"), None),
        P(None, ("groups", "dev"), None),
    )
    out_specs = P(None, ("groups", "dev"), None)
    return jax.shard_map(body, mesh=mesh, in_specs=in_specs, out_specs=out_specs, check_vma=False)
```

time: 200 us -> 173 us (0.86)
  waiting for transfers between devices: 67.4 us -> 53.5 us
  Pallas kernels: 55.9 us -> 44.1 us
  local copies, waits for them, and re-layouts: 13 us -> 17.7 us
  other arithmetic: 9.08 us -> 5.17 us
    pallas_call x6 -> x15, Pallas kernels: 55.9 us -> 44.1 us  [the longest x10 27.5 us: run_expert(): pl.pallas_call(functools.partial(expert_kernel, places=places, offset=bat...]
    all_to_all x2, waiting for transfers between devices: 8.64 us -> 0.01 us  [exchange(): lax.all_to_all(heads.reshape(devices, length // devices, -1), 'dev', spli...]
    ppermute x50 -> x58, waiting for transfers between devices: 58.7 us -> 53.5 us  [the longest x16 39.4 us: body(): send_ahead = lambda x: lax.ppermute(x, 'dev', forward)]
    unnamed x40 -> x36, local copies, waits for them, and re-layouts: 8.64 us -> 13.1 us
    ppermute x50 -> x58, starting transfers between devices: 42.2 us -> 38.1 us  [the longest x16 18.8 us: body(): send_ahead = lambda x: lax.ppermute(x, 'dev', forward)]
    concatenate x7 -> x2, local copies, waits for them, and re-layouts: 4.03 us -> 0.02 us  [land(): self.held[step] = [jnp.concatenate(self.moving, axis=1)]]
    concatenate x5 -> x0, other arithmetic: 3.39 us -> none  [the longest x2 2.64 us: body(): jnp.concatenate([held, swapped], axis=0)]
    slice x7, local copies, waits for them, and re-layouts: 0.15 us -> 2.85 us  [the longest x1 0.97 us: prepare(): self.rows = to_owners(arrived[..., :feat_width], kv_heads)]
  transfers between devices with their start and end apart: 52 -> 60, of which waited for: 28 -> 25; matrix products, arithmetic and copies ran while one was open for 7% -> 4% of each run, Pallas kernels for 28% -> 22%
where the time goes in v2:
time: 173 us; the launch traced here: 172 us
  waiting for transfers between devices  53.5 us (31%)
  starting transfers between devices  51.4 us (30%)
  Pallas kernels  44.1 us (25%)
  local copies, waits for them, and re-layouts  17.7 us (10%)
  other arithmetic  5.17 us (3%)
    ppermute x16, waiting for transfers between devices, body(): send_ahead = lambda x: lax.ppermute(x, 'dev', forward)  39.4 us
    pallas_call x10, Pallas kernels, run_expert(): pl.pallas_call(functools.partial(expert_kernel, places=places, offset=bat...  27.5 us
    ppermute x16, starting transfers between devices, body(): send_ahead = lambda x: lax.ppermute(x, 'dev', forward)  18.8 us
    ppermute x16, waiting for transfers between devices, body(): send_behind = lambda x: lax.ppermute(x, 'dev', backward)  14 us
    ppermute x16, starting transfers between devices, body(): send_behind = lambda x: lax.ppermute(x, 'dev', backward)  14 us
    all_to_all x2, starting transfers between devices, exchange(): lax.all_to_all(heads.reshape(devices, length // devices, -1), 'dev', spli...  13.2 us
    unnamed x36, local copies, waits for them, and re-layouts  13.1 us
    pallas_call x2, Pallas kernels, attend(): pl.pallas_call(functools.partial(attend_kernel, devices=devices), out_sha...  10.8 us
  transfers between devices with their start and end apart: 60, of which 25 were waited for; matrix products, arithmetic and copies ran while one was open for 4% of the time, Pallas kernels for 22%

profile of v2, /device:TPU:0, one launch (start us, length us, event | category | flops | bytes accessed | tf_op | source)
XLA Modules:
  0.0 172.2 jit_solution(13593377178265605638)
XLA Ops:
  1.4 5.8 %attend.2 = (bf16[128,1152]{1,0:T(8,128)(2,1)}, f32[16,128]{1,0:T(8,128)S(1)}) custom-call(f32[16,128]{1,0:T(8,128)S(1)} %broadcast_in_dim.3.token_ref, bf16[2,1,128,1024]{3,2,1,0:T(8,128)(2,1)} %q_ref.3, bf16[2,1,2,1664,128]{4,3,2,1,0:T(8,128)(2,1)} %kv_ref.3, s32[2,8,64]{2,1,0:T(8,128)S(1)} %bitcast.33, s32[2,8,64]{2,1,0:T(8,128)S(1)} %bitcast.34), custom_call_target="tpu_custom_call" | custom-call | flops 872415232 | bytes 1376256 | tf_op jit(solution)/shard_map/attend/pallas_call | solution.py:72
  7.2 7.4 %all-to-all-start = ((bf16[16,8,1152]{2,1,0:T(8,128)(2,1)}), bf16[16,8,1152]{2,1,0:T(8,128)(2,1)}, u32[]{:S(2)}, u32[]{:S(2)}) async-start(bf16[16,8,1152]{2,1,0:T(8,128)(2,1)} %bitcast.3), calls=%async_computation | async-start | bytes 589824 | tf_op jit(solution)/shard_map/all_to_all | solution.py:281
  14.6 5.0 %attend.3 = (bf16[128,1024]{1,0:T(8,128)(2,1)S(1)}, f32[16,128]{1,0:T(8,128)S(1)}) custom-call(f32[16,128]{1,0:T(8,128)S(1)} %get-tuple-element.136.token_ref, bf16[2,1,128,1024]{3,2,1,0:T(8,128)(2,1)} %q_ref.3, bf16[2,1,2,1664,128]{4,3,2,1,0:T(8,128)(2,1)} %kv_ref.3), custom_call_target="tpu_custom_call" | custom-call | flops 872415232 | bytes 1376256 | tf_op jit(solution)/shard_map/attend/pallas_call | solution.py:72
  20.4 3.7 %load.1 = (f32[16,128]{1,0:T(8,128)S(1)}, bf16[1,2048,1536]{2,1,0:T(8,128)(2,1)S(1)}, bf16[1,768,2048]{2,1,0:T(8,128)(2,1)S(1)}) custom-call(f32[16,128]{1,0:T(8,128)S(1)} %get-tuple-element.137.token_ref, bf16[1,2048,1536]{2,1,0:T(8,128)(2,1)} %gate_up_ref.1, bf16[1,768,2048]{2,1,0:T(8,128)(2,1)} %down_ref.1), custom_call_target="tpu_custom_call" | custom-call | tf_op jit(solution)/shard_map/load/pallas_call | solution.py:211
  24.1 2.6 %copy-done = bf16[1,2048,1536]{2,1,0:T(8,128)(2,1)} copy-done((bf16[1,2048,1536]{2,1,0:T(8,128)(2,1)}, bf16[1,2048,1536]{2,1,0:T(8,128)(2,1)S(1)}, u32[]{:S(2)}) %copy-start) | copy-done | bytes 6291480
  33.7 5.8 %all-to-all-start.1 = ((bf16[16,8,1024]{2,1,0:T(8,128)(2,1)}), bf16[16,8,1024]{2,1,0:T(8,128)(2,1)}, u32[]{:S(2)}, u32[]{:S(2)}) async-start(bf16[16,8,1024]{2,1,0:T(8,128)(2,1)} %bitcast.30), calls=%async_computation.1 | async-start | bytes 524288 | tf_op jit(solution)/shard_map/all_to_all | solution.py:281
  40.3 2.8 %copy-done.1 = bf16[1,2048,1536]{2,1,0:T(8,128)(2,1)S(1)} copy-done((bf16[1,2048,1536]{2,1,0:T(8,128)(2,1)S(1)}, bf16[1,2048,1536]{2,1,0:T(8,128)(2,1)}, u32[]{:S(2)}) %copy-start.1) | copy-done | bytes 6291480
  43.0 3.2 %expert.10 = (bf16[64,2048]{1,0:T(8,128)(2,1)S(1)}, bf16[64,2048]{1,0:T(8,128)(2,1)}, f32[16,128]{1,0:T(8,128)S(1)}) custom-call(s32[1]{0:T(128)} %bitcast.7.me_ref, f32[16,128]{1,0:T(8,128)S(1)} %get-tuple-element.140.token_ref, f32[16,128]{1,0:T(8,128)S(1)} %add_bitcast_fusion.share_ref, bf16[1,2048,1536]{2,1,0:T(8,128)(2,1)S(1)} %copy-done.1, ...), custom_call_target="tpu_custom_call" | custom-call | flops 1 | bytes 1 | tf_op jit(solution)/shard_map/expert/pallas_call | solution.py:179
  49.5 6.3 %collective-permute-done.4.refs_1_ = bf16[64,2048]{1,0:T(8,128)(2,1)} collective-permute-done((bf16[64,2048]{1,0:T(8,128)(2,1)}, bf16[64,2048]{1,0:T(8,128)(2,1)}, u32[]{:S(2)}, u32[]{:S(2)}) %collective-permute-start.4) | collective-permute-done | bytes 262176 | tf_op jit(solution)/shard_map/ppermute | solution.py:272
  63.5 3.3 %collective-permute-done.11.refs_1_ = bf16[64,2048]{1,0:T(8,128)(2,1)} collective-permute-done((bf16[64,2048]{1,0:T(8,128)(2,1)}, bf16[64,2048]{1,0:T(8,128)(2,1)}, u32[]{:S(2)}, u32[]{:S(2)}) %collective-permute-start.11) | collective-permute-done | bytes 262176 | tf_op jit(solution)/shard_map/ppermute | solution.py:272
  66.8 2.8 %copy-done.2 = bf16[1,2048,1536]{2,1,0:T(8,128)(2,1)S(1)} copy-done((bf16[1,2048,1536]{2,1,0:T(8,128)(2,1)S(1)}, bf16[1,2048,1536]{2,1,0:T(8,128)(2,1)}, u32[]{:S(2)}) %copy-start.2) | copy-done | bytes 6291480
  69.6 4.0 %expert.11 = (bf16[128,2048]{1,0:T(8,128)(2,1)S(1)}, bf16[128,2048]{1,0:T(8,128)(2,1)S(1)}, f32[16,128]{1,0:T(8,128)S(1)}) custom-call(s32[1]{0:T(128)} %bitcast.7.me_ref, f32[16,128]{1,0:T(8,128)S(1)} %get-tuple-element.156.token_ref, f32[16,128]{1,0:T(8,128)S(1)} %add_bitcast_fusion.share_ref, bf16[1,2048,1536]{2,1,0:T(8,128)(2,1)S(1)} %copy-done.2, ...), custom_call_target="tpu_custom_call" | custom-call | flops 1 | bytes 1 | tf_op jit(solution)/shard_map/expert/pallas_call | solution.py:179
  84.0 3.7 %expert.12 = (bf16[128,2048]{1,0:T(8,128)(2,1)S(1)}, bf16[128,2048]{1,0:T(8,128)(2,1)S(1)}, f32[16,128]{1,0:T(8,128)S(1)}) custom-call(s32[1]{0:T(128)} %bitcast.7.me_ref, f32[16,128]{1,0:T(8,128)S(1)} %get-tuple-element.168.token_ref, f32[16,128]{1,0:T(8,128)S(1)} %add_bitcast_fusion.share_ref, bf16[1,2048,1536]{2,1,0:T(8,128)(2,1)S(1)} %copy-done.3, ...), custom_call_target="tpu_custom_call" | custom-call | flops 1 | bytes 1 | tf_op jit(solution)/shard_map/expert/pallas_call | solution.py:179
  88.4 3.7 %expert.13 = (bf16[128,2048]{1,0:T(8,128)(2,1)S(1)}, bf16[128,2048]{1,0:T(8,128)(2,1)S(1)}, f32[16,128]{1,0:T(8,128)S(1)}) custom-call(s32[1]{0:T(128)} %bitcast.7.me_ref, f32[16,128]{1,0:T(8,128)S(1)} %get-tuple-element.172.token_ref, f32[16,128]{1,0:T(8,128)S(1)} %add_bitcast_fusion.share_ref, bf16[1,2048,1536]{2,1,0:T(8,128)(2,1)S(1)} %copy-done.3, ...), custom_call_target="tpu_custom_call" | custom-call | flops 1 | bytes 1 | tf_op jit(solution)/shard_map/expert/pallas_call | solution.py:179
  96.1 4.8 %collective-permute-done.25.refs_1_ = bf16[64,2048]{1,0:T(8,128)(2,1)S(1)} collective-permute-done((bf16[64,2048]{1,0:T(8,128)(2,1)S(1)}, bf16[64,2048]{1,0:T(8,128)(2,1)S(1)}, u32[]{:S(2)}, u32[]{:S(2)}) %collective-permute-start.25) | collective-permute-done | bytes 262176 | tf_op jit(solution)/shard_map/ppermute | solution.py:272
  106.2 4.0 %collective-permute-done.30 = bf16[64,1024]{1,0:T(8,128)(2,1)S(1)} collective-permute-done((bf16[64,1024]{1,0:T(8,128)(2,1)S(1)}, bf16[64,1024]{1,0:T(8,128)(2,1)S(1)}, u32[]{:S(2)}, u32[]{:S(2)}) %collective-permute-start.30) | collective-permute-done | bytes 131104 | tf_op jit(solution)/shard_map/ppermute | solution.py:272
  110.8 4.4 %collective-permute-done.31 = bf16[64,1024]{1,0:T(8,128)(2,1)S(1)} collective-permute-done((bf16[64,1024]{1,0:T(8,128)(2,1)S(1)}, bf16[64,1024]{1,0:T(8,128)(2,1)S(1)}, u32[]{:S(2)}, u32[]{:S(2)}) %collective-permute-start.31) | collective-permute-done | bytes 131104 | tf_op jit(solution)/shard_map/ppermute | solution.py:273
  117.2 2.7 %expert.16 = (bf16[128,2048]{1,0:T(8,128)(2,1)S(1)}, bf16[128,2048]{1,0:T(8,128)(2,1)S(1)}, f32[16,128]{1,0:T(8,128)S(1)}) custom-call(s32[1]{0:T(128)} %bitcast.7.me_ref, f32[16,128]{1,0:T(8,128)S(1)} %get-tuple-element.197.token_ref, f32[16,128]{1,0:T(8,128)S(1)} %add_bitcast_fusion.share_ref, bf16[1,2048,1536]{2,1,0:T(8,128)(2,1)S(1)} %copy-done.3, ...), custom_call_target="tpu_custom_call" | custom-call | flops 1 | bytes 1 | tf_op jit(solution)/shard_map/expert/pallas_call | solution.py:179
  122.3 2.7 %expert.17 = (bf16[128,2048]{1,0:T(8,128)(2,1)S(1)}, bf16[128,2048]{1,0:T(8,128)(2,1)S(1)}, f32[16,128]{1,0:T(8,128)S(1)}) custom-call(s32[1]{0:T(128)} %bitcast.7.me_ref, f32[16,128]{1,0:T(8,128)S(1)} %get-tuple-element.210.token_ref, f32[16,128]{1,0:T(8,128)S(1)} %add_bitcast_fusion.share_ref, bf16[1,2048,1536]{2,1,0:T(8,128)(2,1)S(1)} %copy-done.3, ...), custom_call_target="tpu_custom_call" | custom-call | flops 1 | bytes 1 | tf_op jit(solution)/shard_map/expert/pallas_call | solution.py:179
  127.1 2.7 %expert.18 = (bf16[128,2048]{1,0:T(8,128)(2,1)S(1)}, bf16[128,2048]{1,0:T(8,128)(2,1)S(1)}, f32[16,128]{1,0:T(8,128)S(1)}) custom-call(s32[1]{0:T(128)} %bitcast.7.me_ref, f32[16,128]{1,0:T(8,128)S(1)} %get-tuple-element.212.token_ref, f32[16,128]{1,0:T(8,128)S(1)} %add_bitcast_fusion.share_ref, bf16[1,2048,1536]{2,1,0:T(8,128)(2,1)S(1)} %copy-done.3, ...), custom_call_target="tpu_custom_call" | custom-call | flops 1 | bytes 1 | tf_op jit(solution)/shard_map/expert/pallas_call | solution.py:179
  143.7 2.5 %collective-permute-done.43 = bf16[64,2048]{1,0:T(8,128)(2,1)S(1)} collective-permute-done((bf16[64,2048]{1,0:T(8,128)(2,1)S(1)}, bf16[64,2048]{1,0:T(8,128)(2,1)S(1)}, u32[]{:S(2)}, u32[]{:S(2)}) %collective-permute-start.43) | collective-permute-done | bytes 262176 | tf_op jit(solution)/shard_map/ppermute | solution.py:272
  147.1 3.5 %collective-permute-done.51 = bf16[64,2048]{1,0:T(8,128)(2,1)S(1)} collective-permute-done((bf16[64,2048]{1,0:T(8,128)(2,1)S(1)}, bf16[64,2048]{1,0:T(8,128)(2,1)S(1)}, u32[]{:S(2)}, u32[]{:S(2)}) %collective-permute-start.51) | collective-permute-done | bytes 262176 | tf_op jit(solution)/shard_map/ppermute | solution.py:272
  155.8 4.9 %collective-permute-done.54 = bf16[64,2048]{1,0:T(8,128)(2,1)S(1)} collective-permute-done((bf16[64,2048]{1,0:T(8,128)(2,1)S(1)}, bf16[64,2048]{1,0:T(8,128)(2,1)S(1)}, u32[]{:S(2)}, u32[]{:S(2)}) %collective-permute-start.54) | collective-permute-done | bytes 262176 | tf_op jit(solution)/shard_map/ppermute | solution.py:272
  166.9 2.5 %collective-permute-done.56 = bf16[64,2048]{1,0:T(8,128)(2,1)S(1)} collective-permute-done((bf16[64,2048]{1,0:T(8,128)(2,1)}, bf16[64,2048]{1,0:T(8,128)(2,1)S(1)}, u32[]{:S(2)}, u32[]{:S(2)}) %collective-permute-start.56) | collective-permute-done | bytes 262176 | tf_op jit(solution)/shard_map/ppermute | solution.py:272
  (169 shorter events, 77.2 us)
Async XLA Ops:
  7.2 19.6 %all-to-all-start = ((bf16[16,8,1152]{2,1,0:T(8,128)(2,1)}), bf16[16,8,1152]{2,1,0:T(8,128)(2,1)}, u32[]{:S(2)}, u32[]{:S(2)}) async-start(bf16[16,8,1152]{2,1,0:T(8,128)(2,1)} %bitcast.3), calls=%async_computation | async-start | bytes 589824 | tf_op jit(solution)/shard_map/all_to_all | solution.py:281
  29.6 10.6 %collective-permute-start = (bf16[64,2048]{1,0:T(8,128)(2,1)}, bf16[64,2048]{1,0:T(8,128)(2,1)}, u32[]{:S(2)}, u32[]{:S(2)}) collective-permute-start(bf16[64,2048]{1,0:T(8,128)(2,1)} %prepare.2.refs_0_), channel_id=1, source_target_pairs={{0,1},{1,0},{2,3},{3,2},{4,5},{5,4},{6,7},{7,6},{8,9},{9,8},{10,11... | collective-permute-start | bytes 786440 | tf_op jit(solution)/shard_map/ppermute | solution.py:274
  30.0 17.0 %collective-permute-start.2 = (bf16[64,2048]{1,0:T(8,128)(2,1)}, bf16[64,2048]{1,0:T(8,128)(2,1)}, u32[]{:S(2)}, u32[]{:S(2)}) collective-permute-start(bf16[64,2048]{1,0:T(8,128)(2,1)} %prepare.2.refs_0_), channel_id=1, source_target_pairs={{0,4},{1,5},{4,8},{5,9},{8,12},{9,13},{12,14},{13,15},{14,10},{15,... | collective-permute-start | bytes 786440 | tf_op jit(solution)/shard_map/ppermute | solution.py:272
  31.7 15.3 %collective-permute-start.3 = (bf16[64,2048]{1,0:T(8,128)(2,1)}, bf16[64,2048]{1,0:T(8,128)(2,1)}, u32[]{:S(2)}, u32[]{:S(2)}) collective-permute-start(bf16[64,2048]{1,0:T(8,128)(2,1)} %prepare.2.refs_0_), channel_id=1, source_target_pairs={{4,0},{5,1},{8,4},{9,5},{12,8},{13,9},{14,12},{15,13},{10,14},{11,... | collective-permute-start | bytes 786440 | tf_op jit(solution)/shard_map/ppermute | solution.py:273
  33.7 25.5 %all-to-all-start.1 = ((bf16[16,8,1024]{2,1,0:T(8,128)(2,1)}), bf16[16,8,1024]{2,1,0:T(8,128)(2,1)}, u32[]{:S(2)}, u32[]{:S(2)}) async-start(bf16[16,8,1024]{2,1,0:T(8,128)(2,1)} %bitcast.30), calls=%async_computation.1 | async-start | bytes 524288 | tf_op jit(solution)/shard_map/all_to_all | solution.py:281
  49.0 12.4 %collective-permute-start.1 = (bf16[64,2048]{1,0:T(8,128)(2,1)}, bf16[64,2048]{1,0:T(8,128)(2,1)}, u32[]{:S(2)}, u32[]{:S(2)}) collective-permute-start(bf16[64,2048]{1,0:T(8,128)(2,1)} %get-tuple-element.146), channel_id=1, source_target_pairs={{0,1},{1,0},{2,3},{3,2},{4,5},{5,4},{6,7},{7,6},{8,9},{9,8},{10,11... | collective-permute-start | bytes 786440 | tf_op jit(solution)/shard_map/ppermute | solution.py:274
  49.0 14.0 %collective-permute-start.6 = (bf16[64,2048]{1,0:T(8,128)(2,1)}, bf16[64,2048]{1,0:T(8,128)(2,1)}, u32[]{:S(2)}, u32[]{:S(2)}) collective-permute-start(bf16[64,2048]{1,0:T(8,128)(2,1)} %collective-permute-done.3.refs_0_), channel_id=1, source_target_pairs={{0,1},{1,0},{2,3},{3,2},{4,5},{5,4},{6,7},{7,6},{8,9},{9,8},{10,11... | collective-permute-start | bytes 786440 | tf_op jit(solution)/shard_map/ppermute | solution.py:274
  49.5 14.0 %collective-permute-start.7 = (bf16[64,2048]{1,0:T(8,128)(2,1)}, bf16[64,2048]{1,0:T(8,128)(2,1)}, u32[]{:S(2)}, u32[]{:S(2)}) collective-permute-start(bf16[64,2048]{1,0:T(8,128)(2,1)} %collective-permute-done.2.refs_1_), channel_id=1, source_target_pairs={{0,1},{1,0},{2,3},{3,2},{4,5},{5,4},{6,7},{7,6},{8,9},{9,8},{10,11... | collective-permute-start | bytes 786440 | tf_op jit(solution)/shard_map/ppermute | solution.py:274
  58.7 14.9 %collective-permute-start.12 = (bf16[64,2048]{1,0:T(8,128)(2,1)}, bf16[64,2048]{1,0:T(8,128)(2,1)}, u32[]{:S(2)}, u32[]{:S(2)}) collective-permute-start(bf16[64,2048]{1,0:T(8,128)(2,1)} %collective-permute-done.5.refs_0_), channel_id=1, source_target_pairs={{4,0},{5,1},{8,4},{9,5},{12,8},{13,9},{14,12},{15,13},{10,14},{11,... | collective-permute-start | bytes 786440 | tf_op jit(solution)/shard_map/ppermute | solution.py:273
  61.5 14.6 %collective-permute-start.9 = (bf16[64,2048]{1,0:T(8,128)(2,1)S(1)}, bf16[64,2048]{1,0:T(8,128)(2,1)S(1)}, u32[]{:S(2)}, u32[]{:S(2)}) collective-permute-start(bf16[64,2048]{1,0:T(8,128)(2,1)S(1)} %prepare.3.refs_0_), channel_id=1, source_target_pairs={{0,4},{1,5},{4,8},{5,9},{8,12},{9,13},{12,14},{13,15},{14,10},{15,... | collective-permute-start | bytes 786440 | tf_op jit(solution)/shard_map/ppermute | solution.py:272
  63.0 14.6 %collective-permute-start.10 = (bf16[64,2048]{1,0:T(8,128)(2,1)S(1)}, bf16[64,2048]{1,0:T(8,128)(2,1)S(1)}, u32[]{:S(2)}, u32[]{:S(2)}) collective-permute-start(bf16[64,2048]{1,0:T(8,128)(2,1)S(1)} %prepare.3.refs_0_), channel_id=1, source_target_pairs={{4,0},{5,1},{8,4},{9,5},{12,8},{13,9},{14,12},{15,13},{10,14},{11,... | collective-permute-start | bytes 786440 | tf_op jit(solution)/shard_map/ppermute | solution.py:273
  63.5 14.6 %collective-permute-start.17 = (bf16[64,2048]{1,0:T(8,128)(2,1)}, bf16[64,2048]{1,0:T(8,128)(2,1)S(1)}, u32[]{:S(2)}, u32[]{:S(2)}) collective-permute-start(bf16[64,2048]{1,0:T(8,128)(2,1)} %collective-permute-done.5.refs_0_), channel_id=1, source_target_pairs={{0,1},{1,0},{2,3},{3,2},{4,5},{5,4},{6,7},{7,6},{8,9},{9,8},{10,11... | collective-permute-start | bytes 786440 | tf_op jit(solution)/shard_map/ppermute | solution.py:274
  66.8 12.8 %collective-permute-start.18 = (bf16[64,2048]{1,0:T(8,128)(2,1)}, bf16[64,2048]{1,0:T(8,128)(2,1)S(1)}, u32[]{:S(2)}, u32[]{:S(2)}) collective-permute-start(bf16[64,2048]{1,0:T(8,128)(2,1)} %collective-permute-done.4.refs_1_), channel_id=1, source_target_pairs={{0,1},{1,0},{2,3},{3,2},{4,5},{5,4},{6,7},{7,6},{8,9},{9,8},{10,11... | collective-permute-start | bytes 786440 | tf_op jit(solution)/shard_map/ppermute | solution.py:274
  73.6 14.8 %collective-permute-start.8 = (bf16[128,2048]{1,0:T(8,128)(2,1)S(1)}, bf16[128,2048]{1,0:T(8,128)(2,1)S(1)}, u32[]{:S(2)}, u32[]{:S(2)}) collective-permute-start(bf16[128,2048]{1,0:T(8,128)(2,1)S(1)} %get-tuple-element.158), channel_id=1, source_target_pairs={{0,1},{1,0},{2,3},{3,2},{4,5},{5,4},{6,7},{7,6},{8,9},{9,8},{10,11... | collective-permute-start | bytes 1572872 | tf_op jit(solution)/shard_map/ppermute | solution.py:274
  87.7 14.4 %collective-permute-start.24 = (bf16[128,2048]{1,0:T(8,128)(2,1)S(1)}, bf16[128,2048]{1,0:T(8,128)(2,1)S(1)}, u32[]{:S(2)}, u32[]{:S(2)}) collective-permute-start(bf16[128,2048]{1,0:T(8,128)(2,1)S(1)} %get-tuple-element.181), channel_id=1, source_target_pairs={{0,1},{1,0},{2,3},{3,2},{4,5},{5,4},{6,7},{7,6},{8,9},{9,8},{10,11... | collective-permute-start | bytes 1572872 | tf_op jit(solution)/shard_map/ppermute | solution.py:274
  92.1 12.1 %collective-permute-start.23 = (bf16[128,2048]{1,0:T(8,128)(2,1)S(1)}, bf16[128,2048]{1,0:T(8,128)(2,1)S(1)}, u32[]{:S(2)}, u32[]{:S(2)}) collective-permute-start(bf16[128,2048]{1,0:T(8,128)(2,1)S(1)} %get-tuple-element.179), channel_id=1, source_target_pairs={{0,1},{1,0},{2,3},{3,2},{4,5},{5,4},{6,7},{7,6},{8,9},{9,8},{10,11... | collective-permute-start | bytes 1572872 | tf_op jit(solution)/shard_map/ppermute | solution.py:274
  102.1 14.5 %collective-permute-start.32 = (bf16[64,2048]{1,0:T(8,128)(2,1)S(1)}, bf16[64,2048]{1,0:T(8,128)(2,1)S(1)}, u32[]{:S(2)}, u32[]{:S(2)}) collective-permute-start(bf16[64,2048]{1,0:T(8,128)(2,1)S(1)} %collective-permute-done.10.refs_0_), channel_id=1, source_target_pairs={{0,1},{1,0},{2,3},{3,2},{4,5},{5,4},{6,7},{7,6},{8,9},{9,8},{10,11... | collective-permute-start | bytes 786440 | tf_op jit(solution)/shard_map/ppermute | solution.py:274
  102.1 15.1 %collective-permute-start.33 = (bf16[64,2048]{1,0:T(8,128)(2,1)S(1)}, bf16[64,2048]{1,0:T(8,128)(2,1)S(1)}, u32[]{:S(2)}, u32[]{:S(2)}) collective-permute-start(bf16[64,2048]{1,0:T(8,128)(2,1)S(1)} %collective-permute-done.9.refs_1_), channel_id=1, source_target_pairs={{0,1},{1,0},{2,3},{3,2},{4,5},{5,4},{6,7},{7,6},{8,9},{9,8},{10,11... | collective-permute-start | bytes 786440 | tf_op jit(solution)/shard_map/ppermute | solution.py:274
  102.6 19.0 %collective-permute-start.38 = (bf16[64,2048]{1,0:T(8,128)(2,1)S(1)}, bf16[64,2048]{1,0:T(8,128)(2,1)S(1)}, u32[]{:S(2)}, u32[]{:S(2)}) collective-permute-start(bf16[64,2048]{1,0:T(8,128)(2,1)S(1)} %collective-permute-done.14.refs_0_), channel_id=1, source_target_pairs={{0,1},{1,0},{2,3},{3,2},{4,5},{5,4},{6,7},{7,6},{8,9},{9,8},{10,11... | collective-permute-start | bytes 786440 | tf_op jit(solution)/shard_map/ppermute | solution.py:274
  104.2 17.9 %collective-permute-start.39 = (bf16[64,2048]{1,0:T(8,128)(2,1)S(1)}, bf16[64,2048]{1,0:T(8,128)(2,1)S(1)}, u32[]{:S(2)}, u32[]{:S(2)}) collective-permute-start(bf16[64,2048]{1,0:T(8,128)(2,1)S(1)} %collective-permute-done.13.refs_1_), channel_id=1, source_target_pairs={{0,1},{1,0},{2,3},{3,2},{4,5},{5,4},{6,7},{7,6},{8,9},{9,8},{10,11... | collective-permute-start | bytes 786440 | tf_op jit(solution)/shard_map/ppermute | solution.py:274
  119.9 9.9 %collective-permute-start.36 = (bf16[128,2048]{1,0:T(8,128)(2,1)S(1)}, bf16[128,2048]{1,0:T(8,128)(2,1)S(1)}, u32[]{:S(2)}, u32[]{:S(2)}) collective-permute-start(bf16[128,2048]{1,0:T(8,128)(2,1)S(1)} %get-tuple-element.207), channel_id=1, source_target_pairs={{0,1},{1,0},{2,3},{3,2},{4,5},{5,4},{6,7},{7,6},{8,9},{9,8},{10,11... | collective-permute-start | bytes 1572872 | tf_op jit(solution)/shard_map/ppermute | solution.py:274
  132.3 14.8 %collective-permute-start.53 = (bf16[128,2048]{1,0:T(8,128)(2,1)S(1)}, bf16[128,2048]{1,0:T(8,128)(2,1)S(1)}, u32[]{:S(2)}, u32[]{:S(2)}) collective-permute-start(bf16[128,2048]{1,0:T(8,128)(2,1)S(1)} %get-tuple-element.251), channel_id=1, source_target_pairs={{0,1},{1,0},{2,3},{3,2},{4,5},{5,4},{6,7},{7,6},{8,9},{9,8},{10,11... | collective-permute-start | bytes 1572872 | tf_op jit(solution)/shard_map/ppermute | solution.py:274
  153.7 12.6 %collective-permute-start.45 = (bf16[64,2048]{1,0:T(8,128)(2,1)S(1)}, bf16[64,2048]{1,0:T(8,128)(2,1)S(1)}, u32[]{:S(2)}, u32[]{:S(2)}) collective-permute-start(bf16[64,2048]{1,0:T(8,128)(2,1)S(1)} %get-tuple-element.229), channel_id=1, source_target_pairs={{0,4},{1,5},{4,8},{5,9},{8,12},{9,13},{12,14},{13,15},{14,10},{15,... | collective-permute-start | bytes 786440 | tf_op jit(solution)/shard_map/ppermute | solution.py:272
  154.4 12.5 %collective-permute-start.46 = (bf16[64,2048]{1,0:T(8,128)(2,1)S(1)}, bf16[64,2048]{1,0:T(8,128)(2,1)S(1)}, u32[]{:S(2)}, u32[]{:S(2)}) collective-permute-start(bf16[64,2048]{1,0:T(8,128)(2,1)S(1)} %get-tuple-element.230), channel_id=1, source_target_pairs={{4,0},{5,1},{8,4},{9,5},{12,8},{13,9},{14,12},{15,13},{10,14},{11,... | collective-permute-start | bytes 786440 | tf_op jit(solution)/shard_map/ppermute | solution.py:273
  (53 other events, 394.3 us)

commit v3 on v0

v3 whole, which is shorter than its diff:
```python
import functools
import math

import jax
import jax.numpy as jnp
import numpy as np
from jax import lax
from jax.experimental import pallas as pl
from jax.experimental.pallas import tpu as pltpu
from jax.sharding import PartitionSpec as P

F32 = jnp.float32
BF16 = jnp.bfloat16


def attend_kernel(q_ref, kv_ref, ids_ref, gates_ref, out_ref, *, devices):
    length, feat_width = q_ref.shape
    context, head_size = kv_ref.shape[1:]
    positions = length // devices
    scale = math.log2(math.e) / math.sqrt(head_size)
    keys, values = kv_ref[0], kv_ref[1]
    row = lax.broadcasted_iota(jnp.int32, (length, length), 0)
    col = lax.broadcasted_iota(jnp.int32, (length, length), 1)
    allowed = col <= row

    def put(cols, value):
        if len(out_ref.shape) == 3:
            value = value.reshape(devices, positions, value.shape[-1])
            out_ref[:, :, cols] = value.astype(BF16)
        else:
            out_ref[:, cols] = value.astype(BF16)

    for head in range(feat_width // head_size):
        cols = slice(head * head_size, (head + 1) * head_size)
        scores = lax.dot_general(
            q_ref[:, cols], keys, (((1,), (1,)), ((), ())), preferred_element_type=F32
        )
        cached = scores[:, : context - length]
        fresh = jnp.where(allowed, scores[:, context - length :], -1e30)
        highest = jnp.maximum(
            jnp.max(cached, axis=-1, keepdims=True), jnp.max(fresh, axis=-1, keepdims=True)
        )
        grown = jnp.concatenate(
            [jnp.exp2((cached - highest) * scale), jnp.exp2((fresh - highest) * scale)], axis=1
        )
        total = jnp.sum(grown, axis=-1, keepdims=True)
        blended = jnp.dot(grown.astype(BF16), values, preferred_element_type=F32)
        put(cols, blended / total)

    batches, top, tokens = ids_ref.shape
    lines = batches * tokens
    last = slice(feat_width, feat_width + lines)
    tables = []
    for batch in range(batches):
        shares = gates_ref[batch].astype(F32)
        shares = shares / jnp.sum(shares, axis=0, keepdims=True)
        expert = lax.broadcasted_iota(jnp.int32, (devices, tokens), 0)
        table = jnp.zeros((devices, tokens), F32)
        for k in range(top):
            named = expert == ids_ref[batch, k : k + 1]
            table += jnp.where(named, shares[k : k + 1], 0.0)
        tables.append(table)
    table = jnp.concatenate(tables, axis=1)
    high = table.astype(BF16).astype(F32)
    part = lax.broadcasted_iota(jnp.int32, (devices, positions, lines), 1)
    spread = [jnp.broadcast_to(x[:, None, :], part.shape) for x in (high, table - high)]
    both = jnp.where(part == 0, spread[0], jnp.where(part == 1, spread[1], 0.0))
    put(last, both.reshape(length, lines))


def attend(queries, keys_values, expert_ids, expert_gates, devices):
    batches, _, length, feat_width = queries.shape
    context, head_size = keys_values.shape[3:]
    positions = length // devices
    pairs = batches * length * (feat_width // head_size) * context
    queries, keys_values, *choices = [
        pltpu.with_memory_space_constraint(x, pltpu.HBM)
        for x in (
            queries,
            keys_values,
            jnp.swapaxes(expert_ids, 1, 2),
            jnp.swapaxes(expert_gates, 1, 2),
        )
    ]
    width = feat_width + batches * expert_ids.shape[1]
    direct = positions % 8 == 0
    if direct:
        shape = (devices, batches, positions, width)
        out_spec = pl.BlockSpec((devices, None, positions, width), lambda i: (0, i, 0, 0))
    else:
        shape = (batches, length, width)
        out_spec = pl.BlockSpec((None, length, width), lambda i: (i, 0, 0))
    rows = pl.pallas_call(
        functools.partial(attend_kernel, devices=devices),
        out_shape=jax.ShapeDtypeStruct(shape, BF16),
        grid=(batches,),
        in_specs=[
            pl.BlockSpec((None, None, length, feat_width), lambda i: (i, 0, 0, 0)),
            pl.BlockSpec((None, None, 2, context, head_size), lambda i: (i, 0, 0, 0, 0)),
        ]
        + [pl.BlockSpec(c.shape, lambda i: (0, 0, 0)) for c in choices],
        out_specs=out_spec,
        compiler_params=pltpu.CompilerParams(vmem_limit_bytes=24 << 20),
        cost_estimate=pl.CostEstimate(
            flops=4 * pairs * head_size,
            bytes_accessed=2 * batches * (2 * length * feat_width + 2 * context * head_size),
            transcendentals=pairs,
        ),
        name="attend",
    )(queries, keys_values, *choices)
    if not direct:
        rows = jnp.swapaxes(rows.reshape(batches, devices, positions, width), 0, 1)
    return rows


def prepare_kernel(arrived_ref, residual_ref, gain_ref, left_ref, right_ref, *stream_refs, kv_heads):
    batches, tokens, model_width = residual_ref.shape
    feat_width = model_width // kv_heads
    half = model_width // batches
    for batch, stream_ref in enumerate(stream_refs):
        if len(arrived_ref.shape) == 4:
            sources, _, positions, _ = arrived_ref.shape
            for source in range(sources):
                first = source // kv_heads * positions
                left = source % kv_heads * feat_width
                stream_ref[first : first + positions, left : left + feat_width] = arrived_ref[
                    source, batch, :, :feat_width
                ].astype(F32)
            rows = stream_ref[...]
        else:
            rows = arrived_ref[batch].astype(F32)
        stream = residual_ref[batch].astype(F32) + rows
        stream_ref[...] = stream
        meansq = jnp.mean(stream * stream, axis=-1, keepdims=True)
        own = (stream * lax.rsqrt(meansq + 1e-06) * gain_ref[...]).astype(BF16)
        left_ref[:, batch * half : (batch + 1) * half] = own[:, :half]
        right_ref[:, batch * half : (batch + 1) * half] = own[:, half:]


def prepare(arrived, residual, norm_gain, kv_heads):
    batches, tokens, model_width = residual.shape
    sources, _, positions, _ = arrived.shape
    feat_width = model_width // kv_heads
    if positions % 8:
        rows = arrived[..., :feat_width]
        rows = rows.reshape(sources // kv_heads, kv_heads, batches, positions, feat_width)
        arrived = jnp.transpose(rows, (2, 0, 3, 1, 4)).reshape(batches, tokens, model_width)
    row = (tokens, model_width)
    whole = pl.BlockSpec(memory_space=pltpu.VMEM)
    left, right, *streams = pl.pallas_call(
        functools.partial(prepare_kernel, kv_heads=kv_heads),
        out_shape=[jax.ShapeDtypeStruct(row, BF16)] * 2
        + [jax.ShapeDtypeStruct(row, F32)] * batches,
        in_specs=[whole] * 3,
        out_specs=[whole] * (2 + batches),
        compiler_params=pltpu.CompilerParams(vmem_limit_bytes=8 << 20),
        name="prepare",
    )(arrived, residual, norm_gain.reshape(1, model_width))
    return left, right, streams


def ring_place(device, step, devices):
    chips = devices // 2
    chip, core = device // 2, device % 2
    place = jnp.where(chip % 2 == 0, chip // 2, chips - 1 - chip // 2)
    place = (place + step) % chips
    chip = jnp.where(place < chips // 2, 2 * place, 2 * (chips - 1 - place) + 1)
    return 2 * chip + core


def expert_kernel(me_ref, token_ref, share_a, share_b, gate_up_a, gate_up_b, down_a, down_b, *refs, places):
    *held_refs, out_ref, next_ref, x_all, hidden_a, hidden_b = refs
    next_ref[...] = token_ref[...]
    tokens, model_width = held_refs[0].shape
    half = model_width // 2
    blocks = len(places)
    hidden_width = down_a.shape[1]
    devices, lanes = share_a.shape
    part = min(256, hidden_width)
    chunk = min(512, half)

    row_of = lambda block, batch: (block * 2 + batch) * tokens
    for block in range(blocks):
        for side in range(2):
            cols = slice(side * half, (side + 1) * half)
            for batch in range(2):
                row = row_of(block, batch)
                came = slice(batch * half, (batch + 1) * half)
                x_all[row : row + tokens, cols] = held_refs[2 * block + side][:, came]
    token = lax.broadcasted_iota(jnp.int32, (tokens, lanes), 0)
    lane = lax.broadcasted_iota(jnp.int32, (tokens, lanes), 1)
    for share_ref, gate_up_ref, hidden_ref in (
        (share_a, gate_up_a, hidden_a),
        (share_b, gate_up_b, hidden_b),
    ):
        shares = []
        for place in places:
            source = ring_place(me_ref[0], place, devices)
            line = jnp.broadcast_to(share_ref[pl.ds(source, 1), :], (tokens, lanes))
            for batch in range(2):
                spread = jnp.where(lane == token + batch * tokens, line, 0.0)
                shares.append(jnp.sum(spread, axis=-1, keepdims=True))
        share = jnp.concatenate(shares, axis=0)
        for start in range(0, hidden_width, part):
            gate = jnp.dot(
                x_all[...], gate_up_ref[0, :, start : start + part], preferred_element_type=F32
            )
            up = jnp.dot(
                x_all[...],
                gate_up_ref[0, :, hidden_width + start : hidden_width + start + part],
                preferred_element_type=F32,
            )
            act = gate / (1.0 + jnp.exp(-gate)) * up
            hidden_ref[:, start : start + part] = (act * share).astype(BF16)
    for start in range(0, model_width, chunk):
        cols = slice(start, start + chunk)
        total = jnp.dot(hidden_a[...], down_a[0, :, cols], preferred_element_type=F32)
        total += jnp.dot(hidden_b[...], down_b[0, :, cols], preferred_element_type=F32)
        weighted = total.astype(BF16)
        side, left = start // half, start % half
        for block in range(blocks):
            rows = slice((2 * block + side) * tokens, (2 * block + side + 1) * tokens)
            for batch in range(2):
                row = row_of(block, batch)
                goes = slice(batch * half + left, batch * half + left + chunk)
                out_ref[rows, goes] = weighted[row : row + tokens]


def run_experts(me, token, shares, weights, held, places):
    tokens, model_width = held[0].shape
    rows = tokens * len(held)
    hidden_width = weights[2].shape[1]
    whole = pl.BlockSpec(memory_space=pltpu.VMEM)
    return pl.pallas_call(
        functools.partial(expert_kernel, places=places),
        out_shape=[
            jax.ShapeDtypeStruct((rows, model_width), BF16),
            jax.ShapeDtypeStruct(token.shape, token.dtype),
        ],
        in_specs=[pl.BlockSpec(memory_space=pltpu.SMEM)] + [whole] * (7 + len(held)),
        out_specs=[whole] * 2,
        scratch_shapes=[
            pltpu.VMEM((rows, model_width), BF16),
            pltpu.VMEM((rows, hidden_width), BF16),
            pltpu.VMEM((rows, hidden_width), BF16),
        ],
        compiler_params=pltpu.CompilerParams(vmem_limit_bytes=10 << 20),
        cost_estimate=pl.CostEstimate(flops=1, bytes_accessed=1, transcendentals=0),
        name="experts",
    )(me, token, *shares, *weights, *held)


def load_kernel(token_ref, *refs):
    count = len(refs) // 2 - 1
    next_ref, *out_refs = refs[count:-1]
    copies = [
        pltpu.make_async_copy(ref, out_ref, refs[-1].at[k])
        for k, (ref, out_ref) in enumerate(zip(refs[:count], out_refs))
    ]
    for copy in copies:
        copy.start()
    next_ref[...] = token_ref[...]
    for copy in copies:
        copy.wait()


def load(token, *arrays):
    whole = pl.BlockSpec(memory_space=pltpu.VMEM)
    place = pl.BlockSpec(memory_space=pl.ANY)
    return pl.pallas_call(
        load_kernel,
        out_shape=[jax.ShapeDtypeStruct(x.shape, x.dtype) for x in (token, *arrays)],
        in_specs=[whole] + [place] * len(arrays),
        out_specs=[whole] * (1 + len(arrays)),
        scratch_shapes=[pltpu.SemaphoreType.DMA((len(arrays),))],
        compiler_params=pltpu.CompilerParams(vmem_limit_bytes=1 << 20),
        cost_estimate=pl.CostEstimate(flops=1, bytes_accessed=1, transcendentals=0),
        name="load",
    )(token, *arrays)


def ring_orders(devices):
    chips = devices // 2
    order = [2 * r if r < chips // 2 else 2 * (chips - 1 - r) + 1 for r in range(chips)]
    forward = [
        (2 * order[r] + core, 2 * order[(r + 1) % chips] + core)
        for r in range(chips)
        for core in range(2)
    ]
    backward = [(b, a) for a, b in forward]
    swap = [(i, i ^ 1) for i in range(devices)]
    return forward, backward, swap


def fence_kernel(token_ref, *refs):
    refs[len(refs) // 2][...] = token_ref[...]


def fence(token, values):
    place = pl.BlockSpec(memory_space=pl.ANY)
    whole = pl.BlockSpec(memory_space=pltpu.VMEM)
    token, *values = pl.pallas_call(
        fence_kernel,
        out_shape=[jax.ShapeDtypeStruct(x.shape, x.dtype) for x in (token, *values)],
        in_specs=[whole] + [place] * len(values),
        out_specs=[whole] + [place] * len(values),
        input_output_aliases={k: k for k in range(1, len(values) + 1)},
        compiler_params=pltpu.CompilerParams(vmem_limit_bytes=1 << 20),
        cost_estimate=pl.CostEstimate(flops=1, bytes_accessed=4 << 20, transcendentals=0),
        name="fence",
    )(token, *values)
    return token, values


def merge_kernel(token_ref, terms_ref, *refs, cuts):
    *moving, next_ref, ahead_ref, behind_ref = refs
    next_ref[...] = token_ref[...]
    for way, out_ref in enumerate((ahead_ref, behind_ref)):
        total = terms_ref[cuts[way]]
        if moving:
            total = (total.astype(F32) + moving[way][...].astype(F32)).astype(BF16)
        out_ref[...] = total


def merge(token, terms, moving, cuts):
    whole = pl.BlockSpec(memory_space=pltpu.VMEM)
    part = jax.ShapeDtypeStruct((cuts[0].stop - cuts[0].start, terms.shape[1]), BF16)
    return pl.pallas_call(
        functools.partial(merge_kernel, cuts=cuts),
        out_shape=[jax.ShapeDtypeStruct(token.shape, token.dtype), part, part],
        in_specs=[whole] * (2 + len(moving)),
        out_specs=[whole] * 3,
        compiler_params=pltpu.CompilerParams(vmem_limit_bytes=4 << 20),
        cost_estimate=pl.CostEstimate(flops=1, bytes_accessed=1, transcendentals=0),
        name="merge",
    )(token, terms, *moving)


def finish_kernel(terms_ref, *refs):
    *sum_refs, out_ref = refs
    batches, tokens, model_width = out_ref.shape
    stream_refs, sum_refs = sum_refs[:batches], sum_refs[batches:]
    half = model_width // batches
    for side in range(2):
        total = terms_ref[side * tokens : (side + 1) * tokens].astype(F32)
        for sum_ref in sum_refs[2 * side : 2 * side + 2]:
            total = total + sum_ref[...].astype(F32)
        cols = slice(side * half, (side + 1) * half)
        for batch, stream_ref in enumerate(stream_refs):
            came = total[:, batch * half : (batch + 1) * half]
            out_ref[batch, :, cols] = (stream_ref[:, cols] + came).astype(BF16)


def finish(terms, streams, sums):
    whole = pl.BlockSpec(memory_space=pltpu.VMEM)
    return pl.pallas_call(
        finish_kernel,
        out_shape=jax.ShapeDtypeStruct((len(streams), *streams[0].shape), BF16),
        in_specs=[whole] * (1 + len(streams) + len(sums)),
        out_specs=whole,
        compiler_params=pltpu.CompilerParams(vmem_limit_bytes=8 << 20),
        name="finish",
    )(terms, *streams, *sums)


class Line:
    def __init__(self):
        self.token = jnp.zeros((16, 128), F32)

    def hold(self, values):
        self.token, values = fence(self.token, values)
        return values


def body(queries, keys_values, residual, norm_gain, gate_up, down_proj, expert_ids, expert_gates):
    devices = lax.axis_size("dev")
    batches, tokens, model_width = residual.shape
    length, feat_width = queries.shape[2:]
    kv_heads = model_width // feat_width
    forward, backward, swap = ring_orders(devices)
    chips = devices // 2
    reach = chips // 2
    half = model_width // 2
    me = lax.axis_index("dev").astype(jnp.int32).reshape(1)
    me, queries = lax.optimization_barrier((me, queries))
    send_ahead = lambda x: lax.ppermute(x, "dev", forward)
    send_behind = lambda x: lax.ppermute(x, "dev", backward)
    swapped = lambda x: lax.ppermute(x, "dev", swap)
    line = Line()

    gate_up_b, down_b = swapped(gate_up), swapped(down_proj)
    rows = attend(queries, keys_values, expert_ids, expert_gates, devices)
    arrived = lax.all_to_all(
        rows.reshape(devices, -1, rows.shape[-1]), "dev", split_axis=0, concat_axis=0, tiled=True
    )
    arrived, gate_up_b, down_b = line.hold([arrived, gate_up_b, down_b])
    arrived = arrived.reshape(rows.shape)
    left, right, streams = prepare(arrived, residual, norm_gain, kv_heads)
    shares = arrived[:, 0, 0, feat_width:].astype(F32) + arrived[:, 0, 1, feat_width:].astype(F32)
    shares = [shares, swapped(shares)]

    class Chain:
        def __init__(self, ahead, behind):
            self.moving = [ahead, behind]

        def send(self):
            self.moving = [send_ahead(self.moving[0]), send_behind(self.moving[1])]

        def land(self):
            self.moving = line.hold(self.moving)

    long, short = Chain(left, right), Chain(right, left)
    held = {0: [left, right]}
    terms = {}

    def experts(step):
        places = [step] if step in (0, reach) else [step, chips - step]
        terms[step], line.token = run_experts(
            me, line.token, shares, weights, held[step], places
        )

    def send_back(chain, step, first=False):
        sides = (0, 1) if step == reach else (0, 3) if chain is long else (1, 2)
        cuts = [slice(side * tokens, (side + 1) * tokens) for side in sides]
        line.token, *chain.moving = merge(
            line.token, terms[step], [] if first else chain.moving, cuts
        )
        chain.send()

    short.send()
    long.send()
    line.token, gate_up_b = load(line.token, gate_up_b)
    weights = [gate_up, gate_up_b, down_proj, down_b]
    for step in range(1, reach):
        short.land()
        came_right, came_left = short.moving
        if step < reach - 1:
            short.send()
        long.land()
        held[step] = [came_left, long.moving[1], long.moving[0], came_right]
        long.send()
        if step < reach - 1:
            experts(step - 1)
    experts(reach - 1)
    send_back(short, reach - 1, True)
    long.land()
    held[reach] = long.moving
    experts(reach)
    send_back(long, reach, True)
    experts(reach - 2)
    for step in range(reach - 2, 0, -1):
        send_back(short, step)
        send_back(long, step + 1)
    short.land()
    send_back(long, 1)
    ahead, behind = long.moving
    short_ahead, short_behind = short.moving
    return finish(terms[0], streams, [ahead, short_behind, behind, short_ahead])


def solution(mesh):
    in_specs = (
        P(None, ("groups", "dev"), None, None),
        P(None, ("groups", "dev"), None, None, None),
        P(None, ("groups", "dev"), None),
        P(),
        P("dev", None, None),
        P("dev", None, None),
        P(None, ("groups", "dev"), None),
        P(None, ("groups", "dev"), None),
    )
    out_specs = P(None, ("groups", "dev"), None)
    return jax.shard_map(body, mesh=mesh, in_specs=in_specs, out_specs=out_specs, check_vma=False)
```

time: 326 us -> 124 us (0.38)
  the two profiles are of different devices: /device:TPU:15 before, /device:TPU:0 now
where the time goes in v3:
time: 124 us
  Pallas kernels  35.5 us (29%)
  waiting for transfers between devices  33.8 us (27%)
  starting transfers between devices  29.4 us (24%)
  blocking collectives  24.6 us (20%)
    ppermute x14, waiting for transfers between devices, body(): send_ahead = lambda x: lax.ppermute(x, 'dev', forward)  24.6 us
    all_to_all x1, blocking collectives, body(): lax.all_to_all(rows.reshape(devices, -1, rows.shape[-1]), 'dev', split_ax...  24.6 us
    pallas_call x5, Pallas kernels, run_experts(): pl.pallas_call(functools.partial(expert_kernel, places=places), out_shape...  21.1 us
    ppermute x14, starting transfers between devices, body(): send_behind = lambda x: lax.ppermute(x, 'dev', backward)  16.5 us
    ppermute x14, starting transfers between devices, body(): send_ahead = lambda x: lax.ppermute(x, 'dev', forward)  12.3 us
    pallas_call x1, Pallas kernels, attend(): pl.pallas_call(functools.partial(attend_kernel, devices=devices), out_sha...  8.93 us
    ppermute x14, waiting for transfers between devices, body(): send_behind = lambda x: lax.ppermute(x, 'dev', backward)  8.03 us
    pallas_call x1, Pallas kernels, load(): pl.pallas_call(load_kernel, out_shape=[jax.ShapeDtypeStruct(x.shape, x.dt...  2.79 us
  transfers between devices with their start and end apart: 31, of which 18 were waited for; matrix products, arithmetic and copies ran while one was open for 0% of the time, Pallas kernels for 27%

profile of v3, /device:TPU:0, one launch (start us, length us, event | category | flops | bytes accessed | tf_op | source)
XLA Modules:
  0.0 123.7 jit_solution(14712764685630111620)
XLA Ops:
  0.5 8.9 %attend.1 = bf16[16,2,8,1152]{3,2,1,0:T(8,128)(2,1)S(1)} custom-call(bf16[2,1,128,1024]{3,2,1,0:T(8,128)(2,1)} %q_ref, bf16[2,1,2,1664,128]{4,3,2,1,0:T(8,128)(2,1)} %kv_ref.1, s32[2,8,64]{2,1,0:T(8,128)} %bitcast.15, s32[2,8,64]{2,1,0:T(8,128)} %bitcast.16), custom_call_target="tpu_custom_call" | custom-call | flops 1744830464 | bytes 2752512 | tf_op jit(solution)/shard_map/attend/pallas_call | solution.py:93
  9.5 24.6 %all_to_all.5.refs_0_ = bf16[16,16,1152]{2,1,0:T(8,128)(2,1)S(1)} all-to-all(bf16[16,16,1152]{2,1,0:T(8,128)(2,1)S(1)} %bitcast.12), channel_id=1, replica_groups=mesh['groups'=2,'dev'=16] {'dev'}, dimensions={0} | all-to-all | bytes 1179648 | tf_op jit(solution)/shard_map/all_to_all | solution.py:393
  37.2 1.4 %collective-permute-start.4 = (bf16[64,2048]{1,0:T(8,128)(2,1)S(1)}, bf16[64,2048]{1,0:T(8,128)(2,1)S(1)}, u32[]{:S(2)}, u32[]{:S(2)}) collective-permute-start(bf16[64,2048]{1,0:T(8,128)(2,1)S(1)} %get-tuple-element.78.refs_0_), channel_id=1, source_target_pairs={{0,4},{1,5},{4,8},{5,9},{8,12},{9,13},{12,14},{13,15},{14,10},{15,... | collective-permute-start | bytes 786440 | tf_op jit(solution)/shard_map/ppermute | solution.py:386
  38.6 2.8 %load.1 = (f32[16,128]{1,0:T(8,128)S(1)}, bf16[1,2048,1536]{2,1,0:T(8,128)(2,1)S(1)}) custom-call(f32[16,128]{1,0:T(8,128)S(1)} %get-tuple-element.73.token_ref, bf16[1,2048,1536]{2,1,0:T(8,128)(2,1)} %get-tuple-element.74.refs_0_), custom_call_target="tpu_custom_call" | custom-call | flops 1 | bytes 1 | tf_op jit(solution)/shard_map/load/pallas_call | solution.py:270
  41.4 2.3 %collective-permute-done.2.refs_0_ = bf16[64,2048]{1,0:T(8,128)(2,1)S(1)} collective-permute-done((bf16[64,2048]{1,0:T(8,128)(2,1)S(1)}, bf16[64,2048]{1,0:T(8,128)(2,1)S(1)}, u32[]{:S(2)}, u32[]{:S(2)}) %collective-permute-start.2) | collective-permute-done | bytes 262176 | tf_op jit(solution)/shard_map/ppermute | solution.py:386
  46.4 3.6 %collective-permute-done.5.refs_1_ = bf16[64,2048]{1,0:T(8,128)(2,1)S(1)} collective-permute-done((bf16[64,2048]{1,0:T(8,128)(2,1)S(1)}, bf16[64,2048]{1,0:T(8,128)(2,1)S(1)}, u32[]{:S(2)}, u32[]{:S(2)}) %collective-permute-start.5) | collective-permute-done | bytes 262176 | tf_op jit(solution)/shard_map/ppermute | solution.py:387
  53.4 2.8 %experts.5 = (bf16[128,2048]{1,0:T(8,128)(2,1)S(1)}, f32[16,128]{1,0:T(8,128)S(1)}) custom-call(s32[1]{0:T(128)} %bitcast.me_ref, f32[16,128]{1,0:T(8,128)S(1)} %get-tuple-element.80.token_ref, f32[16,128]{1,0:T(8,128)S(1)} %add_bitcast_fusion.share_a, f32[16,128]{1,0:T(8,128)S(1)} %collective-permute-done.6.share_b, bf16[1,2048,1536]{2,1,0:T(8,128)(2,1)S(1)} %bitcast.10, ...), custom_call_target="tpu_custom_call" | custom-call | flops 1 | bytes 1 | tf_op jit(solution)/shard_map/experts/pallas_call | solution.py:234
  58.3 2.0 %collective-permute-done.9.refs_0_ = bf16[64,2048]{1,0:T(8,128)(2,1)S(1)} collective-permute-done((bf16[64,2048]{1,0:T(8,128)(2,1)S(1)}, bf16[64,2048]{1,0:T(8,128)(2,1)S(1)}, u32[]{:S(2)}, u32[]{:S(2)}) %collective-permute-start.9) | collective-permute-done | bytes 262176 | tf_op jit(solution)/shard_map/ppermute | solution.py:386
  60.8 1.7 %collective-permute-start.14 = (bf16[64,2048]{1,0:T(8,128)(2,1)S(1)}, bf16[64,2048]{1,0:T(8,128)(2,1)S(1)}, u32[]{:S(2)}, u32[]{:S(2)}) collective-permute-start(bf16[64,2048]{1,0:T(8,128)(2,1)S(1)} %get-tuple-element.98.refs_1_), channel_id=1, source_target_pairs={{4,0},{5,1},{8,4},{9,5},{12,8},{13,9},{14,12},{15,13},{10,14},{11,... | collective-permute-start | bytes 786440 | tf_op jit(solution)/shard_map/ppermute | solution.py:387
  62.6 5.2 %experts.6 = (bf16[256,2048]{1,0:T(8,128)(2,1)S(1)}, f32[16,128]{1,0:T(8,128)S(1)}) custom-call(s32[1]{0:T(128)} %bitcast.me_ref, f32[16,128]{1,0:T(8,128)S(1)} %get-tuple-element.92.token_ref, f32[16,128]{1,0:T(8,128)S(1)} %add_bitcast_fusion.share_a, f32[16,128]{1,0:T(8,128)S(1)} %collective-permute-done.6.share_b, bf16[1,2048,1536]{2,1,0:T(8,128)(2,1)S(1)} %bitcast.10, ...), custom_call_target="tpu_custom_call" | custom-call | flops 1 | bytes 1 | tf_op jit(solution)/shard_map/experts/pallas_call | solution.py:234
  67.8 3.2 %collective-permute-done.13.refs_0_ = bf16[64,2048]{1,0:T(8,128)(2,1)S(1)} collective-permute-done((bf16[64,2048]{1,0:T(8,128)(2,1)S(1)}, bf16[64,2048]{1,0:T(8,128)(2,1)S(1)}, u32[]{:S(2)}, u32[]{:S(2)}) %collective-permute-start.13) | collective-permute-done | bytes 262176 | tf_op jit(solution)/shard_map/ppermute | solution.py:386
  71.3 1.4 %collective-permute-start.16 = (bf16[64,2048]{1,0:T(8,128)(2,1)S(1)}, bf16[64,2048]{1,0:T(8,128)(2,1)S(1)}, u32[]{:S(2)}, u32[]{:S(2)}) collective-permute-start(bf16[64,2048]{1,0:T(8,128)(2,1)S(1)} %get-tuple-element.101.refs_1_), channel_id=1, source_target_pairs={{4,0},{5,1},{8,4},{9,5},{12,8},{13,9},{14,12},{15,13},{10,14},{11,... | collective-permute-start | bytes 786440 | tf_op jit(solution)/shard_map/ppermute | solution.py:387
  73.4 5.2 %experts.7 = (bf16[256,2048]{1,0:T(8,128)(2,1)S(1)}, f32[16,128]{1,0:T(8,128)S(1)}) custom-call(s32[1]{0:T(128)} %bitcast.me_ref, f32[16,128]{1,0:T(8,128)S(1)} %get-tuple-element.99.token_ref, f32[16,128]{1,0:T(8,128)S(1)} %add_bitcast_fusion.share_a, f32[16,128]{1,0:T(8,128)S(1)} %collective-permute-done.6.share_b, bf16[1,2048,1536]{2,1,0:T(8,128)(2,1)S(1)} %bitcast.10, ...), custom_call_target="tpu_custom_call" | custom-call | flops 1 | bytes 1 | tf_op jit(solution)/shard_map/experts/pallas_call | solution.py:234
  79.3 1.4 %collective-permute-start.18 = (bf16[64,2048]{1,0:T(8,128)(2,1)S(1)}, bf16[64,2048]{1,0:T(8,128)(2,1)S(1)}, u32[]{:S(2)}, u32[]{:S(2)}) collective-permute-start(bf16[64,2048]{1,0:T(8,128)(2,1)S(1)} %get-tuple-element.116), channel_id=1, source_target_pairs={{4,0},{5,1},{8,4},{9,5},{12,8},{13,9},{14,12},{15,13},{10,14},{11,... | collective-permute-start | bytes 786440 | tf_op jit(solution)/shard_map/ppermute | solution.py:387
  80.7 2.8 %experts.8 = (bf16[128,2048]{1,0:T(8,128)(2,1)S(1)}, f32[16,128]{1,0:T(8,128)S(1)}) custom-call(s32[1]{0:T(128)} %bitcast.me_ref, f32[16,128]{1,0:T(8,128)S(1)} %get-tuple-element.107.token_ref, f32[16,128]{1,0:T(8,128)S(1)} %add_bitcast_fusion.share_a, f32[16,128]{1,0:T(8,128)S(1)} %collective-permute-done.6.share_b, bf16[1,2048,1536]{2,1,0:T(8,128)(2,1)S(1)} %bitcast.10, ...), custom_call_target="tpu_custom_call" | custom-call | flops 1 | bytes 1 | tf_op jit(solution)/shard_map/experts/pallas_call | solution.py:234
  84.2 1.4 %collective-permute-start.20 = (bf16[64,2048]{1,0:T(8,128)(2,1)S(1)}, bf16[64,2048]{1,0:T(8,128)(2,1)S(1)}, u32[]{:S(2)}, u32[]{:S(2)}) collective-permute-start(bf16[64,2048]{1,0:T(8,128)(2,1)S(1)} %get-tuple-element.119), channel_id=1, source_target_pairs={{4,0},{5,1},{8,4},{9,5},{12,8},{13,9},{14,12},{15,13},{10,14},{11,... | collective-permute-start | bytes 786440 | tf_op jit(solution)/shard_map/ppermute | solution.py:387
  85.6 5.2 %experts.9 = (bf16[256,2048]{1,0:T(8,128)(2,1)S(1)}, f32[16,128]{1,0:T(8,128)S(1)}) custom-call(s32[1]{0:T(128)} %bitcast.me_ref, f32[16,128]{1,0:T(8,128)S(1)} %get-tuple-element.112.token_ref, f32[16,128]{1,0:T(8,128)S(1)} %add_bitcast_fusion.share_a, f32[16,128]{1,0:T(8,128)S(1)} %collective-permute-done.6.share_b, bf16[1,2048,1536]{2,1,0:T(8,128)(2,1)S(1)} %bitcast.10, ...), custom_call_target="tpu_custom_call" | custom-call | flops 1 | bytes 1 | tf_op jit(solution)/shard_map/experts/pallas_call | solution.py:234
  91.7 1.4 %collective-permute-start.22 = (bf16[64,2048]{1,0:T(8,128)(2,1)S(1)}, bf16[64,2048]{1,0:T(8,128)(2,1)S(1)}, u32[]{:S(2)}, u32[]{:S(2)}) collective-permute-start(bf16[64,2048]{1,0:T(8,128)(2,1)S(1)} %get-tuple-element.123), channel_id=1, source_target_pairs={{4,0},{5,1},{8,4},{9,5},{12,8},{13,9},{14,12},{15,13},{10,14},{11,... | collective-permute-start | bytes 786440 | tf_op jit(solution)/shard_map/ppermute | solution.py:387
  93.9 1.4 %collective-permute-start.24 = (bf16[64,2048]{1,0:T(8,128)(2,1)S(1)}, bf16[64,2048]{1,0:T(8,128)(2,1)S(1)}, u32[]{:S(2)}, u32[]{:S(2)}) collective-permute-start(bf16[64,2048]{1,0:T(8,128)(2,1)S(1)} %get-tuple-element.126), channel_id=1, source_target_pairs={{4,0},{5,1},{8,4},{9,5},{12,8},{13,9},{14,12},{15,13},{10,14},{11,... | collective-permute-start | bytes 786440 | tf_op jit(solution)/shard_map/ppermute | solution.py:387
  95.3 5.0 %collective-permute-done.21.refs_0_ = bf16[64,2048]{1,0:T(8,128)(2,1)S(1)} collective-permute-done((bf16[64,2048]{1,0:T(8,128)(2,1)S(1)}, bf16[64,2048]{1,0:T(8,128)(2,1)S(1)}, u32[]{:S(2)}, u32[]{:S(2)}) %collective-permute-start.21) | collective-permute-done | bytes 262176 | tf_op jit(solution)/shard_map/ppermute | solution.py:386
  103.1 2.8 %collective-permute-done.23.refs_0_ = bf16[64,2048]{1,0:T(8,128)(2,1)S(1)} collective-permute-done((bf16[64,2048]{1,0:T(8,128)(2,1)S(1)}, bf16[64,2048]{1,0:T(8,128)(2,1)S(1)}, u32[]{:S(2)}, u32[]{:S(2)}) %collective-permute-start.23) | collective-permute-done | bytes 262176 | tf_op jit(solution)/shard_map/ppermute | solution.py:386
  108.7 2.4 %collective-permute-done.25.refs_0_ = bf16[64,2048]{1,0:T(8,128)(2,1)S(1)} collective-permute-done((bf16[64,2048]{1,0:T(8,128)(2,1)S(1)}, bf16[64,2048]{1,0:T(8,128)(2,1)S(1)}, u32[]{:S(2)}, u32[]{:S(2)}) %collective-permute-start.25) | collective-permute-done | bytes 262176 | tf_op jit(solution)/shard_map/ppermute | solution.py:386
  111.3 2.7 %collective-permute-done.27.refs_0_ = bf16[64,2048]{1,0:T(8,128)(2,1)S(1)} collective-permute-done((bf16[64,2048]{1,0:T(8,128)(2,1)S(1)}, bf16[64,2048]{1,0:T(8,128)(2,1)S(1)}, u32[]{:S(2)}, u32[]{:S(2)}) %collective-permute-start.27) | collective-permute-done | bytes 262176 | tf_op jit(solution)/shard_map/ppermute | solution.py:386
  117.0 4.3 %collective-permute-done.29.refs_2_ = bf16[64,2048]{1,0:T(8,128)(2,1)S(1)} collective-permute-done((bf16[64,2048]{1,0:T(8,128)(2,1)S(1)}, bf16[64,2048]{1,0:T(8,128)(2,1)S(1)}, u32[]{:S(2)}, u32[]{:S(2)}) %collective-permute-start.29) | collective-permute-done | bytes 262176 | tf_op jit(solution)/shard_map/ppermute | solution.py:386
  (78 shorter events, 27.7 us)
Async XLA Ops:
  0.0 34.1 %collective-permute-start = (bf16[1,2048,1536]{2,1,0:T(8,128)(2,1)}, bf16[1,2048,1536]{2,1,0:T(8,128)(2,1)}, u32[]{:S(2)}, u32[]{:S(2)}) collective-permute-start(bf16[1,2048,1536]{2,1,0:T(8,128)(2,1)} %gate_up_a.9), channel_id=1, source_target_pairs={{0,1},{1,0},{2,3},{3,2},{4,5},{5,4},{6,7},{7,6},{8,9},{9,8},{10,11... | collective-permute-start | bytes 18874376 | tf_op jit(solution)/shard_map/ppermute | solution.py:388
  0.5 33.6 %collective-permute-start.1 = (bf16[1,768,2048]{2,1,0:T(8,128)(2,1)}, bf16[1,768,2048]{2,1,0:T(8,128)(2,1)S(1)}, u32[]{:S(2)}, u32[]{:S(2)}) collective-permute-start(bf16[1,768,2048]{2,1,0:T(8,128)(2,1)} %down_a.9), channel_id=1, source_target_pairs={{0,1},{1,0},{2,3},{3,2},{4,5},{5,4},{6,7},{7,6},{8,9},{9,8},{10,11... | collective-permute-start | bytes 9437192 | tf_op jit(solution)/shard_map/ppermute | solution.py:388
  34.5 9.2 %collective-permute-start.2 = (bf16[64,2048]{1,0:T(8,128)(2,1)S(1)}, bf16[64,2048]{1,0:T(8,128)(2,1)S(1)}, u32[]{:S(2)}, u32[]{:S(2)}) collective-permute-start(bf16[64,2048]{1,0:T(8,128)(2,1)S(1)} %get-tuple-element.77.refs_1_), channel_id=1, source_target_pairs={{0,4},{1,5},{4,8},{5,9},{8,12},{9,13},{12,14},{13,15},{14,10},{15,... | collective-permute-start | bytes 786440 | tf_op jit(solution)/shard_map/ppermute | solution.py:386
  35.2 9.2 %collective-permute-start.3 = (bf16[64,2048]{1,0:T(8,128)(2,1)S(1)}, bf16[64,2048]{1,0:T(8,128)(2,1)S(1)}, u32[]{:S(2)}, u32[]{:S(2)}) collective-permute-start(bf16[64,2048]{1,0:T(8,128)(2,1)S(1)} %get-tuple-element.78.refs_0_), channel_id=1, source_target_pairs={{4,0},{5,1},{8,4},{9,5},{12,8},{13,9},{14,12},{15,13},{10,14},{11,... | collective-permute-start | bytes 786440 | tf_op jit(solution)/shard_map/ppermute | solution.py:387
  36.6 13.4 %collective-permute-start.5 = (bf16[64,2048]{1,0:T(8,128)(2,1)S(1)}, bf16[64,2048]{1,0:T(8,128)(2,1)S(1)}, u32[]{:S(2)}, u32[]{:S(2)}) collective-permute-start(bf16[64,2048]{1,0:T(8,128)(2,1)S(1)} %get-tuple-element.77.refs_1_), channel_id=1, source_target_pairs={{4,0},{5,1},{8,4},{9,5},{12,8},{13,9},{14,12},{15,13},{10,14},{11,... | collective-permute-start | bytes 786440 | tf_op jit(solution)/shard_map/ppermute | solution.py:387
  37.2 12.8 %collective-permute-start.4 = (bf16[64,2048]{1,0:T(8,128)(2,1)S(1)}, bf16[64,2048]{1,0:T(8,128)(2,1)S(1)}, u32[]{:S(2)}, u32[]{:S(2)}) collective-permute-start(bf16[64,2048]{1,0:T(8,128)(2,1)S(1)} %get-tuple-element.78.refs_0_), channel_id=1, source_target_pairs={{0,4},{1,5},{4,8},{5,9},{8,12},{9,13},{12,14},{13,15},{14,10},{15,... | collective-permute-start | bytes 786440 | tf_op jit(solution)/shard_map/ppermute | solution.py:386
  44.4 11.8 %collective-permute-start.7 = (bf16[64,2048]{1,0:T(8,128)(2,1)S(1)}, bf16[64,2048]{1,0:T(8,128)(2,1)S(1)}, u32[]{:S(2)}, u32[]{:S(2)}) collective-permute-start(bf16[64,2048]{1,0:T(8,128)(2,1)S(1)} %get-tuple-element.87.refs_3_), channel_id=1, source_target_pairs={{0,4},{1,5},{4,8},{5,9},{8,12},{9,13},{12,14},{13,15},{14,10},{15,... | collective-permute-start | bytes 786440 | tf_op jit(solution)/shard_map/ppermute | solution.py:386
  45.2 11.0 %collective-permute-start.8 = (bf16[64,2048]{1,0:T(8,128)(2,1)S(1)}, bf16[64,2048]{1,0:T(8,128)(2,1)S(1)}, u32[]{:S(2)}, u32[]{:S(2)}) collective-permute-start(bf16[64,2048]{1,0:T(8,128)(2,1)S(1)} %get-tuple-element.88.refs_0_), channel_id=1, source_target_pairs={{4,0},{5,1},{8,4},{9,5},{12,8},{13,9},{14,12},{15,13},{10,14},{11,... | collective-permute-start | bytes 786440 | tf_op jit(solution)/shard_map/ppermute | solution.py:387
  50.0 10.3 %collective-permute-start.9 = (bf16[64,2048]{1,0:T(8,128)(2,1)S(1)}, bf16[64,2048]{1,0:T(8,128)(2,1)S(1)}, u32[]{:S(2)}, u32[]{:S(2)}) collective-permute-start(bf16[64,2048]{1,0:T(8,128)(2,1)S(1)} %get-tuple-element.90.refs_2_), channel_id=1, source_target_pairs={{0,4},{1,5},{4,8},{5,9},{8,12},{9,13},{12,14},{13,15},{14,10},{15,... | collective-permute-start | bytes 786440 | tf_op jit(solution)/shard_map/ppermute | solution.py:386
  50.8 9.7 %collective-permute-start.10 = (bf16[64,2048]{1,0:T(8,128)(2,1)S(1)}, bf16[64,2048]{1,0:T(8,128)(2,1)S(1)}, u32[]{:S(2)}, u32[]{:S(2)}) collective-permute-start(bf16[64,2048]{1,0:T(8,128)(2,1)S(1)} %get-tuple-element.91.refs_1_), channel_id=1, source_target_pairs={{4,0},{5,1},{8,4},{9,5},{12,8},{13,9},{14,12},{15,13},{10,14},{11,... | collective-permute-start | bytes 786440 | tf_op jit(solution)/shard_map/ppermute | solution.py:387
  56.3 11.5 %collective-permute-start.11 = (bf16[64,2048]{1,0:T(8,128)(2,1)S(1)}, bf16[64,2048]{1,0:T(8,128)(2,1)S(1)}, u32[]{:S(2)}, u32[]{:S(2)}) collective-permute-start(bf16[64,2048]{1,0:T(8,128)(2,1)S(1)} %get-tuple-element.94.refs_3_), channel_id=1, source_target_pairs={{0,4},{1,5},{4,8},{5,9},{8,12},{9,13},{12,14},{13,15},{14,10},{15,... | collective-permute-start | bytes 786440 | tf_op jit(solution)/shard_map/ppermute | solution.py:386
  57.1 10.7 %collective-permute-start.12 = (bf16[64,2048]{1,0:T(8,128)(2,1)S(1)}, bf16[64,2048]{1,0:T(8,128)(2,1)S(1)}, u32[]{:S(2)}, u32[]{:S(2)}) collective-permute-start(bf16[64,2048]{1,0:T(8,128)(2,1)S(1)} %get-tuple-element.95.refs_0_), channel_id=1, source_target_pairs={{4,0},{5,1},{8,4},{9,5},{12,8},{13,9},{14,12},{15,13},{10,14},{11,... | collective-permute-start | bytes 786440 | tf_op jit(solution)/shard_map/ppermute | solution.py:387
  60.5 10.4 %collective-permute-start.13 = (bf16[64,2048]{1,0:T(8,128)(2,1)S(1)}, bf16[64,2048]{1,0:T(8,128)(2,1)S(1)}, u32[]{:S(2)}, u32[]{:S(2)}) collective-permute-start(bf16[64,2048]{1,0:T(8,128)(2,1)S(1)} %get-tuple-element.97.refs_2_), channel_id=1, source_target_pairs={{0,4},{1,5},{4,8},{5,9},{8,12},{9,13},{12,14},{13,15},{14,10},{15,... | collective-permute-start | bytes 786440 | tf_op jit(solution)/shard_map/ppermute | solution.py:386
  60.8 10.5 %collective-permute-start.14 = (bf16[64,2048]{1,0:T(8,128)(2,1)S(1)}, bf16[64,2048]{1,0:T(8,128)(2,1)S(1)}, u32[]{:S(2)}, u32[]{:S(2)}) collective-permute-start(bf16[64,2048]{1,0:T(8,128)(2,1)S(1)} %get-tuple-element.98.refs_1_), channel_id=1, source_target_pairs={{4,0},{5,1},{8,4},{9,5},{12,8},{13,9},{14,12},{15,13},{10,14},{11,... | collective-permute-start | bytes 786440 | tf_op jit(solution)/shard_map/ppermute | solution.py:387
  71.3 9.3 %collective-permute-start.16 = (bf16[64,2048]{1,0:T(8,128)(2,1)S(1)}, bf16[64,2048]{1,0:T(8,128)(2,1)S(1)}, u32[]{:S(2)}, u32[]{:S(2)}) collective-permute-start(bf16[64,2048]{1,0:T(8,128)(2,1)S(1)} %get-tuple-element.101.refs_1_), channel_id=1, source_target_pairs={{4,0},{5,1},{8,4},{9,5},{12,8},{13,9},{14,12},{15,13},{10,14},{11,... | collective-permute-start | bytes 786440 | tf_op jit(solution)/shard_map/ppermute | solution.py:387
  78.6 12.2 %collective-permute-start.17 = (bf16[64,2048]{1,0:T(8,128)(2,1)S(1)}, bf16[64,2048]{1,0:T(8,128)(2,1)S(1)}, u32[]{:S(2)}, u32[]{:S(2)}) collective-permute-start(bf16[64,2048]{1,0:T(8,128)(2,1)S(1)} %get-tuple-element.115), channel_id=1, source_target_pairs={{0,4},{1,5},{4,8},{5,9},{8,12},{9,13},{12,14},{13,15},{14,10},{15,... | collective-permute-start | bytes 786440 | tf_op jit(solution)/shard_map/ppermute | solution.py:386
  79.3 11.5 %collective-permute-start.18 = (bf16[64,2048]{1,0:T(8,128)(2,1)S(1)}, bf16[64,2048]{1,0:T(8,128)(2,1)S(1)}, u32[]{:S(2)}, u32[]{:S(2)}) collective-permute-start(bf16[64,2048]{1,0:T(8,128)(2,1)S(1)} %get-tuple-element.116), channel_id=1, source_target_pairs={{4,0},{5,1},{8,4},{9,5},{12,8},{13,9},{14,12},{15,13},{10,14},{11,... | collective-permute-start | bytes 786440 | tf_op jit(solution)/shard_map/ppermute | solution.py:387
  83.5 9.5 %collective-permute-start.19 = (bf16[64,2048]{1,0:T(8,128)(2,1)S(1)}, bf16[64,2048]{1,0:T(8,128)(2,1)S(1)}, u32[]{:S(2)}, u32[]{:S(2)}) collective-permute-start(bf16[64,2048]{1,0:T(8,128)(2,1)S(1)} %get-tuple-element.118), channel_id=1, source_target_pairs={{0,4},{1,5},{4,8},{5,9},{8,12},{9,13},{12,14},{13,15},{14,10},{15,... | collective-permute-start | bytes 786440 | tf_op jit(solution)/shard_map/ppermute | solution.py:386
  91.0 9.3 %collective-permute-start.21 = (bf16[64,2048]{1,0:T(8,128)(2,1)S(1)}, bf16[64,2048]{1,0:T(8,128)(2,1)S(1)}, u32[]{:S(2)}, u32[]{:S(2)}) collective-permute-start(bf16[64,2048]{1,0:T(8,128)(2,1)S(1)} %get-tuple-element.122), channel_id=1, source_target_pairs={{0,4},{1,5},{4,8},{5,9},{8,12},{9,13},{12,14},{13,15},{14,10},{15,... | collective-permute-start | bytes 786440 | tf_op jit(solution)/shard_map/ppermute | solution.py:386
  91.7 9.2 %collective-permute-start.22 = (bf16[64,2048]{1,0:T(8,128)(2,1)S(1)}, bf16[64,2048]{1,0:T(8,128)(2,1)S(1)}, u32[]{:S(2)}, u32[]{:S(2)}) collective-permute-start(bf16[64,2048]{1,0:T(8,128)(2,1)S(1)} %get-tuple-element.123), channel_id=1, source_target_pairs={{4,0},{5,1},{8,4},{9,5},{12,8},{13,9},{14,12},{15,13},{10,14},{11,... | collective-permute-start | bytes 786440 | tf_op jit(solution)/shard_map/ppermute | solution.py:387
  93.2 12.7 %collective-permute-start.23 = (bf16[64,2048]{1,0:T(8,128)(2,1)S(1)}, bf16[64,2048]{1,0:T(8,128)(2,1)S(1)}, u32[]{:S(2)}, u32[]{:S(2)}) collective-permute-start(bf16[64,2048]{1,0:T(8,128)(2,1)S(1)} %get-tuple-element.125), channel_id=1, source_target_pairs={{0,4},{1,5},{4,8},{5,9},{8,12},{9,13},{12,14},{13,15},{14,10},{15,... | collective-permute-start | bytes 786440 | tf_op jit(solution)/shard_map/ppermute | solution.py:386
  93.9 12.7 %collective-permute-start.24 = (bf16[64,2048]{1,0:T(8,128)(2,1)S(1)}, bf16[64,2048]{1,0:T(8,128)(2,1)S(1)}, u32[]{:S(2)}, u32[]{:S(2)}) collective-permute-start(bf16[64,2048]{1,0:T(8,128)(2,1)S(1)} %get-tuple-element.126), channel_id=1, source_target_pairs={{4,0},{5,1},{8,4},{9,5},{12,8},{13,9},{14,12},{15,13},{10,14},{11,... | collective-permute-start | bytes 786440 | tf_op jit(solution)/shard_map/ppermute | solution.py:387
  101.0 10.1 %collective-permute-start.25 = (bf16[64,2048]{1,0:T(8,128)(2,1)S(1)}, bf16[64,2048]{1,0:T(8,128)(2,1)S(1)}, u32[]{:S(2)}, u32[]{:S(2)}) collective-permute-start(bf16[64,2048]{1,0:T(8,128)(2,1)S(1)} %get-tuple-element.128), channel_id=1, source_target_pairs={{0,4},{1,5},{4,8},{5,9},{8,12},{9,13},{12,14},{13,15},{14,10},{15,... | collective-permute-start | bytes 786440 | tf_op jit(solution)/shard_map/ppermute | solution.py:386
  102.4 8.9 %collective-permute-start.26 = (bf16[64,2048]{1,0:T(8,128)(2,1)S(1)}, bf16[64,2048]{1,0:T(8,128)(2,1)S(1)}, u32[]{:S(2)}, u32[]{:S(2)}) collective-permute-start(bf16[64,2048]{1,0:T(8,128)(2,1)S(1)} %get-tuple-element.129), channel_id=1, source_target_pairs={{4,0},{5,1},{8,4},{9,5},{12,8},{13,9},{14,12},{15,13},{10,14},{11,... | collective-permute-start | bytes 786440 | tf_op jit(solution)/shard_map/ppermute | solution.py:387
  (12 other events, 151.7 us)

commit v4 on v3

--- a/solution.py
+++ b/solution.py
@@ -13,15 +13,19 @@
 BF16 = jnp.bfloat16
 
 
-def attend_kernel(q_ref, kv_ref, ids_ref, gates_ref, out_ref, *, devices):
+def attend_kernel(q_ref, kv_ref, ids_ref, gates_ref, out_ref, values_ref, *, devices):
     length, feat_width = q_ref.shape
     context, head_size = kv_ref.shape[1:]
     positions = length // devices
     scale = math.log2(math.e) / math.sqrt(head_size)
-    keys, values = kv_ref[0], kv_ref[1]
+    keys = kv_ref[0]
+    values_ref[:, :head_size] = kv_ref[1]
+    values_ref[:, head_size:] = jnp.ones((context, head_size), BF16)
     row = lax.broadcasted_iota(jnp.int32, (length, length), 0)
     col = lax.broadcasted_iota(jnp.int32, (length, length), 1)
-    allowed = col <= row
+    heads = feat_width // head_size
+    stack = 2 if heads % 2 == 0 else 1
+    allowed = jnp.concatenate([col <= row] * stack, axis=0)
 
     def put(cols, value):
         if len(out_ref.shape) == 3:
@@ -30,10 +34,13 @@
         else:
             out_ref[:, cols] = value.astype(BF16)
 
-    for head in range(feat_width // head_size):
-        cols = slice(head * head_size, (head + 1) * head_size)
+    for first in range(0, heads, stack):
+        cols = [slice(h * head_size, (h + 1) * head_size) for h in range(first, first + stack)]
         scores = lax.dot_general(
-            q_ref[:, cols], keys, (((1,), (1,)), ((), ())), preferred_element_type=F32
+            jnp.concatenate([q_ref[:, c] for c in cols], axis=0),
+            keys,
+            (((1,), (1,)), ((), ())),
+            preferred_element_type=F32,
         )
         cached = scores[:, : context - length]
         fresh = jnp.where(allowed, scores[:, context - length :], -1e30)
@@ -43,9 +50,10 @@
         grown = jnp.concatenate(
             [jnp.exp2((cached - highest) * scale), jnp.exp2((fresh - highest) * scale)], axis=1
         )
-        total = jnp.sum(grown, axis=-1, keepdims=True)
-        blended = jnp.dot(grown.astype(BF16), values, preferred_element_type=F32)
-        put(cols, blended / total)
+        both = jnp.dot(grown.astype(BF16), values_ref[...], preferred_element_type=F32)
+        blended = both[:, :head_size] / both[:, head_size:]
+        for k, c in enumerate(cols):
+            put(c, blended[k * length : (k + 1) * length])
 
     batches, top, tokens = ids_ref.shape
     lines = batches * tokens
@@ -100,6 +108,7 @@
         ]
         + [pl.BlockSpec(c.shape, lambda i: (0, 0, 0)) for c in choices],
         out_specs=out_spec,
+        scratch_shapes=[pltpu.VMEM((context, 2 * head_size), BF16)],
         compiler_params=pltpu.CompilerParams(vmem_limit_bytes=24 << 20),
         cost_estimate=pl.CostEstimate(
             flops=4 * pairs * head_size,
@@ -312,28 +321,30 @@
     return token, values
 
 
-def merge_kernel(token_ref, terms_ref, *refs, cuts):
+def merge_kernel(token_ref, ahead_terms, behind_terms, *refs, cuts):
     *moving, next_ref, ahead_ref, behind_ref = refs
     next_ref[...] = token_ref[...]
-    for way, out_ref in enumerate((ahead_ref, behind_ref)):
+    for way, (terms_ref, out_ref) in enumerate(
+        ((ahead_terms, ahead_ref), (behind_terms, behind_ref))
+    ):
         total = terms_ref[cuts[way]]
         if moving:
             total = (total.astype(F32) + moving[way][...].astype(F32)).astype(BF16)
         out_ref[...] = total
 
 
-def merge(token, terms, moving, cuts):
-    whole = pl.BlockSpec(memory_space=pltpu.VMEM)
-    part = jax.ShapeDtypeStruct((cuts[0].stop - cuts[0].start, terms.shape[1]), BF16)
+def merge(token, terms, cuts, moving):
+    whole = pl.BlockSpec(memory_space=pltpu.VMEM)
+    part = jax.ShapeDtypeStruct((cuts[0].stop - cuts[0].start, terms[0].shape[1]), BF16)
     return pl.pallas_call(
         functools.partial(merge_kernel, cuts=cuts),
         out_shape=[jax.ShapeDtypeStruct(token.shape, token.dtype), part, part],
-        in_specs=[whole] * (2 + len(moving)),
+        in_specs=[whole] * (3 + len(moving)),
         out_specs=[whole] * 3,
         compiler_params=pltpu.CompilerParams(vmem_limit_bytes=4 << 20),
         cost_estimate=pl.CostEstimate(flops=1, bytes_accessed=1, transcendentals=0),
         name="merge",
-    )(token, terms, *moving)
+    )(token, *terms, *moving)
 
 
 def finish_kernel(terms_ref, *refs):
@@ -413,18 +424,20 @@
     held = {0: [left, right]}
     terms = {}
 
-    def experts(step):
-        places = [step] if step in (0, reach) else [step, chips - step]
-        terms[step], line.token = run_experts(
-            me, line.token, shares, weights, held[step], places
-        )
+    def experts(*places):
+        blocks = [block for place in places for block in held[place]]
+        out, line.token = run_experts(me, line.token, shares, weights, blocks, places)
+        for k, place in enumerate(places):
+            terms[place] = (out, 2 * k * tokens)
 
     def send_back(chain, step, first=False):
-        sides = (0, 1) if step == reach else (0, 3) if chain is long else (1, 2)
-        cuts = [slice(side * tokens, (side + 1) * tokens) for side in sides]
-        line.token, *chain.moving = merge(
-            line.token, terms[step], [] if first else chain.moving, cuts
-        )
+        pairs = ((step, 0), (-step % chips, 1)) if chain is long else ((step, 1), (-step % chips, 0))
+        outs, cuts = [], []
+        for place, side in pairs:
+            out, row = terms[place]
+            outs.append(out)
+            cuts.append(slice(row + side * tokens, row + (side + 1) * tokens))
+        line.token, *chain.moving = merge(line.token, outs, cuts, [] if first else chain.moving)
         chain.send()
 
     short.send()
@@ -436,26 +449,31 @@
         came_right, came_left = short.moving
         if step < reach - 1:
             short.send()
+        if step == 2:
+            experts(chips - 1)
         long.land()
-        held[step] = [came_left, long.moving[1], long.moving[0], came_right]
+        held[step] = [came_left, long.moving[1]]
+        held[chips - step] = [long.moving[0], came_right]
         long.send()
-        if step < reach - 1:
-            experts(step - 1)
-    experts(reach - 1)
+        if step == 1:
+            experts(1)
+        else:
+            experts(step, chips - step)
     send_back(short, reach - 1, True)
     long.land()
     held[reach] = long.moving
     experts(reach)
     send_back(long, reach, True)
-    experts(reach - 2)
     for step in range(reach - 2, 0, -1):
         send_back(short, step)
         send_back(long, step + 1)
+        if step == 1:
+            experts(0)
     short.land()
     send_back(long, 1)
     ahead, behind = long.moving
     short_ahead, short_behind = short.moving
-    return finish(terms[0], streams, [ahead, short_behind, behind, short_ahead])
+    return finish(terms[0][0], streams, [ahead, short_behind, behind, short_ahead])
 
 
 def solution(mesh):

time: 124 us -> 121 us (0.976)
  Pallas kernels: 35.5 us -> 33.3 us
    ppermute x14, waiting for transfers between devices: 24.6 us -> 19.8 us  [body(): send_ahead = lambda x: lax.ppermute(x, 'dev', forward)]
    ppermute x14, waiting for transfers between devices: 8.03 us -> 12 us  [body(): send_behind = lambda x: lax.ppermute(x, 'dev', backward)]
    pallas_call x1, Pallas kernels: 8.93 us -> 6.37 us  [attend(): pl.pallas_call(functools.partial(attend_kernel, devices=devices), out_sha...]
    pallas_call x5 -> x6, Pallas kernels: 21.1 us -> 21.6 us  [run_experts(): pl.pallas_call(functools.partial(expert_kernel, places=places), out_shape...]
  transfers between devices with their start and end apart: 31 -> 31, of which waited for: 18 -> 19; matrix products, arithmetic and copies ran while one was open for 0% -> 0% of each run, Pallas kernels for 27% -> 26%
where the time goes in v4:
time: 121 us
  Pallas kernels  33.3 us (28%)
  waiting for transfers between devices  32.9 us (27%)
  starting transfers between devices  29.4 us (24%)
  blocking collectives  24.6 us (20%)
    all_to_all x1, blocking collectives, body(): lax.all_to_all(rows.reshape(devices, -1, rows.shape[-1]), 'dev', split_ax...  24.6 us
    pallas_call x6, Pallas kernels, run_experts(): pl.pallas_call(functools.partial(expert_kernel, places=places), out_shape...  21.6 us
    ppermute x14, waiting for transfers between devices, body(): send_ahead = lambda x: lax.ppermute(x, 'dev', forward)  19.8 us
    ppermute x14, starting transfers between devices, body(): send_behind = lambda x: lax.ppermute(x, 'dev', backward)  15.7 us
    ppermute x14, starting transfers between devices, body(): send_ahead = lambda x: lax.ppermute(x, 'dev', forward)  13.1 us
    ppermute x14, waiting for transfers between devices, body(): send_behind = lambda x: lax.ppermute(x, 'dev', backward)  12 us
    pallas_call x1, Pallas kernels, attend(): pl.pallas_call(functools.partial(attend_kernel, devices=devices), out_sha...  6.37 us
    pallas_call x1, Pallas kernels, load(): pl.pallas_call(load_kernel, out_shape=[jax.ShapeDtypeStruct(x.shape, x.dt...  2.79 us
  transfers between devices with their start and end apart: 31, of which 19 were waited for; matrix products, arithmetic and copies ran while one was open for 0% of the time, Pallas kernels for 26%

profile of v4, /device:TPU:0, one launch (start us, length us, event | category | flops | bytes accessed | tf_op | source)
XLA Modules:
  0.0 120.7 jit_solution(16696353017774015295)
XLA Ops:
  0.5 6.4 %attend.1 = bf16[16,2,8,1152]{3,2,1,0:T(8,128)(2,1)S(1)} custom-call(bf16[2,1,128,1024]{3,2,1,0:T(8,128)(2,1)} %q_ref, bf16[2,1,2,1664,128]{4,3,2,1,0:T(8,128)(2,1)} %kv_ref.1, s32[2,8,64]{2,1,0:T(8,128)} %bitcast.15, s32[2,8,64]{2,1,0:T(8,128)} %bitcast.16), custom_call_target="tpu_custom_call" | custom-call | flops 1744830464 | bytes 2752512 | tf_op jit(solution)/shard_map/attend/pallas_call | solution.py:101
  6.9 24.6 %all_to_all.5.refs_0_ = bf16[16,16,1152]{2,1,0:T(8,128)(2,1)S(1)} all-to-all(bf16[16,16,1152]{2,1,0:T(8,128)(2,1)S(1)} %bitcast.12), channel_id=1, replica_groups=mesh['groups'=2,'dev'=16] {'dev'}, dimensions={0} | all-to-all | bytes 1179648 | tf_op jit(solution)/shard_map/all_to_all | solution.py:404
  32.6 1.4 %collective-permute-start.3 = (bf16[64,2048]{1,0:T(8,128)(2,1)S(1)}, bf16[64,2048]{1,0:T(8,128)(2,1)S(1)}, u32[]{:S(2)}, u32[]{:S(2)}) collective-permute-start(bf16[64,2048]{1,0:T(8,128)(2,1)S(1)} %get-tuple-element.80.refs_0_), channel_id=1, source_target_pairs={{4,0},{5,1},{8,4},{9,5},{12,8},{13,9},{14,12},{15,13},{10,14},{11,... | collective-permute-start | bytes 786440 | tf_op jit(solution)/shard_map/ppermute | solution.py:398
  34.6 1.4 %collective-permute-start.4 = (bf16[64,2048]{1,0:T(8,128)(2,1)S(1)}, bf16[64,2048]{1,0:T(8,128)(2,1)S(1)}, u32[]{:S(2)}, u32[]{:S(2)}) collective-permute-start(bf16[64,2048]{1,0:T(8,128)(2,1)S(1)} %get-tuple-element.80.refs_0_), channel_id=1, source_target_pairs={{0,4},{1,5},{4,8},{5,9},{8,12},{9,13},{12,14},{13,15},{14,10},{15,... | collective-permute-start | bytes 786440 | tf_op jit(solution)/shard_map/ppermute | solution.py:397
  36.1 2.8 %load.1 = (f32[16,128]{1,0:T(8,128)S(1)}, bf16[1,2048,1536]{2,1,0:T(8,128)(2,1)S(1)}) custom-call(f32[16,128]{1,0:T(8,128)S(1)} %get-tuple-element.75.token_ref, bf16[1,2048,1536]{2,1,0:T(8,128)(2,1)} %get-tuple-element.76.refs_0_), custom_call_target="tpu_custom_call" | custom-call | flops 1 | bytes 1 | tf_op jit(solution)/shard_map/load/pallas_call | solution.py:279
  38.9 2.3 %collective-permute-done.2.refs_0_ = bf16[64,2048]{1,0:T(8,128)(2,1)S(1)} collective-permute-done((bf16[64,2048]{1,0:T(8,128)(2,1)S(1)}, bf16[64,2048]{1,0:T(8,128)(2,1)S(1)}, u32[]{:S(2)}, u32[]{:S(2)}) %collective-permute-start.2) | collective-permute-done | bytes 262176 | tf_op jit(solution)/shard_map/ppermute | solution.py:397
  41.8 1.4 %collective-permute-start.8 = (bf16[64,2048]{1,0:T(8,128)(2,1)S(1)}, bf16[64,2048]{1,0:T(8,128)(2,1)S(1)}, u32[]{:S(2)}, u32[]{:S(2)}) collective-permute-start(bf16[64,2048]{1,0:T(8,128)(2,1)S(1)} %get-tuple-element.85.refs_0_), channel_id=1, source_target_pairs={{4,0},{5,1},{8,4},{9,5},{12,8},{13,9},{14,12},{15,13},{10,14},{11,... | collective-permute-start | bytes 786440 | tf_op jit(solution)/shard_map/ppermute | solution.py:398
  43.9 3.6 %collective-permute-done.5.refs_1_ = bf16[64,2048]{1,0:T(8,128)(2,1)S(1)} collective-permute-done((bf16[64,2048]{1,0:T(8,128)(2,1)S(1)}, bf16[64,2048]{1,0:T(8,128)(2,1)S(1)}, u32[]{:S(2)}, u32[]{:S(2)}) %collective-permute-start.5) | collective-permute-done | bytes 262176 | tf_op jit(solution)/shard_map/ppermute | solution.py:398
  47.5 1.4 %collective-permute-start.10 = (bf16[64,2048]{1,0:T(8,128)(2,1)S(1)}, bf16[64,2048]{1,0:T(8,128)(2,1)S(1)}, u32[]{:S(2)}, u32[]{:S(2)}) collective-permute-start(bf16[64,2048]{1,0:T(8,128)(2,1)S(1)} %get-tuple-element.86.refs_1_), channel_id=1, source_target_pairs={{4,0},{5,1},{8,4},{9,5},{12,8},{13,9},{14,12},{15,13},{10,14},{11,... | collective-permute-start | bytes 786440 | tf_op jit(solution)/shard_map/ppermute | solution.py:398
  50.9 2.8 %experts.6 = (bf16[128,2048]{1,0:T(8,128)(2,1)S(1)}, f32[16,128]{1,0:T(8,128)S(1)}) custom-call(s32[1]{0:T(128)} %bitcast.me_ref, f32[16,128]{1,0:T(8,128)S(1)} %get-tuple-element.82.token_ref, f32[16,128]{1,0:T(8,128)S(1)} %add_bitcast_fusion.share_a, f32[16,128]{1,0:T(8,128)S(1)} %collective-permute-done.6.share_b, bf16[1,2048,1536]{2,1,0:T(8,128)(2,1)S(1)} %bitcast.10, ...), custom_call_target="tpu_custom_call" | custom-call | flops 1 | bytes 1 | tf_op jit(solution)/shard_map/experts/pallas_call | solution.py:243
  53.7 1.4 %collective-permute-start.12 = (bf16[64,2048]{1,0:T(8,128)(2,1)S(1)}, bf16[64,2048]{1,0:T(8,128)(2,1)S(1)}, u32[]{:S(2)}, u32[]{:S(2)}) collective-permute-start(bf16[64,2048]{1,0:T(8,128)(2,1)S(1)} %get-tuple-element.93.refs_0_), channel_id=1, source_target_pairs={{4,0},{5,1},{8,4},{9,5},{12,8},{13,9},{14,12},{15,13},{10,14},{11,... | collective-permute-start | bytes 786440 | tf_op jit(solution)/shard_map/ppermute | solution.py:398
  55.8 2.8 %experts.7 = (bf16[128,2048]{1,0:T(8,128)(2,1)S(1)}, f32[16,128]{1,0:T(8,128)S(1)}) custom-call(s32[1]{0:T(128)} %bitcast.me_ref, f32[16,128]{1,0:T(8,128)S(1)} %get-tuple-element.89.token_ref, f32[16,128]{1,0:T(8,128)S(1)} %add_bitcast_fusion.share_a, f32[16,128]{1,0:T(8,128)S(1)} %collective-permute-done.6.share_b, bf16[1,2048,1536]{2,1,0:T(8,128)(2,1)S(1)} %bitcast.10, ...), custom_call_target="tpu_custom_call" | custom-call | flops 1 | bytes 1 | tf_op jit(solution)/shard_map/experts/pallas_call | solution.py:243
  58.7 1.4 %collective-permute-start.14 = (bf16[64,2048]{1,0:T(8,128)(2,1)S(1)}, bf16[64,2048]{1,0:T(8,128)(2,1)S(1)}, u32[]{:S(2)}, u32[]{:S(2)}) collective-permute-start(bf16[64,2048]{1,0:T(8,128)(2,1)S(1)} %get-tuple-element.94.refs_1_), channel_id=1, source_target_pairs={{4,0},{5,1},{8,4},{9,5},{12,8},{13,9},{14,12},{15,13},{10,14},{11,... | collective-permute-start | bytes 786440 | tf_op jit(solution)/shard_map/ppermute | solution.py:398
  60.7 5.2 %experts.8 = (bf16[256,2048]{1,0:T(8,128)(2,1)S(1)}, f32[16,128]{1,0:T(8,128)S(1)}) custom-call(s32[1]{0:T(128)} %bitcast.me_ref, f32[16,128]{1,0:T(8,128)S(1)} %get-tuple-element.92.token_ref, f32[16,128]{1,0:T(8,128)S(1)} %add_bitcast_fusion.share_a, f32[16,128]{1,0:T(8,128)S(1)} %collective-permute-done.6.share_b, bf16[1,2048,1536]{2,1,0:T(8,128)(2,1)S(1)} %bitcast.10, ...), custom_call_target="tpu_custom_call" | custom-call | flops 1 | bytes 1 | tf_op jit(solution)/shard_map/experts/pallas_call | solution.py:243
  65.9 2.8 %collective-permute-done.14.refs_1_ = bf16[64,2048]{1,0:T(8,128)(2,1)S(1)} collective-permute-done((bf16[64,2048]{1,0:T(8,128)(2,1)S(1)}, bf16[64,2048]{1,0:T(8,128)(2,1)S(1)}, u32[]{:S(2)}, u32[]{:S(2)}) %collective-permute-start.14) | collective-permute-done | bytes 262176 | tf_op jit(solution)/shard_map/ppermute | solution.py:398
  70.9 5.2 %experts.9 = (bf16[256,2048]{1,0:T(8,128)(2,1)S(1)}, f32[16,128]{1,0:T(8,128)S(1)}) custom-call(s32[1]{0:T(128)} %bitcast.me_ref, f32[16,128]{1,0:T(8,128)S(1)} %get-tuple-element.99.token_ref, f32[16,128]{1,0:T(8,128)S(1)} %add_bitcast_fusion.share_a, f32[16,128]{1,0:T(8,128)S(1)} %collective-permute-done.6.share_b, bf16[1,2048,1536]{2,1,0:T(8,128)(2,1)S(1)} %bitcast.10, ...), custom_call_target="tpu_custom_call" | custom-call | flops 1 | bytes 1 | tf_op jit(solution)/shard_map/experts/pallas_call | solution.py:243
  76.8 1.4 %collective-permute-start.18 = (bf16[64,2048]{1,0:T(8,128)(2,1)S(1)}, bf16[64,2048]{1,0:T(8,128)(2,1)S(1)}, u32[]{:S(2)}, u32[]{:S(2)}) collective-permute-start(bf16[64,2048]{1,0:T(8,128)(2,1)S(1)} %get-tuple-element.115), channel_id=1, source_target_pairs={{4,0},{5,1},{8,4},{9,5},{12,8},{13,9},{14,12},{15,13},{10,14},{11,... | collective-permute-start | bytes 786440 | tf_op jit(solution)/shard_map/ppermute | solution.py:398
  78.2 2.8 %experts.10 = (bf16[128,2048]{1,0:T(8,128)(2,1)S(1)}, f32[16,128]{1,0:T(8,128)S(1)}) custom-call(s32[1]{0:T(128)} %bitcast.me_ref, f32[16,128]{1,0:T(8,128)S(1)} %get-tuple-element.107.token_ref, f32[16,128]{1,0:T(8,128)S(1)} %add_bitcast_fusion.share_a, f32[16,128]{1,0:T(8,128)S(1)} %collective-permute-done.6.share_b, bf16[1,2048,1536]{2,1,0:T(8,128)(2,1)S(1)} %bitcast.10, ...), custom_call_target="tpu_custom_call" | custom-call | flops 1 | bytes 1 | tf_op jit(solution)/shard_map/experts/pallas_call | solution.py:243
  86.8 3.6 %collective-permute-done.19.refs_0_ = bf16[64,2048]{1,0:T(8,128)(2,1)S(1)} collective-permute-done((bf16[64,2048]{1,0:T(8,128)(2,1)S(1)}, bf16[64,2048]{1,0:T(8,128)(2,1)S(1)}, u32[]{:S(2)}, u32[]{:S(2)}) %collective-permute-start.19) | collective-permute-done | bytes 262176 | tf_op jit(solution)/shard_map/ppermute | solution.py:397
  93.2 2.7 %collective-permute-done.21.refs_0_ = bf16[64,2048]{1,0:T(8,128)(2,1)S(1)} collective-permute-done((bf16[64,2048]{1,0:T(8,128)(2,1)S(1)}, bf16[64,2048]{1,0:T(8,128)(2,1)S(1)}, u32[]{:S(2)}, u32[]{:S(2)}) %collective-permute-start.21) | collective-permute-done | bytes 262176 | tf_op jit(solution)/shard_map/ppermute | solution.py:397
  98.8 2.7 %collective-permute-done.23.refs_0_ = bf16[64,2048]{1,0:T(8,128)(2,1)S(1)} collective-permute-done((bf16[64,2048]{1,0:T(8,128)(2,1)S(1)}, bf16[64,2048]{1,0:T(8,128)(2,1)S(1)}, u32[]{:S(2)}, u32[]{:S(2)}) %collective-permute-start.23) | collective-permute-done | bytes 262176 | tf_op jit(solution)/shard_map/ppermute | solution.py:397
  104.5 2.8 %experts.11 = (bf16[128,2048]{1,0:T(8,128)(2,1)S(1)}, f32[16,128]{1,0:T(8,128)S(1)}) custom-call(s32[1]{0:T(128)} %bitcast.me_ref, f32[16,128]{1,0:T(8,128)S(1)} %get-tuple-element.127.token_ref, f32[16,128]{1,0:T(8,128)S(1)} %add_bitcast_fusion.share_a, f32[16,128]{1,0:T(8,128)S(1)} %collective-permute-done.6.share_b, bf16[1,2048,1536]{2,1,0:T(8,128)(2,1)S(1)} %bitcast.10, ...), custom_call_target="tpu_custom_call" | custom-call | flops 1 | bytes 1 | tf_op jit(solution)/shard_map/experts/pallas_call | solution.py:243
  107.9 3.1 %collective-permute-done.27.refs_0_ = bf16[64,2048]{1,0:T(8,128)(2,1)S(1)} collective-permute-done((bf16[64,2048]{1,0:T(8,128)(2,1)S(1)}, bf16[64,2048]{1,0:T(8,128)(2,1)S(1)}, u32[]{:S(2)}, u32[]{:S(2)}) %collective-permute-start.27) | collective-permute-done | bytes 262176 | tf_op jit(solution)/shard_map/ppermute | solution.py:397
  114.2 4.3 %collective-permute-done.29.refs_2_ = bf16[64,2048]{1,0:T(8,128)(2,1)S(1)} collective-permute-done((bf16[64,2048]{1,0:T(8,128)(2,1)S(1)}, bf16[64,2048]{1,0:T(8,128)(2,1)S(1)}, u32[]{:S(2)}, u32[]{:S(2)}) %collective-permute-start.29) | collective-permute-done | bytes 262176 | tf_op jit(solution)/shard_map/ppermute | solution.py:397
  (79 shorter events, 30.1 us)
Async XLA Ops:
  0.0 31.5 %collective-permute-start = (bf16[1,2048,1536]{2,1,0:T(8,128)(2,1)}, bf16[1,2048,1536]{2,1,0:T(8,128)(2,1)}, u32[]{:S(2)}, u32[]{:S(2)}) collective-permute-start(bf16[1,2048,1536]{2,1,0:T(8,128)(2,1)} %gate_up_a.11), channel_id=1, source_target_pairs={{0,1},{1,0},{2,3},{3,2},{4,5},{5,4},{6,7},{7,6},{8,9},{9,8},{10,11... | collective-permute-start | bytes 18874376 | tf_op jit(solution)/shard_map/ppermute | solution.py:399
  0.5 31.1 %collective-permute-start.1 = (bf16[1,768,2048]{2,1,0:T(8,128)(2,1)}, bf16[1,768,2048]{2,1,0:T(8,128)(2,1)S(1)}, u32[]{:S(2)}, u32[]{:S(2)}) collective-permute-start(bf16[1,768,2048]{2,1,0:T(8,128)(2,1)} %down_a.11), channel_id=1, source_target_pairs={{0,1},{1,0},{2,3},{3,2},{4,5},{5,4},{6,7},{7,6},{8,9},{9,8},{10,11... | collective-permute-start | bytes 9437192 | tf_op jit(solution)/shard_map/ppermute | solution.py:399
  31.9 9.2 %collective-permute-start.2 = (bf16[64,2048]{1,0:T(8,128)(2,1)S(1)}, bf16[64,2048]{1,0:T(8,128)(2,1)S(1)}, u32[]{:S(2)}, u32[]{:S(2)}) collective-permute-start(bf16[64,2048]{1,0:T(8,128)(2,1)S(1)} %get-tuple-element.79.refs_1_), channel_id=1, source_target_pairs={{0,4},{1,5},{4,8},{5,9},{8,12},{9,13},{12,14},{13,15},{14,10},{15,... | collective-permute-start | bytes 786440 | tf_op jit(solution)/shard_map/ppermute | solution.py:397
  32.6 9.2 %collective-permute-start.3 = (bf16[64,2048]{1,0:T(8,128)(2,1)S(1)}, bf16[64,2048]{1,0:T(8,128)(2,1)S(1)}, u32[]{:S(2)}, u32[]{:S(2)}) collective-permute-start(bf16[64,2048]{1,0:T(8,128)(2,1)S(1)} %get-tuple-element.80.refs_0_), channel_id=1, source_target_pairs={{4,0},{5,1},{8,4},{9,5},{12,8},{13,9},{14,12},{15,13},{10,14},{11,... | collective-permute-start | bytes 786440 | tf_op jit(solution)/shard_map/ppermute | solution.py:398
  34.0 13.4 %collective-permute-start.5 = (bf16[64,2048]{1,0:T(8,128)(2,1)S(1)}, bf16[64,2048]{1,0:T(8,128)(2,1)S(1)}, u32[]{:S(2)}, u32[]{:S(2)}) collective-permute-start(bf16[64,2048]{1,0:T(8,128)(2,1)S(1)} %get-tuple-element.79.refs_1_), channel_id=1, source_target_pairs={{4,0},{5,1},{8,4},{9,5},{12,8},{13,9},{14,12},{15,13},{10,14},{11,... | collective-permute-start | bytes 786440 | tf_op jit(solution)/shard_map/ppermute | solution.py:398
  34.6 12.8 %collective-permute-start.4 = (bf16[64,2048]{1,0:T(8,128)(2,1)S(1)}, bf16[64,2048]{1,0:T(8,128)(2,1)S(1)}, u32[]{:S(2)}, u32[]{:S(2)}) collective-permute-start(bf16[64,2048]{1,0:T(8,128)(2,1)S(1)} %get-tuple-element.80.refs_0_), channel_id=1, source_target_pairs={{0,4},{1,5},{4,8},{5,9},{8,12},{9,13},{12,14},{13,15},{14,10},{15,... | collective-permute-start | bytes 786440 | tf_op jit(solution)/shard_map/ppermute | solution.py:397
  41.8 11.8 %collective-permute-start.8 = (bf16[64,2048]{1,0:T(8,128)(2,1)S(1)}, bf16[64,2048]{1,0:T(8,128)(2,1)S(1)}, u32[]{:S(2)}, u32[]{:S(2)}) collective-permute-start(bf16[64,2048]{1,0:T(8,128)(2,1)S(1)} %get-tuple-element.85.refs_0_), channel_id=1, source_target_pairs={{4,0},{5,1},{8,4},{9,5},{12,8},{13,9},{14,12},{15,13},{10,14},{11,... | collective-permute-start | bytes 786440 | tf_op jit(solution)/shard_map/ppermute | solution.py:398
  43.2 10.5 %collective-permute-start.7 = (bf16[64,2048]{1,0:T(8,128)(2,1)S(1)}, bf16[64,2048]{1,0:T(8,128)(2,1)S(1)}, u32[]{:S(2)}, u32[]{:S(2)}) collective-permute-start(bf16[64,2048]{1,0:T(8,128)(2,1)S(1)} %get-tuple-element.88.refs_1_), channel_id=1, source_target_pairs={{0,4},{1,5},{4,8},{5,9},{8,12},{9,13},{12,14},{13,15},{14,10},{15,... | collective-permute-start | bytes 786440 | tf_op jit(solution)/shard_map/ppermute | solution.py:397
  47.5 11.2 %collective-permute-start.10 = (bf16[64,2048]{1,0:T(8,128)(2,1)S(1)}, bf16[64,2048]{1,0:T(8,128)(2,1)S(1)}, u32[]{:S(2)}, u32[]{:S(2)}) collective-permute-start(bf16[64,2048]{1,0:T(8,128)(2,1)S(1)} %get-tuple-element.86.refs_1_), channel_id=1, source_target_pairs={{4,0},{5,1},{8,4},{9,5},{12,8},{13,9},{14,12},{15,13},{10,14},{11,... | collective-permute-start | bytes 786440 | tf_op jit(solution)/shard_map/ppermute | solution.py:398
  48.8 9.8 %collective-permute-start.9 = (bf16[64,2048]{1,0:T(8,128)(2,1)S(1)}, bf16[64,2048]{1,0:T(8,128)(2,1)S(1)}, u32[]{:S(2)}, u32[]{:S(2)}) collective-permute-start(bf16[64,2048]{1,0:T(8,128)(2,1)S(1)} %get-tuple-element.90.refs_0_), channel_id=1, source_target_pairs={{0,4},{1,5},{4,8},{5,9},{8,12},{9,13},{12,14},{13,15},{14,10},{15,... | collective-permute-start | bytes 786440 | tf_op jit(solution)/shard_map/ppermute | solution.py:397
  53.7 12.2 %collective-permute-start.12 = (bf16[64,2048]{1,0:T(8,128)(2,1)S(1)}, bf16[64,2048]{1,0:T(8,128)(2,1)S(1)}, u32[]{:S(2)}, u32[]{:S(2)}) collective-permute-start(bf16[64,2048]{1,0:T(8,128)(2,1)S(1)} %get-tuple-element.93.refs_0_), channel_id=1, source_target_pairs={{4,0},{5,1},{8,4},{9,5},{12,8},{13,9},{14,12},{15,13},{10,14},{11,... | collective-permute-start | bytes 786440 | tf_op jit(solution)/shard_map/ppermute | solution.py:398
  55.1 10.8 %collective-permute-start.11 = (bf16[64,2048]{1,0:T(8,128)(2,1)S(1)}, bf16[64,2048]{1,0:T(8,128)(2,1)S(1)}, u32[]{:S(2)}, u32[]{:S(2)}) collective-permute-start(bf16[64,2048]{1,0:T(8,128)(2,1)S(1)} %get-tuple-element.96.refs_3_), channel_id=1, source_target_pairs={{0,4},{1,5},{4,8},{5,9},{8,12},{9,13},{12,14},{13,15},{14,10},{15,... | collective-permute-start | bytes 786440 | tf_op jit(solution)/shard_map/ppermute | solution.py:397
  58.7 10.1 %collective-permute-start.14 = (bf16[64,2048]{1,0:T(8,128)(2,1)S(1)}, bf16[64,2048]{1,0:T(8,128)(2,1)S(1)}, u32[]{:S(2)}, u32[]{:S(2)}) collective-permute-start(bf16[64,2048]{1,0:T(8,128)(2,1)S(1)} %get-tuple-element.94.refs_1_), channel_id=1, source_target_pairs={{4,0},{5,1},{8,4},{9,5},{12,8},{13,9},{14,12},{15,13},{10,14},{11,... | collective-permute-start | bytes 786440 | tf_op jit(solution)/shard_map/ppermute | solution.py:398
  60.1 8.8 %collective-permute-start.13 = (bf16[64,2048]{1,0:T(8,128)(2,1)S(1)}, bf16[64,2048]{1,0:T(8,128)(2,1)S(1)}, u32[]{:S(2)}, u32[]{:S(2)}) collective-permute-start(bf16[64,2048]{1,0:T(8,128)(2,1)S(1)} %get-tuple-element.95.refs_2_), channel_id=1, source_target_pairs={{0,4},{1,5},{4,8},{5,9},{8,12},{9,13},{12,14},{13,15},{14,10},{15,... | collective-permute-start | bytes 786440 | tf_op jit(solution)/shard_map/ppermute | solution.py:397
  68.8 9.3 %collective-permute-start.16 = (bf16[64,2048]{1,0:T(8,128)(2,1)S(1)}, bf16[64,2048]{1,0:T(8,128)(2,1)S(1)}, u32[]{:S(2)}, u32[]{:S(2)}) collective-permute-start(bf16[64,2048]{1,0:T(8,128)(2,1)S(1)} %get-tuple-element.101.refs_1_), channel_id=1, source_target_pairs={{4,0},{5,1},{8,4},{9,5},{12,8},{13,9},{14,12},{15,13},{10,14},{11,... | collective-permute-start | bytes 786440 | tf_op jit(solution)/shard_map/ppermute | solution.py:398
  81.1 9.3 %collective-permute-start.19 = (bf16[64,2048]{1,0:T(8,128)(2,1)S(1)}, bf16[64,2048]{1,0:T(8,128)(2,1)S(1)}, u32[]{:S(2)}, u32[]{:S(2)}) collective-permute-start(bf16[64,2048]{1,0:T(8,128)(2,1)S(1)} %get-tuple-element.117), channel_id=1, source_target_pairs={{0,4},{1,5},{4,8},{5,9},{8,12},{9,13},{12,14},{13,15},{14,10},{15,... | collective-permute-start | bytes 786440 | tf_op jit(solution)/shard_map/ppermute | solution.py:397
  81.8 9.2 %collective-permute-start.20 = (bf16[64,2048]{1,0:T(8,128)(2,1)S(1)}, bf16[64,2048]{1,0:T(8,128)(2,1)S(1)}, u32[]{:S(2)}, u32[]{:S(2)}) collective-permute-start(bf16[64,2048]{1,0:T(8,128)(2,1)S(1)} %get-tuple-element.118), channel_id=1, source_target_pairs={{4,0},{5,1},{8,4},{9,5},{12,8},{13,9},{14,12},{15,13},{10,14},{11,... | collective-permute-start | bytes 786440 | tf_op jit(solution)/shard_map/ppermute | solution.py:398
  84.7 11.2 %collective-permute-start.21 = (bf16[64,2048]{1,0:T(8,128)(2,1)S(1)}, bf16[64,2048]{1,0:T(8,128)(2,1)S(1)}, u32[]{:S(2)}, u32[]{:S(2)}) collective-permute-start(bf16[64,2048]{1,0:T(8,128)(2,1)S(1)} %get-tuple-element.122), channel_id=1, source_target_pairs={{0,4},{1,5},{4,8},{5,9},{8,12},{9,13},{12,14},{13,15},{14,10},{15,... | collective-permute-start | bytes 786440 | tf_op jit(solution)/shard_map/ppermute | solution.py:397
  85.9 10.7 %collective-permute-start.22 = (bf16[64,2048]{1,0:T(8,128)(2,1)S(1)}, bf16[64,2048]{1,0:T(8,128)(2,1)S(1)}, u32[]{:S(2)}, u32[]{:S(2)}) collective-permute-start(bf16[64,2048]{1,0:T(8,128)(2,1)S(1)} %get-tuple-element.123), channel_id=1, source_target_pairs={{4,0},{5,1},{8,4},{9,5},{12,8},{13,9},{14,12},{15,13},{10,14},{11,... | collective-permute-start | bytes 786440 | tf_op jit(solution)/shard_map/ppermute | solution.py:398
  91.2 10.4 %collective-permute-start.23 = (bf16[64,2048]{1,0:T(8,128)(2,1)S(1)}, bf16[64,2048]{1,0:T(8,128)(2,1)S(1)}, u32[]{:S(2)}, u32[]{:S(2)}) collective-permute-start(bf16[64,2048]{1,0:T(8,128)(2,1)S(1)} %get-tuple-element.125), channel_id=1, source_target_pairs={{0,4},{1,5},{4,8},{5,9},{8,12},{9,13},{12,14},{13,15},{14,10},{15,... | collective-permute-start | bytes 786440 | tf_op jit(solution)/shard_map/ppermute | solution.py:397
  92.4 9.8 %collective-permute-start.24 = (bf16[64,2048]{1,0:T(8,128)(2,1)S(1)}, bf16[64,2048]{1,0:T(8,128)(2,1)S(1)}, u32[]{:S(2)}, u32[]{:S(2)}) collective-permute-start(bf16[64,2048]{1,0:T(8,128)(2,1)S(1)} %get-tuple-element.126), channel_id=1, source_target_pairs={{4,0},{5,1},{8,4},{9,5},{12,8},{13,9},{14,12},{15,13},{10,14},{11,... | collective-permute-start | bytes 786440 | tf_op jit(solution)/shard_map/ppermute | solution.py:398
  96.8 10.5 %collective-permute-start.25 = (bf16[64,2048]{1,0:T(8,128)(2,1)S(1)}, bf16[64,2048]{1,0:T(8,128)(2,1)S(1)}, u32[]{:S(2)}, u32[]{:S(2)}) collective-permute-start(bf16[64,2048]{1,0:T(8,128)(2,1)S(1)} %get-tuple-element.132), channel_id=1, source_target_pairs={{0,4},{1,5},{4,8},{5,9},{8,12},{9,13},{12,14},{13,15},{14,10},{15,... | collective-permute-start | bytes 786440 | tf_op jit(solution)/shard_map/ppermute | solution.py:397
  98.1 9.8 %collective-permute-start.26 = (bf16[64,2048]{1,0:T(8,128)(2,1)S(1)}, bf16[64,2048]{1,0:T(8,128)(2,1)S(1)}, u32[]{:S(2)}, u32[]{:S(2)}) collective-permute-start(bf16[64,2048]{1,0:T(8,128)(2,1)S(1)} %get-tuple-element.133), channel_id=1, source_target_pairs={{4,0},{5,1},{8,4},{9,5},{12,8},{13,9},{14,12},{15,13},{10,14},{11,... | collective-permute-start | bytes 786440 | tf_op jit(solution)/shard_map/ppermute | solution.py:398
  102.4 8.6 %collective-permute-start.27 = (bf16[64,2048]{1,0:T(8,128)(2,1)S(1)}, bf16[64,2048]{1,0:T(8,128)(2,1)S(1)}, u32[]{:S(2)}, u32[]{:S(2)}) collective-permute-start(bf16[64,2048]{1,0:T(8,128)(2,1)S(1)} %get-tuple-element.135), channel_id=1, source_target_pairs={{0,4},{1,5},{4,8},{5,9},{8,12},{9,13},{12,14},{13,15},{14,10},{15,... | collective-permute-start | bytes 786440 | tf_op jit(solution)/shard_map/ppermute | solution.py:397
  (12 other events, 152.9 us)

commit v5 on v4

--- a/solution.py
+++ b/solution.py
@@ -177,9 +177,71 @@
     return 2 * chip + core
 
 
-def expert_kernel(me_ref, token_ref, share_a, share_b, gate_up_a, gate_up_b, down_a, down_b, *refs, places):
+def pre_activations(x_ref, gate_up_ref, cols, sides, blocks):
+    if sides is None:
+        return jnp.dot(x_ref[...], gate_up_ref[0, :, cols], preferred_element_type=F32)
+    rows, half = x_ref.shape
+    rows = rows // blocks
+    parts = []
+    for block, side in enumerate(sides):
+        parts.append(
+            jnp.dot(
+                x_ref[block * rows : (block + 1) * rows],
+                gate_up_ref[0, side * half : (side + 1) * half, cols],
+                preferred_element_type=F32,
+            )
+        )
+    return jnp.concatenate(parts, axis=0)
+
+
+def gather_halves(x_ref, half_refs):
+    tokens, width = half_refs[0].shape
+    for block, ref in enumerate(half_refs):
+        for batch in range(2):
+            row = (2 * block + batch) * tokens
+            came = slice(batch * width // 2, (batch + 1) * width // 2)
+            x_ref[row : row + tokens] = ref[:, came]
+
+
+def begin_kernel(token_ref, gate_up_a, gate_up_b, *refs, sides):
+    *half_refs, pre_a, pre_b, next_ref, x_ref = refs
+    next_ref[...] = token_ref[...]
+    gather_halves(x_ref, half_refs)
+    for gate_up_ref, pre_ref in ((gate_up_a, pre_a), (gate_up_b, pre_b)):
+        width = pre_ref.shape[1]
+        part = min(256, width)
+        for start in range(0, width, part):
+            cols = slice(start, start + part)
+            pre_ref[:, cols] = pre_activations(x_ref, gate_up_ref, cols, sides, len(half_refs))
+
+
+def begin_experts(token, weights, halves, sides):
+    tokens, width = halves[0].shape
+    rows = 2 * tokens * len(halves)
+    hidden = weights[0].shape[2]
+    whole = pl.BlockSpec(memory_space=pltpu.VMEM)
+    return pl.pallas_call(
+        functools.partial(begin_kernel, sides=sides),
+        out_shape=[jax.ShapeDtypeStruct((rows, hidden), F32)] * 2
+        + [jax.ShapeDtypeStruct(token.shape, token.dtype)],
+        in_specs=[whole] * (3 + len(halves)),
+        out_specs=[whole] * 3,
+        scratch_shapes=[pltpu.VMEM((rows, width // 2), BF16)],
+        compiler_params=pltpu.CompilerParams(vmem_limit_bytes=8 << 20),
+        cost_estimate=pl.CostEstimate(flops=1, bytes_accessed=1, transcendentals=0),
+        name="begin",
+    )(token, *weights[:2], *halves)
+
+
+def expert_kernel(
+    me_ref, token_ref, share_a, share_b, gate_up_a, gate_up_b, down_a, down_b, *refs, places, sides
+):
     *held_refs, out_ref, next_ref, x_all, hidden_a, hidden_b = refs
     next_ref[...] = token_ref[...]
+    begun = (None, None)
+    if sides is not None:
+        *held_refs, pre_a, pre_b = held_refs
+        begun = (pre_a, pre_b)
     tokens, model_width = held_refs[0].shape
     half = model_width // 2
     blocks = len(places)
@@ -189,18 +251,21 @@
     chunk = min(512, half)
 
     row_of = lambda block, batch: (block * 2 + batch) * tokens
-    for block in range(blocks):
-        for side in range(2):
-            cols = slice(side * half, (side + 1) * half)
-            for batch in range(2):
-                row = row_of(block, batch)
-                came = slice(batch * half, (batch + 1) * half)
-                x_all[row : row + tokens, cols] = held_refs[2 * block + side][:, came]
+    if sides is not None:
+        gather_halves(x_all, held_refs)
+    else:
+        for block in range(blocks):
+            for side in range(2):
+                cols = slice(side * half, (side + 1) * half)
+                for batch in range(2):
+                    row = row_of(block, batch)
+                    came = slice(batch * half, (batch + 1) * half)
+                    x_all[row : row + tokens, cols] = held_refs[2 * block + side][:, came]
     token = lax.broadcasted_iota(jnp.int32, (tokens, lanes), 0)
     lane = lax.broadcasted_iota(jnp.int32, (tokens, lanes), 1)
-    for share_ref, gate_up_ref, hidden_ref in (
-        (share_a, gate_up_a, hidden_a),
-        (share_b, gate_up_b, hidden_b),
+    for share_ref, gate_up_ref, hidden_ref, pre_ref in (
+        (share_a, gate_up_a, hidden_a, begun[0]),
+        (share_b, gate_up_b, hidden_b, begun[1]),
     ):
         shares = []
         for place in places:
@@ -211,14 +276,12 @@
                 shares.append(jnp.sum(spread, axis=-1, keepdims=True))
         share = jnp.concatenate(shares, axis=0)
         for start in range(0, hidden_width, part):
-            gate = jnp.dot(
-                x_all[...], gate_up_ref[0, :, start : start + part], preferred_element_type=F32
-            )
-            up = jnp.dot(
-                x_all[...],
-                gate_up_ref[0, :, hidden_width + start : hidden_width + start + part],
-                preferred_element_type=F32,
-            )
+            pair = []
+            for first in (start, hidden_width + start):
+                cols = slice(first, first + part)
+                pre = pre_activations(x_all, gate_up_ref, cols, sides, blocks)
+                pair.append(pre if pre_ref is None else pre + pre_ref[:, cols])
+            gate, up = pair
             act = gate / (1.0 + jnp.exp(-gate)) * up
             hidden_ref[:, start : start + part] = (act * share).astype(BF16)
     for start in range(0, model_width, chunk):
@@ -235,28 +298,28 @@
                 out_ref[rows, goes] = weighted[row : row + tokens]
 
 
-def run_experts(me, token, shares, weights, held, places):
+def run_experts(me, token, shares, weights, held, places, sides=None, begun=()):
     tokens, model_width = held[0].shape
-    rows = tokens * len(held)
+    rows = 2 * tokens * len(places)
     hidden_width = weights[2].shape[1]
     whole = pl.BlockSpec(memory_space=pltpu.VMEM)
     return pl.pallas_call(
-        functools.partial(expert_kernel, places=places),
+        functools.partial(expert_kernel, places=places, sides=sides),
         out_shape=[
             jax.ShapeDtypeStruct((rows, model_width), BF16),
             jax.ShapeDtypeStruct(token.shape, token.dtype),
         ],
-        in_specs=[pl.BlockSpec(memory_space=pltpu.SMEM)] + [whole] * (7 + len(held)),
+        in_specs=[pl.BlockSpec(memory_space=pltpu.SMEM)] + [whole] * (7 + len(held) + len(begun)),
         out_specs=[whole] * 2,
         scratch_shapes=[
-            pltpu.VMEM((rows, model_width), BF16),
+            pltpu.VMEM((rows, model_width if sides is None else model_width // 2), BF16),
             pltpu.VMEM((rows, hidden_width), BF16),
             pltpu.VMEM((rows, hidden_width), BF16),
         ],
         compiler_params=pltpu.CompilerParams(vmem_limit_bytes=10 << 20),
         cost_estimate=pl.CostEstimate(flops=1, bytes_accessed=1, transcendentals=0),
         name="experts",
-    )(me, token, *shares, *weights, *held)
+    )(me, token, *shares, *weights, *held, *begun)
 
 
 def load_kernel(token_ref, *refs):
@@ -347,31 +410,38 @@
     )(token, *terms, *moving)
 
 
-def finish_kernel(terms_ref, *refs):
-    *sum_refs, out_ref = refs
-    batches, tokens, model_width = out_ref.shape
+def finish_kernel(token_ref, terms_ref, *refs):
+    *sum_refs, out_ref, rows_ref, sems = refs
+    batches, tokens, model_width = rows_ref.shape
     stream_refs, sum_refs = sum_refs[:batches], sum_refs[batches:]
     half = model_width // batches
-    for side in range(2):
-        total = terms_ref[side * tokens : (side + 1) * tokens].astype(F32)
-        for sum_ref in sum_refs[2 * side : 2 * side + 2]:
-            total = total + sum_ref[...].astype(F32)
-        cols = slice(side * half, (side + 1) * half)
-        for batch, stream_ref in enumerate(stream_refs):
-            came = total[:, batch * half : (batch + 1) * half]
-            out_ref[batch, :, cols] = (stream_ref[:, cols] + came).astype(BF16)
-
-
-def finish(terms, streams, sums):
-    whole = pl.BlockSpec(memory_space=pltpu.VMEM)
+    copies = []
+    for batch, stream_ref in enumerate(stream_refs):
+        came = slice(batch * half, (batch + 1) * half)
+        for side in range(2):
+            cols = slice(side * half, (side + 1) * half)
+            total = terms_ref[side * tokens : (side + 1) * tokens, came].astype(F32)
+            for sum_ref in sum_refs[2 * side : 2 * side + 2]:
+                total = total + sum_ref[:, came].astype(F32)
+            rows_ref[batch, :, cols] = (stream_ref[:, cols] + total).astype(BF16)
+        copies.append(pltpu.make_async_copy(rows_ref.at[batch], out_ref.at[batch], sems.at[batch]))
+        copies[-1].start()
+    for copy in copies:
+        copy.wait()
+
+
+def finish(token, terms, streams, sums):
+    whole = pl.BlockSpec(memory_space=pltpu.VMEM)
+    shape = (len(streams), *streams[0].shape)
     return pl.pallas_call(
         finish_kernel,
-        out_shape=jax.ShapeDtypeStruct((len(streams), *streams[0].shape), BF16),
-        in_specs=[whole] * (1 + len(streams) + len(sums)),
-        out_specs=whole,
+        out_shape=jax.ShapeDtypeStruct(shape, BF16),
+        in_specs=[whole] * (2 + len(streams) + len(sums)),
+        out_specs=pl.BlockSpec(memory_space=pl.ANY),
+        scratch_shapes=[pltpu.VMEM(shape, BF16), pltpu.SemaphoreType.DMA((len(streams),))],
         compiler_params=pltpu.CompilerParams(vmem_limit_bytes=8 << 20),
         name="finish",
-    )(terms, *streams, *sums)
+    )(token, terms, *streams, *sums)
 
 
 class Line:
@@ -440,25 +510,37 @@
         line.token, *chain.moving = merge(line.token, outs, cuts, [] if first else chain.moving)
         chain.send()
 
+    long.send()
     short.send()
-    long.send()
     line.token, gate_up_b = load(line.token, gate_up_b)
     weights = [gate_up, gate_up_b, down_proj, down_b]
     for step in range(1, reach):
+        long.land()
+        from_behind, from_ahead = long.moving
+        long.send()
+        if step == reach - 1:
+            *begun, line.token = begin_experts(
+                line.token, weights, [from_ahead, from_behind], (1, 0)
+            )
+        elif step == 2:
+            experts(chips - 1)
         short.land()
-        came_right, came_left = short.moving
+        held[step] = [short.moving[1], from_ahead]
+        held[chips - step] = [from_behind, short.moving[0]]
         if step < reach - 1:
             short.send()
-        if step == 2:
-            experts(chips - 1)
-        long.land()
-        held[step] = [came_left, long.moving[1]]
-        held[chips - step] = [long.moving[0], came_right]
-        long.send()
-        if step == 1:
+        if step == reach - 1:
+            places = (step, chips - step)
+            out, line.token = run_experts(
+                me, line.token, shares, weights, short.moving[::-1], places, (0, 1), begun
+            )
+            terms.update({place: (out, 2 * k * tokens) for k, place in enumerate(places)})
+        elif step == 1:
             experts(1)
         else:
             experts(step, chips - step)
+    if reach < 4:
+        experts(chips - 1)
     send_back(short, reach - 1, True)
     long.land()
     held[reach] = long.moving
@@ -473,7 +555,9 @@
     send_back(long, 1)
     ahead, behind = long.moving
     short_ahead, short_behind = short.moving
-    return finish(terms[0][0], streams, [ahead, short_behind, behind, short_ahead])
+    return finish(
+        line.token, terms[0][0], streams, [ahead, short_behind, behind, short_ahead]
+    )
 
 
 def solution(mesh):

time: 121 us -> 119 us (0.983)
  waiting for transfers between devices: 32.9 us -> 29.9 us
    ppermute x14, waiting for transfers between devices: 19.8 us -> 18 us  [body(): send_ahead = lambda x: lax.ppermute(x, 'dev', forward)]
    pallas_call x7 -> x8, Pallas kernels: 22.6 us -> 23.3 us  [the longest x6 20.4 us: run_experts(): pl.pallas_call(functools.partial(expert_kernel, places=places, sides=side...]
  transfers between devices with their start and end apart: 31 -> 31, of which waited for: 19 -> 18; matrix products, arithmetic and copies ran while one was open for 0% -> 0% of each run, Pallas kernels for 26% -> 27%
where the time goes in v5:
time: 119 us
  Pallas kernels  33.7 us (28%)
  waiting for transfers between devices  29.9 us (25%)
  starting transfers between devices  29.4 us (25%)
  blocking collectives  24.5 us (21%)
  local copies, waits for them, and re-layouts  1.27 us (1%)
    all_to_all x1, blocking collectives, body(): lax.all_to_all(rows.reshape(devices, -1, rows.shape[-1]), 'dev', split_ax...  24.5 us
    pallas_call x6, Pallas kernels, run_experts(): pl.pallas_call(functools.partial(expert_kernel, places=places, sides=side...  20.4 us
    ppermute x14, waiting for transfers between devices, body(): send_ahead = lambda x: lax.ppermute(x, 'dev', forward)  18 us
    ppermute x14, starting transfers between devices, body(): send_behind = lambda x: lax.ppermute(x, 'dev', backward)  15.9 us
    ppermute x14, starting transfers between devices, body(): send_ahead = lambda x: lax.ppermute(x, 'dev', forward)  12.9 us
    ppermute x14, waiting for transfers between devices, body(): send_behind = lambda x: lax.ppermute(x, 'dev', backward)  11.8 us
    pallas_call x1, Pallas kernels, attend(): pl.pallas_call(functools.partial(attend_kernel, devices=devices), out_sha...  6.37 us
    pallas_call x1, Pallas kernels, load(): pl.pallas_call(load_kernel, out_shape=[jax.ShapeDtypeStruct(x.shape, x.dt...  2.94 us
  transfers between devices with their start and end apart: 31, of which 18 were waited for; matrix products, arithmetic and copies ran while one was open for 0% of the time, Pallas kernels for 27%

profile of v5, /device:TPU:0, one launch (start us, length us, event | category | flops | bytes accessed | tf_op | source)
XLA Modules:
  0.0 119.2 jit_solution(554136494090090655)
XLA Ops:
  0.5 6.4 %attend.1 = bf16[16,2,8,1152]{3,2,1,0:T(8,128)(2,1)S(1)} custom-call(bf16[2,1,128,1024]{3,2,1,0:T(8,128)(2,1)} %q_ref, bf16[2,1,2,1664,128]{4,3,2,1,0:T(8,128)(2,1)} %kv_ref.1, s32[2,8,64]{2,1,0:T(8,128)} %bitcast.15, s32[2,8,64]{2,1,0:T(8,128)} %bitcast.16), custom_call_target="tpu_custom_call" | custom-call | flops 1744830464 | bytes 2752512 | tf_op jit(solution)/shard_map/attend/pallas_call | solution.py:101
  6.9 24.5 %all_to_all.5.refs_0_ = bf16[16,16,1152]{2,1,0:T(8,128)(2,1)S(1)} all-to-all(bf16[16,16,1152]{2,1,0:T(8,128)(2,1)S(1)} %bitcast.12), channel_id=1, replica_groups=mesh['groups'=2,'dev'=16] {'dev'}, dimensions={0} | all-to-all | bytes 1179648 | tf_op jit(solution)/shard_map/all_to_all | solution.py:474
  33.6 1.4 %collective-permute-start.3 = (bf16[64,2048]{1,0:T(8,128)(2,1)S(1)}, bf16[64,2048]{1,0:T(8,128)(2,1)S(1)}, u32[]{:S(2)}, u32[]{:S(2)}) collective-permute-start(bf16[64,2048]{1,0:T(8,128)(2,1)S(1)} %get-tuple-element.84.refs_1_), channel_id=1, source_target_pairs={{4,0},{5,1},{8,4},{9,5},{12,8},{13,9},{14,12},{15,13},{10,14},{11,... | collective-permute-start | bytes 786440 | tf_op jit(solution)/shard_map/ppermute | solution.py:468
  35.6 1.4 %collective-permute-start.4 = (bf16[64,2048]{1,0:T(8,128)(2,1)S(1)}, bf16[64,2048]{1,0:T(8,128)(2,1)S(1)}, u32[]{:S(2)}, u32[]{:S(2)}) collective-permute-start(bf16[64,2048]{1,0:T(8,128)(2,1)S(1)} %get-tuple-element.84.refs_1_), channel_id=1, source_target_pairs={{0,4},{1,5},{4,8},{5,9},{8,12},{9,13},{12,14},{13,15},{14,10},{15,... | collective-permute-start | bytes 786440 | tf_op jit(solution)/shard_map/ppermute | solution.py:467
  37.0 2.9 %load.1 = (f32[16,128]{1,0:T(8,128)S(1)}, bf16[1,2048,1536]{2,1,0:T(8,128)(2,1)S(1)}) custom-call(f32[16,128]{1,0:T(8,128)S(1)} %get-tuple-element.79.token_ref, bf16[1,2048,1536]{2,1,0:T(8,128)(2,1)} %get-tuple-element.80.refs_0_), custom_call_target="tpu_custom_call" | custom-call | flops 1 | bytes 1 | tf_op jit(solution)/shard_map/load/pallas_call | solution.py:342
  40.0 2.1 %collective-permute-done.2.refs_0_ = bf16[64,2048]{1,0:T(8,128)(2,1)S(1)} collective-permute-done((bf16[64,2048]{1,0:T(8,128)(2,1)S(1)}, bf16[64,2048]{1,0:T(8,128)(2,1)S(1)}, u32[]{:S(2)}, u32[]{:S(2)}) %collective-permute-start.2) | collective-permute-done | bytes 262176 | tf_op jit(solution)/shard_map/ppermute | solution.py:467
  45.0 3.4 %collective-permute-done.5.refs_1_ = bf16[64,2048]{1,0:T(8,128)(2,1)S(1)} collective-permute-done((bf16[64,2048]{1,0:T(8,128)(2,1)S(1)}, bf16[64,2048]{1,0:T(8,128)(2,1)S(1)}, u32[]{:S(2)}, u32[]{:S(2)}) %collective-permute-start.5) | collective-permute-done | bytes 262176 | tf_op jit(solution)/shard_map/ppermute | solution.py:468
  48.4 1.4 %collective-permute-start.10 = (bf16[64,2048]{1,0:T(8,128)(2,1)S(1)}, bf16[64,2048]{1,0:T(8,128)(2,1)S(1)}, u32[]{:S(2)}, u32[]{:S(2)}) collective-permute-start(bf16[64,2048]{1,0:T(8,128)(2,1)S(1)} %get-tuple-element.89.refs_0_), channel_id=1, source_target_pairs={{4,0},{5,1},{8,4},{9,5},{12,8},{13,9},{14,12},{15,13},{10,14},{11,... | collective-permute-start | bytes 786440 | tf_op jit(solution)/shard_map/ppermute | solution.py:468
  50.5 2.8 %experts.6 = (bf16[128,2048]{1,0:T(8,128)(2,1)S(1)}, f32[16,128]{1,0:T(8,128)S(1)}) custom-call(s32[1]{0:T(128)} %bitcast.me_ref, f32[16,128]{1,0:T(8,128)S(1)} %get-tuple-element.86.token_ref, f32[16,128]{1,0:T(8,128)S(1)} %add_bitcast_fusion.share_a, f32[16,128]{1,0:T(8,128)S(1)} %collective-permute-done.6.share_b, bf16[1,2048,1536]{2,1,0:T(8,128)(2,1)S(1)} %bitcast.10, ...), custom_call_target="tpu_custom_call" | custom-call | flops 1 | bytes 1 | tf_op jit(solution)/shard_map/experts/pallas_call | solution.py:306
  54.1 1.4 %collective-permute-start.12 = (bf16[64,2048]{1,0:T(8,128)(2,1)S(1)}, bf16[64,2048]{1,0:T(8,128)(2,1)S(1)}, u32[]{:S(2)}, u32[]{:S(2)}) collective-permute-start(bf16[64,2048]{1,0:T(8,128)(2,1)S(1)} %get-tuple-element.98.refs_1_), channel_id=1, source_target_pairs={{4,0},{5,1},{8,4},{9,5},{12,8},{13,9},{14,12},{15,13},{10,14},{11,... | collective-permute-start | bytes 786440 | tf_op jit(solution)/shard_map/ppermute | solution.py:468
  56.1 2.8 %experts.7 = (bf16[128,2048]{1,0:T(8,128)(2,1)S(1)}, f32[16,128]{1,0:T(8,128)S(1)}) custom-call(s32[1]{0:T(128)} %bitcast.me_ref, f32[16,128]{1,0:T(8,128)S(1)} %get-tuple-element.93.token_ref, f32[16,128]{1,0:T(8,128)S(1)} %add_bitcast_fusion.share_a, f32[16,128]{1,0:T(8,128)S(1)} %collective-permute-done.6.share_b, bf16[1,2048,1536]{2,1,0:T(8,128)(2,1)S(1)} %bitcast.10, ...), custom_call_target="tpu_custom_call" | custom-call | flops 1 | bytes 1 | tf_op jit(solution)/shard_map/experts/pallas_call | solution.py:306
  59.7 1.4 %collective-permute-start.14 = (bf16[64,2048]{1,0:T(8,128)(2,1)S(1)}, bf16[64,2048]{1,0:T(8,128)(2,1)S(1)}, u32[]{:S(2)}, u32[]{:S(2)}) collective-permute-start(bf16[64,2048]{1,0:T(8,128)(2,1)S(1)} %get-tuple-element.97.refs_0_), channel_id=1, source_target_pairs={{4,0},{5,1},{8,4},{9,5},{12,8},{13,9},{14,12},{15,13},{10,14},{11,... | collective-permute-start | bytes 786440 | tf_op jit(solution)/shard_map/ppermute | solution.py:468
  61.7 5.2 %experts.8 = (bf16[256,2048]{1,0:T(8,128)(2,1)S(1)}, f32[16,128]{1,0:T(8,128)S(1)}) custom-call(s32[1]{0:T(128)} %bitcast.me_ref, f32[16,128]{1,0:T(8,128)S(1)} %get-tuple-element.96.token_ref, f32[16,128]{1,0:T(8,128)S(1)} %add_bitcast_fusion.share_a, f32[16,128]{1,0:T(8,128)S(1)} %collective-permute-done.6.share_b, bf16[1,2048,1536]{2,1,0:T(8,128)(2,1)S(1)} %bitcast.10, ...), custom_call_target="tpu_custom_call" | custom-call | flops 1 | bytes 1 | tf_op jit(solution)/shard_map/experts/pallas_call | solution.py:306
  66.9 1.4 %collective-permute-start.16 = (bf16[64,2048]{1,0:T(8,128)(2,1)S(1)}, bf16[64,2048]{1,0:T(8,128)(2,1)S(1)}, u32[]{:S(2)}, u32[]{:S(2)}) collective-permute-start(bf16[64,2048]{1,0:T(8,128)(2,1)S(1)} %get-tuple-element.103.refs_0_), channel_id=1, source_target_pairs={{4,0},{5,1},{8,4},{9,5},{12,8},{13,9},{14,12},{15,13},{10,14},{11,... | collective-permute-start | bytes 786440 | tf_op jit(solution)/shard_map/ppermute | solution.py:468
  69.0 1.9 %begin.1 = (f32[256,1536]{1,0:T(8,128)S(1)}, f32[256,1536]{1,0:T(8,128)S(1)}, f32[16,128]{1,0:T(8,128)S(1)}) custom-call(f32[16,128]{1,0:T(8,128)S(1)} %get-tuple-element.102.token_ref, bf16[1,2048,1536]{2,1,0:T(8,128)(2,1)S(1)} %bitcast.10, bf16[1,2048,1536]{2,1,0:T(8,128)(2,1)S(1)} %get-tuple-element.87.gate_up_b, ...), custom_call_target="tpu_custom_call" | custom-call | flops 1 | bytes 1 | tf_op jit(solution)/shard_map/begin/pallas_call | solution.py:223
  71.0 4.0 %experts.9 = (bf16[256,2048]{1,0:T(8,128)(2,1)S(1)}, f32[16,128]{1,0:T(8,128)S(1)}) custom-call(s32[1]{0:T(128)} %bitcast.me_ref, f32[16,128]{1,0:T(8,128)S(1)} %get-tuple-element.106.token_ref, f32[16,128]{1,0:T(8,128)S(1)} %add_bitcast_fusion.share_a, f32[16,128]{1,0:T(8,128)S(1)} %collective-permute-done.6.share_b, bf16[1,2048,1536]{2,1,0:T(8,128)(2,1)S(1)} %bitcast.10, ...), custom_call_target="tpu_custom_call" | custom-call | flops 1 | bytes 1 | tf_op jit(solution)/shard_map/experts/pallas_call | solution.py:306
  77.1 2.8 %experts.10 = (bf16[128,2048]{1,0:T(8,128)(2,1)S(1)}, f32[16,128]{1,0:T(8,128)S(1)}) custom-call(s32[1]{0:T(128)} %bitcast.me_ref, f32[16,128]{1,0:T(8,128)S(1)} %get-tuple-element.114.token_ref, f32[16,128]{1,0:T(8,128)S(1)} %add_bitcast_fusion.share_a, f32[16,128]{1,0:T(8,128)S(1)} %collective-permute-done.6.share_b, bf16[1,2048,1536]{2,1,0:T(8,128)(2,1)S(1)} %bitcast.10, ...), custom_call_target="tpu_custom_call" | custom-call | flops 1 | bytes 1 | tf_op jit(solution)/shard_map/experts/pallas_call | solution.py:306
  83.0 1.4 %collective-permute-done.18.refs_1_ = bf16[64,2048]{1,0:T(8,128)(2,1)S(1)} collective-permute-done((bf16[64,2048]{1,0:T(8,128)(2,1)S(1)}, bf16[64,2048]{1,0:T(8,128)(2,1)S(1)}, u32[]{:S(2)}, u32[]{:S(2)}) %collective-permute-start.18) | collective-permute-done | bytes 262176 | tf_op jit(solution)/shard_map/ppermute | solution.py:468
  86.6 2.6 %collective-permute-done.19.refs_0_ = bf16[64,2048]{1,0:T(8,128)(2,1)S(1)} collective-permute-done((bf16[64,2048]{1,0:T(8,128)(2,1)S(1)}, bf16[64,2048]{1,0:T(8,128)(2,1)S(1)}, u32[]{:S(2)}, u32[]{:S(2)}) %collective-permute-start.19) | collective-permute-done | bytes 262176 | tf_op jit(solution)/shard_map/ppermute | solution.py:467
  92.2 2.7 %collective-permute-done.21.refs_0_ = bf16[64,2048]{1,0:T(8,128)(2,1)S(1)} collective-permute-done((bf16[64,2048]{1,0:T(8,128)(2,1)S(1)}, bf16[64,2048]{1,0:T(8,128)(2,1)S(1)}, u32[]{:S(2)}, u32[]{:S(2)}) %collective-permute-start.21) | collective-permute-done | bytes 262176 | tf_op jit(solution)/shard_map/ppermute | solution.py:467
  97.9 2.7 %collective-permute-done.23.refs_0_ = bf16[64,2048]{1,0:T(8,128)(2,1)S(1)} collective-permute-done((bf16[64,2048]{1,0:T(8,128)(2,1)S(1)}, bf16[64,2048]{1,0:T(8,128)(2,1)S(1)}, u32[]{:S(2)}, u32[]{:S(2)}) %collective-permute-start.23) | collective-permute-done | bytes 262176 | tf_op jit(solution)/shard_map/ppermute | solution.py:467
  103.5 2.8 %experts.11 = (bf16[128,2048]{1,0:T(8,128)(2,1)S(1)}, f32[16,128]{1,0:T(8,128)S(1)}) custom-call(s32[1]{0:T(128)} %bitcast.me_ref, f32[16,128]{1,0:T(8,128)S(1)} %get-tuple-element.134.token_ref, f32[16,128]{1,0:T(8,128)S(1)} %add_bitcast_fusion.share_a, f32[16,128]{1,0:T(8,128)S(1)} %collective-permute-done.6.share_b, bf16[1,2048,1536]{2,1,0:T(8,128)(2,1)S(1)} %bitcast.10, ...), custom_call_target="tpu_custom_call" | custom-call | flops 1 | bytes 1 | tf_op jit(solution)/shard_map/experts/pallas_call | solution.py:306
  106.9 2.6 %collective-permute-done.27.refs_0_ = bf16[64,2048]{1,0:T(8,128)(2,1)S(1)} collective-permute-done((bf16[64,2048]{1,0:T(8,128)(2,1)S(1)}, bf16[64,2048]{1,0:T(8,128)(2,1)S(1)}, u32[]{:S(2)}, u32[]{:S(2)}) %collective-permute-start.27) | collective-permute-done | bytes 262176 | tf_op jit(solution)/shard_map/ppermute | solution.py:467
  112.6 4.3 %collective-permute-done.29.refs_2_ = bf16[64,2048]{1,0:T(8,128)(2,1)S(1)} collective-permute-done((bf16[64,2048]{1,0:T(8,128)(2,1)S(1)}, bf16[64,2048]{1,0:T(8,128)(2,1)S(1)}, u32[]{:S(2)}, u32[]{:S(2)}) %collective-permute-start.29) | collective-permute-done | bytes 262176 | tf_op jit(solution)/shard_map/ppermute | solution.py:467
  (80 shorter events, 32.4 us)
Async XLA Ops:
  0.0 31.4 %collective-permute-start = (bf16[1,2048,1536]{2,1,0:T(8,128)(2,1)}, bf16[1,2048,1536]{2,1,0:T(8,128)(2,1)}, u32[]{:S(2)}, u32[]{:S(2)}) collective-permute-start(bf16[1,2048,1536]{2,1,0:T(8,128)(2,1)} %gate_up_a.13), channel_id=1, source_target_pairs={{0,1},{1,0},{2,3},{3,2},{4,5},{5,4},{6,7},{7,6},{8,9},{9,8},{10,11... | collective-permute-start | bytes 18874376 | tf_op jit(solution)/shard_map/ppermute | solution.py:469
  0.5 30.9 %collective-permute-start.1 = (bf16[1,768,2048]{2,1,0:T(8,128)(2,1)}, bf16[1,768,2048]{2,1,0:T(8,128)(2,1)S(1)}, u32[]{:S(2)}, u32[]{:S(2)}) collective-permute-start(bf16[1,768,2048]{2,1,0:T(8,128)(2,1)} %down_a.11), channel_id=1, source_target_pairs={{0,1},{1,0},{2,3},{3,2},{4,5},{5,4},{6,7},{7,6},{8,9},{9,8},{10,11... | collective-permute-start | bytes 9437192 | tf_op jit(solution)/shard_map/ppermute | solution.py:469
  32.9 9.2 %collective-permute-start.2 = (bf16[64,2048]{1,0:T(8,128)(2,1)S(1)}, bf16[64,2048]{1,0:T(8,128)(2,1)S(1)}, u32[]{:S(2)}, u32[]{:S(2)}) collective-permute-start(bf16[64,2048]{1,0:T(8,128)(2,1)S(1)} %get-tuple-element.83.refs_0_), channel_id=1, source_target_pairs={{0,4},{1,5},{4,8},{5,9},{8,12},{9,13},{12,14},{13,15},{14,10},{15,... | collective-permute-start | bytes 786440 | tf_op jit(solution)/shard_map/ppermute | solution.py:467
  33.6 9.2 %collective-permute-start.3 = (bf16[64,2048]{1,0:T(8,128)(2,1)S(1)}, bf16[64,2048]{1,0:T(8,128)(2,1)S(1)}, u32[]{:S(2)}, u32[]{:S(2)}) collective-permute-start(bf16[64,2048]{1,0:T(8,128)(2,1)S(1)} %get-tuple-element.84.refs_1_), channel_id=1, source_target_pairs={{4,0},{5,1},{8,4},{9,5},{12,8},{13,9},{14,12},{15,13},{10,14},{11,... | collective-permute-start | bytes 786440 | tf_op jit(solution)/shard_map/ppermute | solution.py:468
  35.0 13.4 %collective-permute-start.5 = (bf16[64,2048]{1,0:T(8,128)(2,1)S(1)}, bf16[64,2048]{1,0:T(8,128)(2,1)S(1)}, u32[]{:S(2)}, u32[]{:S(2)}) collective-permute-start(bf16[64,2048]{1,0:T(8,128)(2,1)S(1)} %get-tuple-element.83.refs_0_), channel_id=1, source_target_pairs={{4,0},{5,1},{8,4},{9,5},{12,8},{13,9},{14,12},{15,13},{10,14},{11,... | collective-permute-start | bytes 786440 | tf_op jit(solution)/shard_map/ppermute | solution.py:468
  35.6 12.8 %collective-permute-start.4 = (bf16[64,2048]{1,0:T(8,128)(2,1)S(1)}, bf16[64,2048]{1,0:T(8,128)(2,1)S(1)}, u32[]{:S(2)}, u32[]{:S(2)}) collective-permute-start(bf16[64,2048]{1,0:T(8,128)(2,1)S(1)} %get-tuple-element.84.refs_1_), channel_id=1, source_target_pairs={{0,4},{1,5},{4,8},{5,9},{8,12},{9,13},{12,14},{13,15},{14,10},{15,... | collective-permute-start | bytes 786440 | tf_op jit(solution)/shard_map/ppermute | solution.py:467
  42.8 11.2 %collective-permute-start.8 = (bf16[64,2048]{1,0:T(8,128)(2,1)S(1)}, bf16[64,2048]{1,0:T(8,128)(2,1)S(1)}, u32[]{:S(2)}, u32[]{:S(2)}) collective-permute-start(bf16[64,2048]{1,0:T(8,128)(2,1)S(1)} %get-tuple-element.90.refs_1_), channel_id=1, source_target_pairs={{4,0},{5,1},{8,4},{9,5},{12,8},{13,9},{14,12},{15,13},{10,14},{11,... | collective-permute-start | bytes 786440 | tf_op jit(solution)/shard_map/ppermute | solution.py:468
  44.2 9.9 %collective-permute-start.7 = (bf16[64,2048]{1,0:T(8,128)(2,1)S(1)}, bf16[64,2048]{1,0:T(8,128)(2,1)S(1)}, u32[]{:S(2)}, u32[]{:S(2)}) collective-permute-start(bf16[64,2048]{1,0:T(8,128)(2,1)S(1)} %get-tuple-element.92.refs_0_), channel_id=1, source_target_pairs={{0,4},{1,5},{4,8},{5,9},{8,12},{9,13},{12,14},{13,15},{14,10},{15,... | collective-permute-start | bytes 786440 | tf_op jit(solution)/shard_map/ppermute | solution.py:467
  48.4 11.2 %collective-permute-start.10 = (bf16[64,2048]{1,0:T(8,128)(2,1)S(1)}, bf16[64,2048]{1,0:T(8,128)(2,1)S(1)}, u32[]{:S(2)}, u32[]{:S(2)}) collective-permute-start(bf16[64,2048]{1,0:T(8,128)(2,1)S(1)} %get-tuple-element.89.refs_0_), channel_id=1, source_target_pairs={{4,0},{5,1},{8,4},{9,5},{12,8},{13,9},{14,12},{15,13},{10,14},{11,... | collective-permute-start | bytes 786440 | tf_op jit(solution)/shard_map/ppermute | solution.py:468
  49.8 9.9 %collective-permute-start.9 = (bf16[64,2048]{1,0:T(8,128)(2,1)S(1)}, bf16[64,2048]{1,0:T(8,128)(2,1)S(1)}, u32[]{:S(2)}, u32[]{:S(2)}) collective-permute-start(bf16[64,2048]{1,0:T(8,128)(2,1)S(1)} %get-tuple-element.94.refs_1_), channel_id=1, source_target_pairs={{0,4},{1,5},{4,8},{5,9},{8,12},{9,13},{12,14},{13,15},{14,10},{15,... | collective-permute-start | bytes 786440 | tf_op jit(solution)/shard_map/ppermute | solution.py:467
  54.1 12.8 %collective-permute-start.12 = (bf16[64,2048]{1,0:T(8,128)(2,1)S(1)}, bf16[64,2048]{1,0:T(8,128)(2,1)S(1)}, u32[]{:S(2)}, u32[]{:S(2)}) collective-permute-start(bf16[64,2048]{1,0:T(8,128)(2,1)S(1)} %get-tuple-element.98.refs_1_), channel_id=1, source_target_pairs={{4,0},{5,1},{8,4},{9,5},{12,8},{13,9},{14,12},{15,13},{10,14},{11,... | collective-permute-start | bytes 786440 | tf_op jit(solution)/shard_map/ppermute | solution.py:468
  55.4 11.4 %collective-permute-start.11 = (bf16[64,2048]{1,0:T(8,128)(2,1)S(1)}, bf16[64,2048]{1,0:T(8,128)(2,1)S(1)}, u32[]{:S(2)}, u32[]{:S(2)}) collective-permute-start(bf16[64,2048]{1,0:T(8,128)(2,1)S(1)} %get-tuple-element.99.refs_2_), channel_id=1, source_target_pairs={{0,4},{1,5},{4,8},{5,9},{8,12},{9,13},{12,14},{13,15},{14,10},{15,... | collective-permute-start | bytes 786440 | tf_op jit(solution)/shard_map/ppermute | solution.py:467
  59.7 11.3 %collective-permute-start.14 = (bf16[64,2048]{1,0:T(8,128)(2,1)S(1)}, bf16[64,2048]{1,0:T(8,128)(2,1)S(1)}, u32[]{:S(2)}, u32[]{:S(2)}) collective-permute-start(bf16[64,2048]{1,0:T(8,128)(2,1)S(1)} %get-tuple-element.97.refs_0_), channel_id=1, source_target_pairs={{4,0},{5,1},{8,4},{9,5},{12,8},{13,9},{14,12},{15,13},{10,14},{11,... | collective-permute-start | bytes 786440 | tf_op jit(solution)/shard_map/ppermute | solution.py:468
  61.1 9.9 %collective-permute-start.13 = (bf16[64,2048]{1,0:T(8,128)(2,1)S(1)}, bf16[64,2048]{1,0:T(8,128)(2,1)S(1)}, u32[]{:S(2)}, u32[]{:S(2)}) collective-permute-start(bf16[64,2048]{1,0:T(8,128)(2,1)S(1)} %get-tuple-element.100.refs_3_), channel_id=1, source_target_pairs={{0,4},{1,5},{4,8},{5,9},{8,12},{9,13},{12,14},{13,15},{14,10},{15,... | collective-permute-start | bytes 786440 | tf_op jit(solution)/shard_map/ppermute | solution.py:467
  66.9 10.2 %collective-permute-start.16 = (bf16[64,2048]{1,0:T(8,128)(2,1)S(1)}, bf16[64,2048]{1,0:T(8,128)(2,1)S(1)}, u32[]{:S(2)}, u32[]{:S(2)}) collective-permute-start(bf16[64,2048]{1,0:T(8,128)(2,1)S(1)} %get-tuple-element.103.refs_0_), channel_id=1, source_target_pairs={{4,0},{5,1},{8,4},{9,5},{12,8},{13,9},{14,12},{15,13},{10,14},{11,... | collective-permute-start | bytes 786440 | tf_op jit(solution)/shard_map/ppermute | solution.py:468
  68.3 8.8 %collective-permute-start.15 = (bf16[64,2048]{1,0:T(8,128)(2,1)S(1)}, bf16[64,2048]{1,0:T(8,128)(2,1)S(1)}, u32[]{:S(2)}, u32[]{:S(2)}) collective-permute-start(bf16[64,2048]{1,0:T(8,128)(2,1)S(1)} %get-tuple-element.104.refs_1_), channel_id=1, source_target_pairs={{0,4},{1,5},{4,8},{5,9},{8,12},{9,13},{12,14},{13,15},{14,10},{15,... | collective-permute-start | bytes 786440 | tf_op jit(solution)/shard_map/ppermute | solution.py:467
  80.0 9.3 %collective-permute-start.19 = (bf16[64,2048]{1,0:T(8,128)(2,1)S(1)}, bf16[64,2048]{1,0:T(8,128)(2,1)S(1)}, u32[]{:S(2)}, u32[]{:S(2)}) collective-permute-start(bf16[64,2048]{1,0:T(8,128)(2,1)S(1)} %get-tuple-element.124), channel_id=1, source_target_pairs={{0,4},{1,5},{4,8},{5,9},{8,12},{9,13},{12,14},{13,15},{14,10},{15,... | collective-permute-start | bytes 786440 | tf_op jit(solution)/shard_map/ppermute | solution.py:467
  80.8 9.2 %collective-permute-start.20 = (bf16[64,2048]{1,0:T(8,128)(2,1)S(1)}, bf16[64,2048]{1,0:T(8,128)(2,1)S(1)}, u32[]{:S(2)}, u32[]{:S(2)}) collective-permute-start(bf16[64,2048]{1,0:T(8,128)(2,1)S(1)} %get-tuple-element.125), channel_id=1, source_target_pairs={{4,0},{5,1},{8,4},{9,5},{12,8},{13,9},{14,12},{15,13},{10,14},{11,... | collective-permute-start | bytes 786440 | tf_op jit(solution)/shard_map/ppermute | solution.py:468
  84.5 10.3 %collective-permute-start.21 = (bf16[64,2048]{1,0:T(8,128)(2,1)S(1)}, bf16[64,2048]{1,0:T(8,128)(2,1)S(1)}, u32[]{:S(2)}, u32[]{:S(2)}) collective-permute-start(bf16[64,2048]{1,0:T(8,128)(2,1)S(1)} %get-tuple-element.129), channel_id=1, source_target_pairs={{0,4},{1,5},{4,8},{5,9},{8,12},{9,13},{12,14},{13,15},{14,10},{15,... | collective-permute-start | bytes 786440 | tf_op jit(solution)/shard_map/ppermute | solution.py:467
  85.4 10.2 %collective-permute-start.22 = (bf16[64,2048]{1,0:T(8,128)(2,1)S(1)}, bf16[64,2048]{1,0:T(8,128)(2,1)S(1)}, u32[]{:S(2)}, u32[]{:S(2)}) collective-permute-start(bf16[64,2048]{1,0:T(8,128)(2,1)S(1)} %get-tuple-element.130), channel_id=1, source_target_pairs={{4,0},{5,1},{8,4},{9,5},{12,8},{13,9},{14,12},{15,13},{10,14},{11,... | collective-permute-start | bytes 786440 | tf_op jit(solution)/shard_map/ppermute | solution.py:468
  90.2 10.3 %collective-permute-start.23 = (bf16[64,2048]{1,0:T(8,128)(2,1)S(1)}, bf16[64,2048]{1,0:T(8,128)(2,1)S(1)}, u32[]{:S(2)}, u32[]{:S(2)}) collective-permute-start(bf16[64,2048]{1,0:T(8,128)(2,1)S(1)} %get-tuple-element.132), channel_id=1, source_target_pairs={{0,4},{1,5},{4,8},{5,9},{8,12},{9,13},{12,14},{13,15},{14,10},{15,... | collective-permute-start | bytes 786440 | tf_op jit(solution)/shard_map/ppermute | solution.py:467
  91.4 9.9 %collective-permute-start.24 = (bf16[64,2048]{1,0:T(8,128)(2,1)S(1)}, bf16[64,2048]{1,0:T(8,128)(2,1)S(1)}, u32[]{:S(2)}, u32[]{:S(2)}) collective-permute-start(bf16[64,2048]{1,0:T(8,128)(2,1)S(1)} %get-tuple-element.133), channel_id=1, source_target_pairs={{4,0},{5,1},{8,4},{9,5},{12,8},{13,9},{14,12},{15,13},{10,14},{11,... | collective-permute-start | bytes 786440 | tf_op jit(solution)/shard_map/ppermute | solution.py:468
  95.8 10.5 %collective-permute-start.25 = (bf16[64,2048]{1,0:T(8,128)(2,1)S(1)}, bf16[64,2048]{1,0:T(8,128)(2,1)S(1)}, u32[]{:S(2)}, u32[]{:S(2)}) collective-permute-start(bf16[64,2048]{1,0:T(8,128)(2,1)S(1)} %get-tuple-element.136), channel_id=1, source_target_pairs={{0,4},{1,5},{4,8},{5,9},{8,12},{9,13},{12,14},{13,15},{14,10},{15,... | collective-permute-start | bytes 786440 | tf_op jit(solution)/shard_map/ppermute | solution.py:467
  97.0 9.9 %collective-permute-start.26 = (bf16[64,2048]{1,0:T(8,128)(2,1)S(1)}, bf16[64,2048]{1,0:T(8,128)(2,1)S(1)}, u32[]{:S(2)}, u32[]{:S(2)}) collective-permute-start(bf16[64,2048]{1,0:T(8,128)(2,1)S(1)} %get-tuple-element.137), channel_id=1, source_target_pairs={{4,0},{5,1},{8,4},{9,5},{12,8},{13,9},{14,12},{15,13},{10,14},{11,... | collective-permute-start | bytes 786440 | tf_op jit(solution)/shard_map/ppermute | solution.py:468
  (12 other events, 104.7 us)

commit v6 on v5

--- a/solution.py
+++ b/solution.py
@@ -24,7 +24,7 @@
     row = lax.broadcasted_iota(jnp.int32, (length, length), 0)
     col = lax.broadcasted_iota(jnp.int32, (length, length), 1)
     heads = feat_width // head_size
-    stack = 2 if heads % 2 == 0 else 1
+    stack = next(k for k in (4, 2, 1) if heads % k == 0)
     allowed = jnp.concatenate([col <= row] * stack, axis=0)
 
     def put(cols, value):
@@ -58,22 +58,29 @@
     batches, top, tokens = ids_ref.shape
     lines = batches * tokens
     last = slice(feat_width, feat_width + lines)
-    tables = []
-    for batch in range(batches):
-        shares = gates_ref[batch].astype(F32)
-        shares = shares / jnp.sum(shares, axis=0, keepdims=True)
-        expert = lax.broadcasted_iota(jnp.int32, (devices, tokens), 0)
-        table = jnp.zeros((devices, tokens), F32)
-        for k in range(top):
-            named = expert == ids_ref[batch, k : k + 1]
-            table += jnp.where(named, shares[k : k + 1], 0.0)
-        tables.append(table)
-    table = jnp.concatenate(tables, axis=1)
-    high = table.astype(BF16).astype(F32)
-    part = lax.broadcasted_iota(jnp.int32, (devices, positions, lines), 1)
-    spread = [jnp.broadcast_to(x[:, None, :], part.shape) for x in (high, table - high)]
-    both = jnp.where(part == 0, spread[0], jnp.where(part == 1, spread[1], 0.0))
-    put(last, both.reshape(length, lines))
+
+    @pl.when(pl.program_id(0) == 0)
+    def _():
+        tables = []
+        for batch in range(batches):
+            shares = gates_ref[batch].astype(F32)
+            shares = shares / jnp.sum(shares, axis=0, keepdims=True)
+            expert = lax.broadcasted_iota(jnp.int32, (devices, tokens), 0)
+            table = jnp.zeros((devices, tokens), F32)
+            for k in range(top):
+                named = expert == ids_ref[batch, k : k + 1]
+                table += jnp.where(named, shares[k : k + 1], 0.0)
+            tables.append(table)
+        table = jnp.concatenate(tables, axis=1)
+        high = table.astype(BF16).astype(F32)
+        part = lax.broadcasted_iota(jnp.int32, (devices, positions, lines), 1)
+        spread = [jnp.broadcast_to(x[:, None, :], part.shape) for x in (high, table - high)]
+        both = jnp.where(part == 0, spread[0], jnp.where(part == 1, spread[1], 0.0))
+        put(last, both.reshape(length, lines))
+
+    @pl.when(pl.program_id(0) > 0)
+    def _():
+        put(last, jnp.zeros((length, lines), F32))
 
 
 def attend(queries, keys_values, expert_ids, expert_gates, devices):
@@ -109,7 +116,7 @@
         + [pl.BlockSpec(c.shape, lambda i: (0, 0, 0)) for c in choices],
         out_specs=out_spec,
         scratch_shapes=[pltpu.VMEM((context, 2 * head_size), BF16)],
-        compiler_params=pltpu.CompilerParams(vmem_limit_bytes=24 << 20),
+        compiler_params=pltpu.CompilerParams(vmem_limit_bytes=14 << 20),
         cost_estimate=pl.CostEstimate(
             flops=4 * pairs * head_size,
             bytes_accessed=2 * batches * (2 * length * feat_width + 2 * context * head_size),

time: 119 us -> 119 us (level)
  no operation moved by 1% of the time
where the time goes in v6:
time: 119 us
  Pallas kernels  33.5 us (28%)
  waiting for transfers between devices  29.9 us (25%)
  starting transfers between devices  29.4 us (25%)
  blocking collectives  24.5 us (21%)
  local copies, waits for them, and re-layouts  1.27 us (1%)
    all_to_all x1, blocking collectives, body(): lax.all_to_all(rows.reshape(devices, -1, rows.shape[-1]), 'dev', split_ax...  24.5 us
    pallas_call x6, Pallas kernels, run_experts(): pl.pallas_call(functools.partial(expert_kernel, places=places, sides=side...  20.4 us
    ppermute x14, waiting for transfers between devices, body(): send_ahead = lambda x: lax.ppermute(x, 'dev', forward)  18 us
    ppermute x14, starting transfers between devices, body(): send_behind = lambda x: lax.ppermute(x, 'dev', backward)  16 us
    ppermute x14, starting transfers between devices, body(): send_ahead = lambda x: lax.ppermute(x, 'dev', forward)  12.8 us
    ppermute x14, waiting for transfers between devices, body(): send_behind = lambda x: lax.ppermute(x, 'dev', backward)  11.9 us
    pallas_call x1, Pallas kernels, attend(): pl.pallas_call(functools.partial(attend_kernel, devices=devices), out_sha...  6.08 us
    pallas_call x1, Pallas kernels, load(): pl.pallas_call(load_kernel, out_shape=[jax.ShapeDtypeStruct(x.shape, x.dt...  2.94 us
  transfers between devices with their start and end apart: 31, of which 18 were waited for; matrix products, arithmetic and copies ran while one was open for 0% of the time, Pallas kernels for 27%

profile of v6, /device:TPU:0, one launch (start us, length us, event | category | flops | bytes accessed | tf_op | source)
XLA Modules:
  0.0 118.9 jit_solution(18295842926782099126)
XLA Ops:
  0.5 6.1 %attend.1 = bf16[16,2,8,1152]{3,2,1,0:T(8,128)(2,1)S(1)} custom-call(bf16[2,1,128,1024]{3,2,1,0:T(8,128)(2,1)} %q_ref, bf16[2,1,2,1664,128]{4,3,2,1,0:T(8,128)(2,1)} %kv_ref.1, s32[2,8,64]{2,1,0:T(8,128)} %bitcast.15, s32[2,8,64]{2,1,0:T(8,128)} %bitcast.16), custom_call_target="tpu_custom_call" | custom-call | flops 1744830464 | bytes 2752512 | tf_op jit(solution)/shard_map/attend/pallas_call | solution.py:108
  6.6 24.5 %all_to_all.5.refs_0_ = bf16[16,16,1152]{2,1,0:T(8,128)(2,1)S(1)} all-to-all(bf16[16,16,1152]{2,1,0:T(8,128)(2,1)S(1)} %bitcast.12), channel_id=1, replica_groups=mesh['groups'=2,'dev'=16] {'dev'}, dimensions={0} | all-to-all | bytes 1179648 | tf_op jit(solution)/shard_map/all_to_all | solution.py:481
  35.3 1.4 %collective-permute-start.4 = (bf16[64,2048]{1,0:T(8,128)(2,1)S(1)}, bf16[64,2048]{1,0:T(8,128)(2,1)S(1)}, u32[]{:S(2)}, u32[]{:S(2)}) collective-permute-start(bf16[64,2048]{1,0:T(8,128)(2,1)S(1)} %get-tuple-element.84.refs_1_), channel_id=1, source_target_pairs={{0,4},{1,5},{4,8},{5,9},{8,12},{9,13},{12,14},{13,15},{14,10},{15,... | collective-permute-start | bytes 786440 | tf_op jit(solution)/shard_map/ppermute | solution.py:474
  36.7 2.9 %load.1 = (f32[16,128]{1,0:T(8,128)S(1)}, bf16[1,2048,1536]{2,1,0:T(8,128)(2,1)S(1)}) custom-call(f32[16,128]{1,0:T(8,128)S(1)} %get-tuple-element.79.token_ref, bf16[1,2048,1536]{2,1,0:T(8,128)(2,1)} %get-tuple-element.80.refs_0_), custom_call_target="tpu_custom_call" | custom-call | flops 1 | bytes 1 | tf_op jit(solution)/shard_map/load/pallas_call | solution.py:349
  39.7 2.1 %collective-permute-done.2.refs_0_ = bf16[64,2048]{1,0:T(8,128)(2,1)S(1)} collective-permute-done((bf16[64,2048]{1,0:T(8,128)(2,1)S(1)}, bf16[64,2048]{1,0:T(8,128)(2,1)S(1)}, u32[]{:S(2)}, u32[]{:S(2)}) %collective-permute-start.2) | collective-permute-done | bytes 262176 | tf_op jit(solution)/shard_map/ppermute | solution.py:474
  42.5 1.4 %collective-permute-start.8 = (bf16[64,2048]{1,0:T(8,128)(2,1)S(1)}, bf16[64,2048]{1,0:T(8,128)(2,1)S(1)}, u32[]{:S(2)}, u32[]{:S(2)}) collective-permute-start(bf16[64,2048]{1,0:T(8,128)(2,1)S(1)} %get-tuple-element.90.refs_1_), channel_id=1, source_target_pairs={{4,0},{5,1},{8,4},{9,5},{12,8},{13,9},{14,12},{15,13},{10,14},{11,... | collective-permute-start | bytes 786440 | tf_op jit(solution)/shard_map/ppermute | solution.py:475
  44.7 3.4 %collective-permute-done.5.refs_1_ = bf16[64,2048]{1,0:T(8,128)(2,1)S(1)} collective-permute-done((bf16[64,2048]{1,0:T(8,128)(2,1)S(1)}, bf16[64,2048]{1,0:T(8,128)(2,1)S(1)}, u32[]{:S(2)}, u32[]{:S(2)}) %collective-permute-start.5) | collective-permute-done | bytes 262176 | tf_op jit(solution)/shard_map/ppermute | solution.py:475
  48.1 1.4 %collective-permute-start.10 = (bf16[64,2048]{1,0:T(8,128)(2,1)S(1)}, bf16[64,2048]{1,0:T(8,128)(2,1)S(1)}, u32[]{:S(2)}, u32[]{:S(2)}) collective-permute-start(bf16[64,2048]{1,0:T(8,128)(2,1)S(1)} %get-tuple-element.89.refs_0_), channel_id=1, source_target_pairs={{4,0},{5,1},{8,4},{9,5},{12,8},{13,9},{14,12},{15,13},{10,14},{11,... | collective-permute-start | bytes 786440 | tf_op jit(solution)/shard_map/ppermute | solution.py:475
  50.2 2.8 %experts.6 = (bf16[128,2048]{1,0:T(8,128)(2,1)S(1)}, f32[16,128]{1,0:T(8,128)S(1)}) custom-call(s32[1]{0:T(128)} %bitcast.me_ref, f32[16,128]{1,0:T(8,128)S(1)} %get-tuple-element.86.token_ref, f32[16,128]{1,0:T(8,128)S(1)} %add_bitcast_fusion.share_a, f32[16,128]{1,0:T(8,128)S(1)} %collective-permute-done.6.share_b, bf16[1,2048,1536]{2,1,0:T(8,128)(2,1)S(1)} %bitcast.10, ...), custom_call_target="tpu_custom_call" | custom-call | flops 1 | bytes 1 | tf_op jit(solution)/shard_map/experts/pallas_call | solution.py:313
  53.8 1.4 %collective-permute-start.12 = (bf16[64,2048]{1,0:T(8,128)(2,1)S(1)}, bf16[64,2048]{1,0:T(8,128)(2,1)S(1)}, u32[]{:S(2)}, u32[]{:S(2)}) collective-permute-start(bf16[64,2048]{1,0:T(8,128)(2,1)S(1)} %get-tuple-element.98.refs_1_), channel_id=1, source_target_pairs={{4,0},{5,1},{8,4},{9,5},{12,8},{13,9},{14,12},{15,13},{10,14},{11,... | collective-permute-start | bytes 786440 | tf_op jit(solution)/shard_map/ppermute | solution.py:475
  55.8 2.8 %experts.7 = (bf16[128,2048]{1,0:T(8,128)(2,1)S(1)}, f32[16,128]{1,0:T(8,128)S(1)}) custom-call(s32[1]{0:T(128)} %bitcast.me_ref, f32[16,128]{1,0:T(8,128)S(1)} %get-tuple-element.93.token_ref, f32[16,128]{1,0:T(8,128)S(1)} %add_bitcast_fusion.share_a, f32[16,128]{1,0:T(8,128)S(1)} %collective-permute-done.6.share_b, bf16[1,2048,1536]{2,1,0:T(8,128)(2,1)S(1)} %bitcast.10, ...), custom_call_target="tpu_custom_call" | custom-call | flops 1 | bytes 1 | tf_op jit(solution)/shard_map/experts/pallas_call | solution.py:313
  59.4 1.4 %collective-permute-start.14 = (bf16[64,2048]{1,0:T(8,128)(2,1)S(1)}, bf16[64,2048]{1,0:T(8,128)(2,1)S(1)}, u32[]{:S(2)}, u32[]{:S(2)}) collective-permute-start(bf16[64,2048]{1,0:T(8,128)(2,1)S(1)} %get-tuple-element.97.refs_0_), channel_id=1, source_target_pairs={{4,0},{5,1},{8,4},{9,5},{12,8},{13,9},{14,12},{15,13},{10,14},{11,... | collective-permute-start | bytes 786440 | tf_op jit(solution)/shard_map/ppermute | solution.py:475
  61.4 5.2 %experts.8 = (bf16[256,2048]{1,0:T(8,128)(2,1)S(1)}, f32[16,128]{1,0:T(8,128)S(1)}) custom-call(s32[1]{0:T(128)} %bitcast.me_ref, f32[16,128]{1,0:T(8,128)S(1)} %get-tuple-element.96.token_ref, f32[16,128]{1,0:T(8,128)S(1)} %add_bitcast_fusion.share_a, f32[16,128]{1,0:T(8,128)S(1)} %collective-permute-done.6.share_b, bf16[1,2048,1536]{2,1,0:T(8,128)(2,1)S(1)} %bitcast.10, ...), custom_call_target="tpu_custom_call" | custom-call | flops 1 | bytes 1 | tf_op jit(solution)/shard_map/experts/pallas_call | solution.py:313
  66.6 1.4 %collective-permute-start.16 = (bf16[64,2048]{1,0:T(8,128)(2,1)S(1)}, bf16[64,2048]{1,0:T(8,128)(2,1)S(1)}, u32[]{:S(2)}, u32[]{:S(2)}) collective-permute-start(bf16[64,2048]{1,0:T(8,128)(2,1)S(1)} %get-tuple-element.103.refs_0_), channel_id=1, source_target_pairs={{4,0},{5,1},{8,4},{9,5},{12,8},{13,9},{14,12},{15,13},{10,14},{11,... | collective-permute-start | bytes 786440 | tf_op jit(solution)/shard_map/ppermute | solution.py:475
  68.7 1.9 %begin.1 = (f32[256,1536]{1,0:T(8,128)S(1)}, f32[256,1536]{1,0:T(8,128)S(1)}, f32[16,128]{1,0:T(8,128)S(1)}) custom-call(f32[16,128]{1,0:T(8,128)S(1)} %get-tuple-element.102.token_ref, bf16[1,2048,1536]{2,1,0:T(8,128)(2,1)S(1)} %bitcast.10, bf16[1,2048,1536]{2,1,0:T(8,128)(2,1)S(1)} %get-tuple-element.87.gate_up_b, ...), custom_call_target="tpu_custom_call" | custom-call | flops 1 | bytes 1 | tf_op jit(solution)/shard_map/begin/pallas_call | solution.py:230
  70.7 4.0 %experts.9 = (bf16[256,2048]{1,0:T(8,128)(2,1)S(1)}, f32[16,128]{1,0:T(8,128)S(1)}) custom-call(s32[1]{0:T(128)} %bitcast.me_ref, f32[16,128]{1,0:T(8,128)S(1)} %get-tuple-element.106.token_ref, f32[16,128]{1,0:T(8,128)S(1)} %add_bitcast_fusion.share_a, f32[16,128]{1,0:T(8,128)S(1)} %collective-permute-done.6.share_b, bf16[1,2048,1536]{2,1,0:T(8,128)(2,1)S(1)} %bitcast.10, ...), custom_call_target="tpu_custom_call" | custom-call | flops 1 | bytes 1 | tf_op jit(solution)/shard_map/experts/pallas_call | solution.py:313
  76.8 2.8 %experts.10 = (bf16[128,2048]{1,0:T(8,128)(2,1)S(1)}, f32[16,128]{1,0:T(8,128)S(1)}) custom-call(s32[1]{0:T(128)} %bitcast.me_ref, f32[16,128]{1,0:T(8,128)S(1)} %get-tuple-element.114.token_ref, f32[16,128]{1,0:T(8,128)S(1)} %add_bitcast_fusion.share_a, f32[16,128]{1,0:T(8,128)S(1)} %collective-permute-done.6.share_b, bf16[1,2048,1536]{2,1,0:T(8,128)(2,1)S(1)} %bitcast.10, ...), custom_call_target="tpu_custom_call" | custom-call | flops 1 | bytes 1 | tf_op jit(solution)/shard_map/experts/pallas_call | solution.py:313
  82.7 1.4 %collective-permute-done.18.refs_1_ = bf16[64,2048]{1,0:T(8,128)(2,1)S(1)} collective-permute-done((bf16[64,2048]{1,0:T(8,128)(2,1)S(1)}, bf16[64,2048]{1,0:T(8,128)(2,1)S(1)}, u32[]{:S(2)}, u32[]{:S(2)}) %collective-permute-start.18) | collective-permute-done | bytes 262176 | tf_op jit(solution)/shard_map/ppermute | solution.py:475
  86.3 2.7 %collective-permute-done.19.refs_0_ = bf16[64,2048]{1,0:T(8,128)(2,1)S(1)} collective-permute-done((bf16[64,2048]{1,0:T(8,128)(2,1)S(1)}, bf16[64,2048]{1,0:T(8,128)(2,1)S(1)}, u32[]{:S(2)}, u32[]{:S(2)}) %collective-permute-start.19) | collective-permute-done | bytes 262176 | tf_op jit(solution)/shard_map/ppermute | solution.py:474
  92.0 2.6 %collective-permute-done.21.refs_0_ = bf16[64,2048]{1,0:T(8,128)(2,1)S(1)} collective-permute-done((bf16[64,2048]{1,0:T(8,128)(2,1)S(1)}, bf16[64,2048]{1,0:T(8,128)(2,1)S(1)}, u32[]{:S(2)}, u32[]{:S(2)}) %collective-permute-start.21) | collective-permute-done | bytes 262176 | tf_op jit(solution)/shard_map/ppermute | solution.py:474
  97.6 2.6 %collective-permute-done.23.refs_0_ = bf16[64,2048]{1,0:T(8,128)(2,1)S(1)} collective-permute-done((bf16[64,2048]{1,0:T(8,128)(2,1)S(1)}, bf16[64,2048]{1,0:T(8,128)(2,1)S(1)}, u32[]{:S(2)}, u32[]{:S(2)}) %collective-permute-start.23) | collective-permute-done | bytes 262176 | tf_op jit(solution)/shard_map/ppermute | solution.py:474
  103.2 2.8 %experts.11 = (bf16[128,2048]{1,0:T(8,128)(2,1)S(1)}, f32[16,128]{1,0:T(8,128)S(1)}) custom-call(s32[1]{0:T(128)} %bitcast.me_ref, f32[16,128]{1,0:T(8,128)S(1)} %get-tuple-element.134.token_ref, f32[16,128]{1,0:T(8,128)S(1)} %add_bitcast_fusion.share_a, f32[16,128]{1,0:T(8,128)S(1)} %collective-permute-done.6.share_b, bf16[1,2048,1536]{2,1,0:T(8,128)(2,1)S(1)} %bitcast.10, ...), custom_call_target="tpu_custom_call" | custom-call | flops 1 | bytes 1 | tf_op jit(solution)/shard_map/experts/pallas_call | solution.py:313
  106.6 2.6 %collective-permute-done.27.refs_0_ = bf16[64,2048]{1,0:T(8,128)(2,1)S(1)} collective-permute-done((bf16[64,2048]{1,0:T(8,128)(2,1)S(1)}, bf16[64,2048]{1,0:T(8,128)(2,1)S(1)}, u32[]{:S(2)}, u32[]{:S(2)}) %collective-permute-start.27) | collective-permute-done | bytes 262176 | tf_op jit(solution)/shard_map/ppermute | solution.py:474
  112.3 4.3 %collective-permute-done.29.refs_2_ = bf16[64,2048]{1,0:T(8,128)(2,1)S(1)} collective-permute-done((bf16[64,2048]{1,0:T(8,128)(2,1)S(1)}, bf16[64,2048]{1,0:T(8,128)(2,1)S(1)}, u32[]{:S(2)}, u32[]{:S(2)}) %collective-permute-start.29) | collective-permute-done | bytes 262176 | tf_op jit(solution)/shard_map/ppermute | solution.py:474
  (80 shorter events, 32.5 us)
Async XLA Ops:
  0.0 31.1 %collective-permute-start = (bf16[1,2048,1536]{2,1,0:T(8,128)(2,1)}, bf16[1,2048,1536]{2,1,0:T(8,128)(2,1)}, u32[]{:S(2)}, u32[]{:S(2)}) collective-permute-start(bf16[1,2048,1536]{2,1,0:T(8,128)(2,1)} %gate_up_a.13), channel_id=1, source_target_pairs={{0,1},{1,0},{2,3},{3,2},{4,5},{5,4},{6,7},{7,6},{8,9},{9,8},{10,11... | collective-permute-start | bytes 18874376 | tf_op jit(solution)/shard_map/ppermute | solution.py:476
  0.5 30.6 %collective-permute-start.1 = (bf16[1,768,2048]{2,1,0:T(8,128)(2,1)}, bf16[1,768,2048]{2,1,0:T(8,128)(2,1)S(1)}, u32[]{:S(2)}, u32[]{:S(2)}) collective-permute-start(bf16[1,768,2048]{2,1,0:T(8,128)(2,1)} %down_a.11), channel_id=1, source_target_pairs={{0,1},{1,0},{2,3},{3,2},{4,5},{5,4},{6,7},{7,6},{8,9},{9,8},{10,11... | collective-permute-start | bytes 9437192 | tf_op jit(solution)/shard_map/ppermute | solution.py:476
  32.6 9.2 %collective-permute-start.2 = (bf16[64,2048]{1,0:T(8,128)(2,1)S(1)}, bf16[64,2048]{1,0:T(8,128)(2,1)S(1)}, u32[]{:S(2)}, u32[]{:S(2)}) collective-permute-start(bf16[64,2048]{1,0:T(8,128)(2,1)S(1)} %get-tuple-element.83.refs_0_), channel_id=1, source_target_pairs={{0,4},{1,5},{4,8},{5,9},{8,12},{9,13},{12,14},{13,15},{14,10},{15,... | collective-permute-start | bytes 786440 | tf_op jit(solution)/shard_map/ppermute | solution.py:474
  33.3 9.2 %collective-permute-start.3 = (bf16[64,2048]{1,0:T(8,128)(2,1)S(1)}, bf16[64,2048]{1,0:T(8,128)(2,1)S(1)}, u32[]{:S(2)}, u32[]{:S(2)}) collective-permute-start(bf16[64,2048]{1,0:T(8,128)(2,1)S(1)} %get-tuple-element.84.refs_1_), channel_id=1, source_target_pairs={{4,0},{5,1},{8,4},{9,5},{12,8},{13,9},{14,12},{15,13},{10,14},{11,... | collective-permute-start | bytes 786440 | tf_op jit(solution)/shard_map/ppermute | solution.py:475
  34.7 13.4 %collective-permute-start.5 = (bf16[64,2048]{1,0:T(8,128)(2,1)S(1)}, bf16[64,2048]{1,0:T(8,128)(2,1)S(1)}, u32[]{:S(2)}, u32[]{:S(2)}) collective-permute-start(bf16[64,2048]{1,0:T(8,128)(2,1)S(1)} %get-tuple-element.83.refs_0_), channel_id=1, source_target_pairs={{4,0},{5,1},{8,4},{9,5},{12,8},{13,9},{14,12},{15,13},{10,14},{11,... | collective-permute-start | bytes 786440 | tf_op jit(solution)/shard_map/ppermute | solution.py:475
  35.3 12.8 %collective-permute-start.4 = (bf16[64,2048]{1,0:T(8,128)(2,1)S(1)}, bf16[64,2048]{1,0:T(8,128)(2,1)S(1)}, u32[]{:S(2)}, u32[]{:S(2)}) collective-permute-start(bf16[64,2048]{1,0:T(8,128)(2,1)S(1)} %get-tuple-element.84.refs_1_), channel_id=1, source_target_pairs={{0,4},{1,5},{4,8},{5,9},{8,12},{9,13},{12,14},{13,15},{14,10},{15,... | collective-permute-start | bytes 786440 | tf_op jit(solution)/shard_map/ppermute | solution.py:474
  42.5 11.2 %collective-permute-start.8 = (bf16[64,2048]{1,0:T(8,128)(2,1)S(1)}, bf16[64,2048]{1,0:T(8,128)(2,1)S(1)}, u32[]{:S(2)}, u32[]{:S(2)}) collective-permute-start(bf16[64,2048]{1,0:T(8,128)(2,1)S(1)} %get-tuple-element.90.refs_1_), channel_id=1, source_target_pairs={{4,0},{5,1},{8,4},{9,5},{12,8},{13,9},{14,12},{15,13},{10,14},{11,... | collective-permute-start | bytes 786440 | tf_op jit(solution)/shard_map/ppermute | solution.py:475
  43.9 9.9 %collective-permute-start.7 = (bf16[64,2048]{1,0:T(8,128)(2,1)S(1)}, bf16[64,2048]{1,0:T(8,128)(2,1)S(1)}, u32[]{:S(2)}, u32[]{:S(2)}) collective-permute-start(bf16[64,2048]{1,0:T(8,128)(2,1)S(1)} %get-tuple-element.92.refs_0_), channel_id=1, source_target_pairs={{0,4},{1,5},{4,8},{5,9},{8,12},{9,13},{12,14},{13,15},{14,10},{15,... | collective-permute-start | bytes 786440 | tf_op jit(solution)/shard_map/ppermute | solution.py:474
  48.1 11.2 %collective-permute-start.10 = (bf16[64,2048]{1,0:T(8,128)(2,1)S(1)}, bf16[64,2048]{1,0:T(8,128)(2,1)S(1)}, u32[]{:S(2)}, u32[]{:S(2)}) collective-permute-start(bf16[64,2048]{1,0:T(8,128)(2,1)S(1)} %get-tuple-element.89.refs_0_), channel_id=1, source_target_pairs={{4,0},{5,1},{8,4},{9,5},{12,8},{13,9},{14,12},{15,13},{10,14},{11,... | collective-permute-start | bytes 786440 | tf_op jit(solution)/shard_map/ppermute | solution.py:475
  49.5 9.9 %collective-permute-start.9 = (bf16[64,2048]{1,0:T(8,128)(2,1)S(1)}, bf16[64,2048]{1,0:T(8,128)(2,1)S(1)}, u32[]{:S(2)}, u32[]{:S(2)}) collective-permute-start(bf16[64,2048]{1,0:T(8,128)(2,1)S(1)} %get-tuple-element.94.refs_1_), channel_id=1, source_target_pairs={{0,4},{1,5},{4,8},{5,9},{8,12},{9,13},{12,14},{13,15},{14,10},{15,... | collective-permute-start | bytes 786440 | tf_op jit(solution)/shard_map/ppermute | solution.py:474
  53.8 12.8 %collective-permute-start.12 = (bf16[64,2048]{1,0:T(8,128)(2,1)S(1)}, bf16[64,2048]{1,0:T(8,128)(2,1)S(1)}, u32[]{:S(2)}, u32[]{:S(2)}) collective-permute-start(bf16[64,2048]{1,0:T(8,128)(2,1)S(1)} %get-tuple-element.98.refs_1_), channel_id=1, source_target_pairs={{4,0},{5,1},{8,4},{9,5},{12,8},{13,9},{14,12},{15,13},{10,14},{11,... | collective-permute-start | bytes 786440 | tf_op jit(solution)/shard_map/ppermute | solution.py:475
  55.1 11.4 %collective-permute-start.11 = (bf16[64,2048]{1,0:T(8,128)(2,1)S(1)}, bf16[64,2048]{1,0:T(8,128)(2,1)S(1)}, u32[]{:S(2)}, u32[]{:S(2)}) collective-permute-start(bf16[64,2048]{1,0:T(8,128)(2,1)S(1)} %get-tuple-element.99.refs_2_), channel_id=1, source_target_pairs={{0,4},{1,5},{4,8},{5,9},{8,12},{9,13},{12,14},{13,15},{14,10},{15,... | collective-permute-start | bytes 786440 | tf_op jit(solution)/shard_map/ppermute | solution.py:474
  59.4 11.3 %collective-permute-start.14 = (bf16[64,2048]{1,0:T(8,128)(2,1)S(1)}, bf16[64,2048]{1,0:T(8,128)(2,1)S(1)}, u32[]{:S(2)}, u32[]{:S(2)}) collective-permute-start(bf16[64,2048]{1,0:T(8,128)(2,1)S(1)} %get-tuple-element.97.refs_0_), channel_id=1, source_target_pairs={{4,0},{5,1},{8,4},{9,5},{12,8},{13,9},{14,12},{15,13},{10,14},{11,... | collective-permute-start | bytes 786440 | tf_op jit(solution)/shard_map/ppermute | solution.py:475
  60.8 9.9 %collective-permute-start.13 = (bf16[64,2048]{1,0:T(8,128)(2,1)S(1)}, bf16[64,2048]{1,0:T(8,128)(2,1)S(1)}, u32[]{:S(2)}, u32[]{:S(2)}) collective-permute-start(bf16[64,2048]{1,0:T(8,128)(2,1)S(1)} %get-tuple-element.100.refs_3_), channel_id=1, source_target_pairs={{0,4},{1,5},{4,8},{5,9},{8,12},{9,13},{12,14},{13,15},{14,10},{15,... | collective-permute-start | bytes 786440 | tf_op jit(solution)/shard_map/ppermute | solution.py:474
  66.6 10.2 %collective-permute-start.16 = (bf16[64,2048]{1,0:T(8,128)(2,1)S(1)}, bf16[64,2048]{1,0:T(8,128)(2,1)S(1)}, u32[]{:S(2)}, u32[]{:S(2)}) collective-permute-start(bf16[64,2048]{1,0:T(8,128)(2,1)S(1)} %get-tuple-element.103.refs_0_), channel_id=1, source_target_pairs={{4,0},{5,1},{8,4},{9,5},{12,8},{13,9},{14,12},{15,13},{10,14},{11,... | collective-permute-start | bytes 786440 | tf_op jit(solution)/shard_map/ppermute | solution.py:475
  68.0 8.8 %collective-permute-start.15 = (bf16[64,2048]{1,0:T(8,128)(2,1)S(1)}, bf16[64,2048]{1,0:T(8,128)(2,1)S(1)}, u32[]{:S(2)}, u32[]{:S(2)}) collective-permute-start(bf16[64,2048]{1,0:T(8,128)(2,1)S(1)} %get-tuple-element.104.refs_1_), channel_id=1, source_target_pairs={{0,4},{1,5},{4,8},{5,9},{8,12},{9,13},{12,14},{13,15},{14,10},{15,... | collective-permute-start | bytes 786440 | tf_op jit(solution)/shard_map/ppermute | solution.py:474
  79.7 9.3 %collective-permute-start.19 = (bf16[64,2048]{1,0:T(8,128)(2,1)S(1)}, bf16[64,2048]{1,0:T(8,128)(2,1)S(1)}, u32[]{:S(2)}, u32[]{:S(2)}) collective-permute-start(bf16[64,2048]{1,0:T(8,128)(2,1)S(1)} %get-tuple-element.124), channel_id=1, source_target_pairs={{0,4},{1,5},{4,8},{5,9},{8,12},{9,13},{12,14},{13,15},{14,10},{15,... | collective-permute-start | bytes 786440 | tf_op jit(solution)/shard_map/ppermute | solution.py:474
  80.5 9.2 %collective-permute-start.20 = (bf16[64,2048]{1,0:T(8,128)(2,1)S(1)}, bf16[64,2048]{1,0:T(8,128)(2,1)S(1)}, u32[]{:S(2)}, u32[]{:S(2)}) collective-permute-start(bf16[64,2048]{1,0:T(8,128)(2,1)S(1)} %get-tuple-element.125), channel_id=1, source_target_pairs={{4,0},{5,1},{8,4},{9,5},{12,8},{13,9},{14,12},{15,13},{10,14},{11,... | collective-permute-start | bytes 786440 | tf_op jit(solution)/shard_map/ppermute | solution.py:475
  84.2 10.4 %collective-permute-start.21 = (bf16[64,2048]{1,0:T(8,128)(2,1)S(1)}, bf16[64,2048]{1,0:T(8,128)(2,1)S(1)}, u32[]{:S(2)}, u32[]{:S(2)}) collective-permute-start(bf16[64,2048]{1,0:T(8,128)(2,1)S(1)} %get-tuple-element.129), channel_id=1, source_target_pairs={{0,4},{1,5},{4,8},{5,9},{8,12},{9,13},{12,14},{13,15},{14,10},{15,... | collective-permute-start | bytes 786440 | tf_op jit(solution)/shard_map/ppermute | solution.py:474
  85.2 10.2 %collective-permute-start.22 = (bf16[64,2048]{1,0:T(8,128)(2,1)S(1)}, bf16[64,2048]{1,0:T(8,128)(2,1)S(1)}, u32[]{:S(2)}, u32[]{:S(2)}) collective-permute-start(bf16[64,2048]{1,0:T(8,128)(2,1)S(1)} %get-tuple-element.130), channel_id=1, source_target_pairs={{4,0},{5,1},{8,4},{9,5},{12,8},{13,9},{14,12},{15,13},{10,14},{11,... | collective-permute-start | bytes 786440 | tf_op jit(solution)/shard_map/ppermute | solution.py:475
  89.9 10.3 %collective-permute-start.23 = (bf16[64,2048]{1,0:T(8,128)(2,1)S(1)}, bf16[64,2048]{1,0:T(8,128)(2,1)S(1)}, u32[]{:S(2)}, u32[]{:S(2)}) collective-permute-start(bf16[64,2048]{1,0:T(8,128)(2,1)S(1)} %get-tuple-element.132), channel_id=1, source_target_pairs={{0,4},{1,5},{4,8},{5,9},{8,12},{9,13},{12,14},{13,15},{14,10},{15,... | collective-permute-start | bytes 786440 | tf_op jit(solution)/shard_map/ppermute | solution.py:474
  91.1 9.9 %collective-permute-start.24 = (bf16[64,2048]{1,0:T(8,128)(2,1)S(1)}, bf16[64,2048]{1,0:T(8,128)(2,1)S(1)}, u32[]{:S(2)}, u32[]{:S(2)}) collective-permute-start(bf16[64,2048]{1,0:T(8,128)(2,1)S(1)} %get-tuple-element.133), channel_id=1, source_target_pairs={{4,0},{5,1},{8,4},{9,5},{12,8},{13,9},{14,12},{15,13},{10,14},{11,... | collective-permute-start | bytes 786440 | tf_op jit(solution)/shard_map/ppermute | solution.py:475
  95.5 10.5 %collective-permute-start.25 = (bf16[64,2048]{1,0:T(8,128)(2,1)S(1)}, bf16[64,2048]{1,0:T(8,128)(2,1)S(1)}, u32[]{:S(2)}, u32[]{:S(2)}) collective-permute-start(bf16[64,2048]{1,0:T(8,128)(2,1)S(1)} %get-tuple-element.136), channel_id=1, source_target_pairs={{0,4},{1,5},{4,8},{5,9},{8,12},{9,13},{12,14},{13,15},{14,10},{15,... | collective-permute-start | bytes 786440 | tf_op jit(solution)/shard_map/ppermute | solution.py:474
  96.7 9.9 %collective-permute-start.26 = (bf16[64,2048]{1,0:T(8,128)(2,1)S(1)}, bf16[64,2048]{1,0:T(8,128)(2,1)S(1)}, u32[]{:S(2)}, u32[]{:S(2)}) collective-permute-start(bf16[64,2048]{1,0:T(8,128)(2,1)S(1)} %get-tuple-element.137), channel_id=1, source_target_pairs={{4,0},{5,1},{8,4},{9,5},{12,8},{13,9},{14,12},{15,13},{10,14},{11,... | collective-permute-start | bytes 786440 | tf_op jit(solution)/shard_map/ppermute | solution.py:475
  (12 other events, 104.6 us)

commit v7 on v6

--- a/solution.py
+++ b/solution.py
@@ -169,7 +169,7 @@
         + [jax.ShapeDtypeStruct(row, F32)] * batches,
         in_specs=[whole] * 3,
         out_specs=[whole] * (2 + batches),
-        compiler_params=pltpu.CompilerParams(vmem_limit_bytes=8 << 20),
+        compiler_params=pltpu.CompilerParams(vmem_limit_bytes=4 << 20),
         name="prepare",
     )(arrived, residual, norm_gain.reshape(1, model_width))
     return left, right, streams
@@ -234,7 +234,7 @@
         in_specs=[whole] * (3 + len(halves)),
         out_specs=[whole] * 3,
         scratch_shapes=[pltpu.VMEM((rows, width // 2), BF16)],
-        compiler_params=pltpu.CompilerParams(vmem_limit_bytes=8 << 20),
+        compiler_params=pltpu.CompilerParams(vmem_limit_bytes=4 << 20),
         cost_estimate=pl.CostEstimate(flops=1, bytes_accessed=1, transcendentals=0),
         name="begin",
     )(token, *weights[:2], *halves)
@@ -323,7 +323,7 @@
             pltpu.VMEM((rows, hidden_width), BF16),
             pltpu.VMEM((rows, hidden_width), BF16),
         ],
-        compiler_params=pltpu.CompilerParams(vmem_limit_bytes=10 << 20),
+        compiler_params=pltpu.CompilerParams(vmem_limit_bytes=6 << 20),
         cost_estimate=pl.CostEstimate(flops=1, bytes_accessed=1, transcendentals=0),
         name="experts",
     )(me, token, *shares, *weights, *held, *begun)
@@ -411,7 +411,7 @@
         out_shape=[jax.ShapeDtypeStruct(token.shape, token.dtype), part, part],
         in_specs=[whole] * (3 + len(moving)),
         out_specs=[whole] * 3,
-        compiler_params=pltpu.CompilerParams(vmem_limit_bytes=4 << 20),
+        compiler_params=pltpu.CompilerParams(vmem_limit_bytes=2 << 20),
         cost_estimate=pl.CostEstimate(flops=1, bytes_accessed=1, transcendentals=0),
         name="merge",
     )(token, *terms, *moving)
@@ -446,7 +446,7 @@
         in_specs=[whole] * (2 + len(streams) + len(sums)),
         out_specs=pl.BlockSpec(memory_space=pl.ANY),
         scratch_shapes=[pltpu.VMEM(shape, BF16), pltpu.SemaphoreType.DMA((len(streams),))],
-        compiler_params=pltpu.CompilerParams(vmem_limit_bytes=8 << 20),
+        compiler_params=pltpu.CompilerParams(vmem_limit_bytes=4 << 20),
         name="finish",
     )(token, terms, *streams, *sums)
 

time: 119 us -> 119 us (level)
  no operation moved by 1% of the time
where the time goes in v7:
time: 119 us
  Pallas kernels  33.5 us (28%)
  waiting for transfers between devices  29.9 us (25%)
  starting transfers between devices  29.4 us (25%)
  blocking collectives  24.5 us (21%)
  local copies, waits for them, and re-layouts  1.27 us (1%)
    all_to_all x1, blocking collectives, body(): lax.all_to_all(rows.reshape(devices, -1, rows.shape[-1]), 'dev', split_ax...  24.5 us
    pallas_call x6, Pallas kernels, run_experts(): pl.pallas_call(functools.partial(expert_kernel, places=places, sides=side...  20.4 us
    ppermute x14, waiting for transfers between devices, body(): send_ahead = lambda x: lax.ppermute(x, 'dev', forward)  17.9 us
    ppermute x14, starting transfers between devices, body(): send_behind = lambda x: lax.ppermute(x, 'dev', backward)  16 us
    ppermute x14, starting transfers between devices, body(): send_ahead = lambda x: lax.ppermute(x, 'dev', forward)  12.8 us
    ppermute x14, waiting for transfers between devices, body(): send_behind = lambda x: lax.ppermute(x, 'dev', backward)  12 us
    pallas_call x1, Pallas kernels, attend(): pl.pallas_call(functools.partial(attend_kernel, devices=devices), out_sha...  6.08 us
    pallas_call x1, Pallas kernels, load(): pl.pallas_call(load_kernel, out_shape=[jax.ShapeDtypeStruct(x.shape, x.dt...  2.94 us
  transfers between devices with their start and end apart: 31, of which 18 were waited for; matrix products, arithmetic and copies ran while one was open for 0% of the time, Pallas kernels for 27%

profile of v7, /device:TPU:0, one launch (start us, length us, event | category | flops | bytes accessed | tf_op | source)
XLA Modules:
  0.0 119.0 jit_solution(8457467630257130887)
XLA Ops:
  0.5 6.1 %attend.1 = bf16[16,2,8,1152]{3,2,1,0:T(8,128)(2,1)S(1)} custom-call(bf16[2,1,128,1024]{3,2,1,0:T(8,128)(2,1)} %q_ref, bf16[2,1,2,1664,128]{4,3,2,1,0:T(8,128)(2,1)} %kv_ref.1, s32[2,8,64]{2,1,0:T(8,128)} %bitcast.15, s32[2,8,64]{2,1,0:T(8,128)} %bitcast.16), custom_call_target="tpu_custom_call" | custom-call | flops 1744830464 | bytes 2752512 | tf_op jit(solution)/shard_map/attend/pallas_call | solution.py:108
  6.6 24.5 %all_to_all.5.refs_0_ = bf16[16,16,1152]{2,1,0:T(8,128)(2,1)S(1)} all-to-all(bf16[16,16,1152]{2,1,0:T(8,128)(2,1)S(1)} %bitcast.12), channel_id=1, replica_groups=mesh['groups'=2,'dev'=16] {'dev'}, dimensions={0} | all-to-all | bytes 1179648 | tf_op jit(solution)/shard_map/all_to_all | solution.py:481
  33.3 1.4 %collective-permute-start.3 = (bf16[64,2048]{1,0:T(8,128)(2,1)S(1)}, bf16[64,2048]{1,0:T(8,128)(2,1)S(1)}, u32[]{:S(2)}, u32[]{:S(2)}) collective-permute-start(bf16[64,2048]{1,0:T(8,128)(2,1)S(1)} %get-tuple-element.84.refs_1_), channel_id=1, source_target_pairs={{4,0},{5,1},{8,4},{9,5},{12,8},{13,9},{14,12},{15,13},{10,14},{11,... | collective-permute-start | bytes 786440 | tf_op jit(solution)/shard_map/ppermute | solution.py:475
  35.3 1.4 %collective-permute-start.4 = (bf16[64,2048]{1,0:T(8,128)(2,1)S(1)}, bf16[64,2048]{1,0:T(8,128)(2,1)S(1)}, u32[]{:S(2)}, u32[]{:S(2)}) collective-permute-start(bf16[64,2048]{1,0:T(8,128)(2,1)S(1)} %get-tuple-element.84.refs_1_), channel_id=1, source_target_pairs={{0,4},{1,5},{4,8},{5,9},{8,12},{9,13},{12,14},{13,15},{14,10},{15,... | collective-permute-start | bytes 786440 | tf_op jit(solution)/shard_map/ppermute | solution.py:474
  36.7 2.9 %load.1 = (f32[16,128]{1,0:T(8,128)S(1)}, bf16[1,2048,1536]{2,1,0:T(8,128)(2,1)S(1)}) custom-call(f32[16,128]{1,0:T(8,128)S(1)} %get-tuple-element.79.token_ref, bf16[1,2048,1536]{2,1,0:T(8,128)(2,1)} %get-tuple-element.80.refs_0_), custom_call_target="tpu_custom_call" | custom-call | flops 1 | bytes 1 | tf_op jit(solution)/shard_map/load/pallas_call | solution.py:349
  39.7 2.1 %collective-permute-done.2.refs_0_ = bf16[64,2048]{1,0:T(8,128)(2,1)S(1)} collective-permute-done((bf16[64,2048]{1,0:T(8,128)(2,1)S(1)}, bf16[64,2048]{1,0:T(8,128)(2,1)S(1)}, u32[]{:S(2)}, u32[]{:S(2)}) %collective-permute-start.2) | collective-permute-done | bytes 262176 | tf_op jit(solution)/shard_map/ppermute | solution.py:474
  44.8 3.4 %collective-permute-done.5.refs_1_ = bf16[64,2048]{1,0:T(8,128)(2,1)S(1)} collective-permute-done((bf16[64,2048]{1,0:T(8,128)(2,1)S(1)}, bf16[64,2048]{1,0:T(8,128)(2,1)S(1)}, u32[]{:S(2)}, u32[]{:S(2)}) %collective-permute-start.5) | collective-permute-done | bytes 262176 | tf_op jit(solution)/shard_map/ppermute | solution.py:475
  48.2 1.4 %collective-permute-start.10 = (bf16[64,2048]{1,0:T(8,128)(2,1)S(1)}, bf16[64,2048]{1,0:T(8,128)(2,1)S(1)}, u32[]{:S(2)}, u32[]{:S(2)}) collective-permute-start(bf16[64,2048]{1,0:T(8,128)(2,1)S(1)} %get-tuple-element.89.refs_0_), channel_id=1, source_target_pairs={{4,0},{5,1},{8,4},{9,5},{12,8},{13,9},{14,12},{15,13},{10,14},{11,... | collective-permute-start | bytes 786440 | tf_op jit(solution)/shard_map/ppermute | solution.py:475
  50.2 2.8 %experts.6 = (bf16[128,2048]{1,0:T(8,128)(2,1)S(1)}, f32[16,128]{1,0:T(8,128)S(1)}) custom-call(s32[1]{0:T(128)} %bitcast.me_ref, f32[16,128]{1,0:T(8,128)S(1)} %get-tuple-element.86.token_ref, f32[16,128]{1,0:T(8,128)S(1)} %add_bitcast_fusion.share_a, f32[16,128]{1,0:T(8,128)S(1)} %collective-permute-done.6.share_b, bf16[1,2048,1536]{2,1,0:T(8,128)(2,1)S(1)} %bitcast.10, ...), custom_call_target="tpu_custom_call" | custom-call | flops 1 | bytes 1 | tf_op jit(solution)/shard_map/experts/pallas_call | solution.py:313
  53.8 1.4 %collective-permute-start.12 = (bf16[64,2048]{1,0:T(8,128)(2,1)S(1)}, bf16[64,2048]{1,0:T(8,128)(2,1)S(1)}, u32[]{:S(2)}, u32[]{:S(2)}) collective-permute-start(bf16[64,2048]{1,0:T(8,128)(2,1)S(1)} %get-tuple-element.98.refs_1_), channel_id=1, source_target_pairs={{4,0},{5,1},{8,4},{9,5},{12,8},{13,9},{14,12},{15,13},{10,14},{11,... | collective-permute-start | bytes 786440 | tf_op jit(solution)/shard_map/ppermute | solution.py:475
  55.8 2.8 %experts.7 = (bf16[128,2048]{1,0:T(8,128)(2,1)S(1)}, f32[16,128]{1,0:T(8,128)S(1)}) custom-call(s32[1]{0:T(128)} %bitcast.me_ref, f32[16,128]{1,0:T(8,128)S(1)} %get-tuple-element.93.token_ref, f32[16,128]{1,0:T(8,128)S(1)} %add_bitcast_fusion.share_a, f32[16,128]{1,0:T(8,128)S(1)} %collective-permute-done.6.share_b, bf16[1,2048,1536]{2,1,0:T(8,128)(2,1)S(1)} %bitcast.10, ...), custom_call_target="tpu_custom_call" | custom-call | flops 1 | bytes 1 | tf_op jit(solution)/shard_map/experts/pallas_call | solution.py:313
  59.4 1.4 %collective-permute-start.14 = (bf16[64,2048]{1,0:T(8,128)(2,1)S(1)}, bf16[64,2048]{1,0:T(8,128)(2,1)S(1)}, u32[]{:S(2)}, u32[]{:S(2)}) collective-permute-start(bf16[64,2048]{1,0:T(8,128)(2,1)S(1)} %get-tuple-element.97.refs_0_), channel_id=1, source_target_pairs={{4,0},{5,1},{8,4},{9,5},{12,8},{13,9},{14,12},{15,13},{10,14},{11,... | collective-permute-start | bytes 786440 | tf_op jit(solution)/shard_map/ppermute | solution.py:475
  61.4 5.2 %experts.8 = (bf16[256,2048]{1,0:T(8,128)(2,1)S(1)}, f32[16,128]{1,0:T(8,128)S(1)}) custom-call(s32[1]{0:T(128)} %bitcast.me_ref, f32[16,128]{1,0:T(8,128)S(1)} %get-tuple-element.96.token_ref, f32[16,128]{1,0:T(8,128)S(1)} %add_bitcast_fusion.share_a, f32[16,128]{1,0:T(8,128)S(1)} %collective-permute-done.6.share_b, bf16[1,2048,1536]{2,1,0:T(8,128)(2,1)S(1)} %bitcast.10, ...), custom_call_target="tpu_custom_call" | custom-call | flops 1 | bytes 1 | tf_op jit(solution)/shard_map/experts/pallas_call | solution.py:313
  66.6 1.4 %collective-permute-start.16 = (bf16[64,2048]{1,0:T(8,128)(2,1)S(1)}, bf16[64,2048]{1,0:T(8,128)(2,1)S(1)}, u32[]{:S(2)}, u32[]{:S(2)}) collective-permute-start(bf16[64,2048]{1,0:T(8,128)(2,1)S(1)} %get-tuple-element.103.refs_0_), channel_id=1, source_target_pairs={{4,0},{5,1},{8,4},{9,5},{12,8},{13,9},{14,12},{15,13},{10,14},{11,... | collective-permute-start | bytes 786440 | tf_op jit(solution)/shard_map/ppermute | solution.py:475
  68.7 1.9 %begin.1 = (f32[256,1536]{1,0:T(8,128)S(1)}, f32[256,1536]{1,0:T(8,128)S(1)}, f32[16,128]{1,0:T(8,128)S(1)}) custom-call(f32[16,128]{1,0:T(8,128)S(1)} %get-tuple-element.102.token_ref, bf16[1,2048,1536]{2,1,0:T(8,128)(2,1)S(1)} %bitcast.10, bf16[1,2048,1536]{2,1,0:T(8,128)(2,1)S(1)} %get-tuple-element.87.gate_up_b, ...), custom_call_target="tpu_custom_call" | custom-call | flops 1 | bytes 1 | tf_op jit(solution)/shard_map/begin/pallas_call | solution.py:230
  70.7 4.0 %experts.9 = (bf16[256,2048]{1,0:T(8,128)(2,1)S(1)}, f32[16,128]{1,0:T(8,128)S(1)}) custom-call(s32[1]{0:T(128)} %bitcast.me_ref, f32[16,128]{1,0:T(8,128)S(1)} %get-tuple-element.106.token_ref, f32[16,128]{1,0:T(8,128)S(1)} %add_bitcast_fusion.share_a, f32[16,128]{1,0:T(8,128)S(1)} %collective-permute-done.6.share_b, bf16[1,2048,1536]{2,1,0:T(8,128)(2,1)S(1)} %bitcast.10, ...), custom_call_target="tpu_custom_call" | custom-call | flops 1 | bytes 1 | tf_op jit(solution)/shard_map/experts/pallas_call | solution.py:313
  76.9 2.8 %experts.10 = (bf16[128,2048]{1,0:T(8,128)(2,1)S(1)}, f32[16,128]{1,0:T(8,128)S(1)}) custom-call(s32[1]{0:T(128)} %bitcast.me_ref, f32[16,128]{1,0:T(8,128)S(1)} %get-tuple-element.114.token_ref, f32[16,128]{1,0:T(8,128)S(1)} %add_bitcast_fusion.share_a, f32[16,128]{1,0:T(8,128)S(1)} %collective-permute-done.6.share_b, bf16[1,2048,1536]{2,1,0:T(8,128)(2,1)S(1)} %bitcast.10, ...), custom_call_target="tpu_custom_call" | custom-call | flops 1 | bytes 1 | tf_op jit(solution)/shard_map/experts/pallas_call | solution.py:313
  82.8 1.4 %collective-permute-done.18.refs_1_ = bf16[64,2048]{1,0:T(8,128)(2,1)S(1)} collective-permute-done((bf16[64,2048]{1,0:T(8,128)(2,1)S(1)}, bf16[64,2048]{1,0:T(8,128)(2,1)S(1)}, u32[]{:S(2)}, u32[]{:S(2)}) %collective-permute-start.18) | collective-permute-done | bytes 262176 | tf_op jit(solution)/shard_map/ppermute | solution.py:475
  86.4 2.6 %collective-permute-done.19.refs_0_ = bf16[64,2048]{1,0:T(8,128)(2,1)S(1)} collective-permute-done((bf16[64,2048]{1,0:T(8,128)(2,1)S(1)}, bf16[64,2048]{1,0:T(8,128)(2,1)S(1)}, u32[]{:S(2)}, u32[]{:S(2)}) %collective-permute-start.19) | collective-permute-done | bytes 262176 | tf_op jit(solution)/shard_map/ppermute | solution.py:474
  92.0 2.6 %collective-permute-done.21.refs_0_ = bf16[64,2048]{1,0:T(8,128)(2,1)S(1)} collective-permute-done((bf16[64,2048]{1,0:T(8,128)(2,1)S(1)}, bf16[64,2048]{1,0:T(8,128)(2,1)S(1)}, u32[]{:S(2)}, u32[]{:S(2)}) %collective-permute-start.21) | collective-permute-done | bytes 262176 | tf_op jit(solution)/shard_map/ppermute | solution.py:474
  97.7 2.6 %collective-permute-done.23.refs_0_ = bf16[64,2048]{1,0:T(8,128)(2,1)S(1)} collective-permute-done((bf16[64,2048]{1,0:T(8,128)(2,1)S(1)}, bf16[64,2048]{1,0:T(8,128)(2,1)S(1)}, u32[]{:S(2)}, u32[]{:S(2)}) %collective-permute-start.23) | collective-permute-done | bytes 262176 | tf_op jit(solution)/shard_map/ppermute | solution.py:474
  103.3 2.8 %experts.11 = (bf16[128,2048]{1,0:T(8,128)(2,1)S(1)}, f32[16,128]{1,0:T(8,128)S(1)}) custom-call(s32[1]{0:T(128)} %bitcast.me_ref, f32[16,128]{1,0:T(8,128)S(1)} %get-tuple-element.134.token_ref, f32[16,128]{1,0:T(8,128)S(1)} %add_bitcast_fusion.share_a, f32[16,128]{1,0:T(8,128)S(1)} %collective-permute-done.6.share_b, bf16[1,2048,1536]{2,1,0:T(8,128)(2,1)S(1)} %bitcast.10, ...), custom_call_target="tpu_custom_call" | custom-call | flops 1 | bytes 1 | tf_op jit(solution)/shard_map/experts/pallas_call | solution.py:313
  106.7 2.6 %collective-permute-done.27.refs_0_ = bf16[64,2048]{1,0:T(8,128)(2,1)S(1)} collective-permute-done((bf16[64,2048]{1,0:T(8,128)(2,1)S(1)}, bf16[64,2048]{1,0:T(8,128)(2,1)S(1)}, u32[]{:S(2)}, u32[]{:S(2)}) %collective-permute-start.27) | collective-permute-done | bytes 262176 | tf_op jit(solution)/shard_map/ppermute | solution.py:474
  112.3 4.3 %collective-permute-done.29.refs_2_ = bf16[64,2048]{1,0:T(8,128)(2,1)S(1)} collective-permute-done((bf16[64,2048]{1,0:T(8,128)(2,1)S(1)}, bf16[64,2048]{1,0:T(8,128)(2,1)S(1)}, u32[]{:S(2)}, u32[]{:S(2)}) %collective-permute-start.29) | collective-permute-done | bytes 262176 | tf_op jit(solution)/shard_map/ppermute | solution.py:474
  (80 shorter events, 32.7 us)
Async XLA Ops:
  0.0 31.1 %collective-permute-start = (bf16[1,2048,1536]{2,1,0:T(8,128)(2,1)}, bf16[1,2048,1536]{2,1,0:T(8,128)(2,1)}, u32[]{:S(2)}, u32[]{:S(2)}) collective-permute-start(bf16[1,2048,1536]{2,1,0:T(8,128)(2,1)} %gate_up_a.13), channel_id=1, source_target_pairs={{0,1},{1,0},{2,3},{3,2},{4,5},{5,4},{6,7},{7,6},{8,9},{9,8},{10,11... | collective-permute-start | bytes 18874376 | tf_op jit(solution)/shard_map/ppermute | solution.py:476
  0.5 30.6 %collective-permute-start.1 = (bf16[1,768,2048]{2,1,0:T(8,128)(2,1)}, bf16[1,768,2048]{2,1,0:T(8,128)(2,1)S(1)}, u32[]{:S(2)}, u32[]{:S(2)}) collective-permute-start(bf16[1,768,2048]{2,1,0:T(8,128)(2,1)} %down_a.11), channel_id=1, source_target_pairs={{0,1},{1,0},{2,3},{3,2},{4,5},{5,4},{6,7},{7,6},{8,9},{9,8},{10,11... | collective-permute-start | bytes 9437192 | tf_op jit(solution)/shard_map/ppermute | solution.py:476
  32.6 9.2 %collective-permute-start.2 = (bf16[64,2048]{1,0:T(8,128)(2,1)S(1)}, bf16[64,2048]{1,0:T(8,128)(2,1)S(1)}, u32[]{:S(2)}, u32[]{:S(2)}) collective-permute-start(bf16[64,2048]{1,0:T(8,128)(2,1)S(1)} %get-tuple-element.83.refs_0_), channel_id=1, source_target_pairs={{0,4},{1,5},{4,8},{5,9},{8,12},{9,13},{12,14},{13,15},{14,10},{15,... | collective-permute-start | bytes 786440 | tf_op jit(solution)/shard_map/ppermute | solution.py:474
  33.3 9.2 %collective-permute-start.3 = (bf16[64,2048]{1,0:T(8,128)(2,1)S(1)}, bf16[64,2048]{1,0:T(8,128)(2,1)S(1)}, u32[]{:S(2)}, u32[]{:S(2)}) collective-permute-start(bf16[64,2048]{1,0:T(8,128)(2,1)S(1)} %get-tuple-element.84.refs_1_), channel_id=1, source_target_pairs={{4,0},{5,1},{8,4},{9,5},{12,8},{13,9},{14,12},{15,13},{10,14},{11,... | collective-permute-start | bytes 786440 | tf_op jit(solution)/shard_map/ppermute | solution.py:475
  34.7 13.4 %collective-permute-start.5 = (bf16[64,2048]{1,0:T(8,128)(2,1)S(1)}, bf16[64,2048]{1,0:T(8,128)(2,1)S(1)}, u32[]{:S(2)}, u32[]{:S(2)}) collective-permute-start(bf16[64,2048]{1,0:T(8,128)(2,1)S(1)} %get-tuple-element.83.refs_0_), channel_id=1, source_target_pairs={{4,0},{5,1},{8,4},{9,5},{12,8},{13,9},{14,12},{15,13},{10,14},{11,... | collective-permute-start | bytes 786440 | tf_op jit(solution)/shard_map/ppermute | solution.py:475
  35.3 12.8 %collective-permute-start.4 = (bf16[64,2048]{1,0:T(8,128)(2,1)S(1)}, bf16[64,2048]{1,0:T(8,128)(2,1)S(1)}, u32[]{:S(2)}, u32[]{:S(2)}) collective-permute-start(bf16[64,2048]{1,0:T(8,128)(2,1)S(1)} %get-tuple-element.84.refs_1_), channel_id=1, source_target_pairs={{0,4},{1,5},{4,8},{5,9},{8,12},{9,13},{12,14},{13,15},{14,10},{15,... | collective-permute-start | bytes 786440 | tf_op jit(solution)/shard_map/ppermute | solution.py:474
  42.5 11.2 %collective-permute-start.8 = (bf16[64,2048]{1,0:T(8,128)(2,1)S(1)}, bf16[64,2048]{1,0:T(8,128)(2,1)S(1)}, u32[]{:S(2)}, u32[]{:S(2)}) collective-permute-start(bf16[64,2048]{1,0:T(8,128)(2,1)S(1)} %get-tuple-element.90.refs_1_), channel_id=1, source_target_pairs={{4,0},{5,1},{8,4},{9,5},{12,8},{13,9},{14,12},{15,13},{10,14},{11,... | collective-permute-start | bytes 786440 | tf_op jit(solution)/shard_map/ppermute | solution.py:475
  43.9 9.9 %collective-permute-start.7 = (bf16[64,2048]{1,0:T(8,128)(2,1)S(1)}, bf16[64,2048]{1,0:T(8,128)(2,1)S(1)}, u32[]{:S(2)}, u32[]{:S(2)}) collective-permute-start(bf16[64,2048]{1,0:T(8,128)(2,1)S(1)} %get-tuple-element.92.refs_0_), channel_id=1, source_target_pairs={{0,4},{1,5},{4,8},{5,9},{8,12},{9,13},{12,14},{13,15},{14,10},{15,... | collective-permute-start | bytes 786440 | tf_op jit(solution)/shard_map/ppermute | solution.py:474
  48.2 11.2 %collective-permute-start.10 = (bf16[64,2048]{1,0:T(8,128)(2,1)S(1)}, bf16[64,2048]{1,0:T(8,128)(2,1)S(1)}, u32[]{:S(2)}, u32[]{:S(2)}) collective-permute-start(bf16[64,2048]{1,0:T(8,128)(2,1)S(1)} %get-tuple-element.89.refs_0_), channel_id=1, source_target_pairs={{4,0},{5,1},{8,4},{9,5},{12,8},{13,9},{14,12},{15,13},{10,14},{11,... | collective-permute-start | bytes 786440 | tf_op jit(solution)/shard_map/ppermute | solution.py:475
  49.5 9.9 %collective-permute-start.9 = (bf16[64,2048]{1,0:T(8,128)(2,1)S(1)}, bf16[64,2048]{1,0:T(8,128)(2,1)S(1)}, u32[]{:S(2)}, u32[]{:S(2)}) collective-permute-start(bf16[64,2048]{1,0:T(8,128)(2,1)S(1)} %get-tuple-element.94.refs_1_), channel_id=1, source_target_pairs={{0,4},{1,5},{4,8},{5,9},{8,12},{9,13},{12,14},{13,15},{14,10},{15,... | collective-permute-start | bytes 786440 | tf_op jit(solution)/shard_map/ppermute | solution.py:474
  53.8 12.8 %collective-permute-start.12 = (bf16[64,2048]{1,0:T(8,128)(2,1)S(1)}, bf16[64,2048]{1,0:T(8,128)(2,1)S(1)}, u32[]{:S(2)}, u32[]{:S(2)}) collective-permute-start(bf16[64,2048]{1,0:T(8,128)(2,1)S(1)} %get-tuple-element.98.refs_1_), channel_id=1, source_target_pairs={{4,0},{5,1},{8,4},{9,5},{12,8},{13,9},{14,12},{15,13},{10,14},{11,... | collective-permute-start | bytes 786440 | tf_op jit(solution)/shard_map/ppermute | solution.py:475
  55.2 11.5 %collective-permute-start.11 = (bf16[64,2048]{1,0:T(8,128)(2,1)S(1)}, bf16[64,2048]{1,0:T(8,128)(2,1)S(1)}, u32[]{:S(2)}, u32[]{:S(2)}) collective-permute-start(bf16[64,2048]{1,0:T(8,128)(2,1)S(1)} %get-tuple-element.99.refs_2_), channel_id=1, source_target_pairs={{0,4},{1,5},{4,8},{5,9},{8,12},{9,13},{12,14},{13,15},{14,10},{15,... | collective-permute-start | bytes 786440 | tf_op jit(solution)/shard_map/ppermute | solution.py:474
  59.4 11.3 %collective-permute-start.14 = (bf16[64,2048]{1,0:T(8,128)(2,1)S(1)}, bf16[64,2048]{1,0:T(8,128)(2,1)S(1)}, u32[]{:S(2)}, u32[]{:S(2)}) collective-permute-start(bf16[64,2048]{1,0:T(8,128)(2,1)S(1)} %get-tuple-element.97.refs_0_), channel_id=1, source_target_pairs={{4,0},{5,1},{8,4},{9,5},{12,8},{13,9},{14,12},{15,13},{10,14},{11,... | collective-permute-start | bytes 786440 | tf_op jit(solution)/shard_map/ppermute | solution.py:475
  60.8 9.9 %collective-permute-start.13 = (bf16[64,2048]{1,0:T(8,128)(2,1)S(1)}, bf16[64,2048]{1,0:T(8,128)(2,1)S(1)}, u32[]{:S(2)}, u32[]{:S(2)}) collective-permute-start(bf16[64,2048]{1,0:T(8,128)(2,1)S(1)} %get-tuple-element.100.refs_3_), channel_id=1, source_target_pairs={{0,4},{1,5},{4,8},{5,9},{8,12},{9,13},{12,14},{13,15},{14,10},{15,... | collective-permute-start | bytes 786440 | tf_op jit(solution)/shard_map/ppermute | solution.py:474
  66.6 10.2 %collective-permute-start.16 = (bf16[64,2048]{1,0:T(8,128)(2,1)S(1)}, bf16[64,2048]{1,0:T(8,128)(2,1)S(1)}, u32[]{:S(2)}, u32[]{:S(2)}) collective-permute-start(bf16[64,2048]{1,0:T(8,128)(2,1)S(1)} %get-tuple-element.103.refs_0_), channel_id=1, source_target_pairs={{4,0},{5,1},{8,4},{9,5},{12,8},{13,9},{14,12},{15,13},{10,14},{11,... | collective-permute-start | bytes 786440 | tf_op jit(solution)/shard_map/ppermute | solution.py:475
  68.1 8.8 %collective-permute-start.15 = (bf16[64,2048]{1,0:T(8,128)(2,1)S(1)}, bf16[64,2048]{1,0:T(8,128)(2,1)S(1)}, u32[]{:S(2)}, u32[]{:S(2)}) collective-permute-start(bf16[64,2048]{1,0:T(8,128)(2,1)S(1)} %get-tuple-element.104.refs_1_), channel_id=1, source_target_pairs={{0,4},{1,5},{4,8},{5,9},{8,12},{9,13},{12,14},{13,15},{14,10},{15,... | collective-permute-start | bytes 786440 | tf_op jit(solution)/shard_map/ppermute | solution.py:474
  79.7 9.3 %collective-permute-start.19 = (bf16[64,2048]{1,0:T(8,128)(2,1)S(1)}, bf16[64,2048]{1,0:T(8,128)(2,1)S(1)}, u32[]{:S(2)}, u32[]{:S(2)}) collective-permute-start(bf16[64,2048]{1,0:T(8,128)(2,1)S(1)} %get-tuple-element.124), channel_id=1, source_target_pairs={{0,4},{1,5},{4,8},{5,9},{8,12},{9,13},{12,14},{13,15},{14,10},{15,... | collective-permute-start | bytes 786440 | tf_op jit(solution)/shard_map/ppermute | solution.py:474
  80.6 9.3 %collective-permute-start.20 = (bf16[64,2048]{1,0:T(8,128)(2,1)S(1)}, bf16[64,2048]{1,0:T(8,128)(2,1)S(1)}, u32[]{:S(2)}, u32[]{:S(2)}) collective-permute-start(bf16[64,2048]{1,0:T(8,128)(2,1)S(1)} %get-tuple-element.125), channel_id=1, source_target_pairs={{4,0},{5,1},{8,4},{9,5},{12,8},{13,9},{14,12},{15,13},{10,14},{11,... | collective-permute-start | bytes 786440 | tf_op jit(solution)/shard_map/ppermute | solution.py:475
  84.4 10.3 %collective-permute-start.21 = (bf16[64,2048]{1,0:T(8,128)(2,1)S(1)}, bf16[64,2048]{1,0:T(8,128)(2,1)S(1)}, u32[]{:S(2)}, u32[]{:S(2)}) collective-permute-start(bf16[64,2048]{1,0:T(8,128)(2,1)S(1)} %get-tuple-element.129), channel_id=1, source_target_pairs={{0,4},{1,5},{4,8},{5,9},{8,12},{9,13},{12,14},{13,15},{14,10},{15,... | collective-permute-start | bytes 786440 | tf_op jit(solution)/shard_map/ppermute | solution.py:474
  85.3 10.2 %collective-permute-start.22 = (bf16[64,2048]{1,0:T(8,128)(2,1)S(1)}, bf16[64,2048]{1,0:T(8,128)(2,1)S(1)}, u32[]{:S(2)}, u32[]{:S(2)}) collective-permute-start(bf16[64,2048]{1,0:T(8,128)(2,1)S(1)} %get-tuple-element.130), channel_id=1, source_target_pairs={{4,0},{5,1},{8,4},{9,5},{12,8},{13,9},{14,12},{15,13},{10,14},{11,... | collective-permute-start | bytes 786440 | tf_op jit(solution)/shard_map/ppermute | solution.py:475
  90.0 10.3 %collective-permute-start.23 = (bf16[64,2048]{1,0:T(8,128)(2,1)S(1)}, bf16[64,2048]{1,0:T(8,128)(2,1)S(1)}, u32[]{:S(2)}, u32[]{:S(2)}) collective-permute-start(bf16[64,2048]{1,0:T(8,128)(2,1)S(1)} %get-tuple-element.132), channel_id=1, source_target_pairs={{0,4},{1,5},{4,8},{5,9},{8,12},{9,13},{12,14},{13,15},{14,10},{15,... | collective-permute-start | bytes 786440 | tf_op jit(solution)/shard_map/ppermute | solution.py:474
  91.2 9.9 %collective-permute-start.24 = (bf16[64,2048]{1,0:T(8,128)(2,1)S(1)}, bf16[64,2048]{1,0:T(8,128)(2,1)S(1)}, u32[]{:S(2)}, u32[]{:S(2)}) collective-permute-start(bf16[64,2048]{1,0:T(8,128)(2,1)S(1)} %get-tuple-element.133), channel_id=1, source_target_pairs={{4,0},{5,1},{8,4},{9,5},{12,8},{13,9},{14,12},{15,13},{10,14},{11,... | collective-permute-start | bytes 786440 | tf_op jit(solution)/shard_map/ppermute | solution.py:475
  95.6 10.5 %collective-permute-start.25 = (bf16[64,2048]{1,0:T(8,128)(2,1)S(1)}, bf16[64,2048]{1,0:T(8,128)(2,1)S(1)}, u32[]{:S(2)}, u32[]{:S(2)}) collective-permute-start(bf16[64,2048]{1,0:T(8,128)(2,1)S(1)} %get-tuple-element.136), channel_id=1, source_target_pairs={{0,4},{1,5},{4,8},{5,9},{8,12},{9,13},{12,14},{13,15},{14,10},{15,... | collective-permute-start | bytes 786440 | tf_op jit(solution)/shard_map/ppermute | solution.py:474
  96.8 9.9 %collective-permute-start.26 = (bf16[64,2048]{1,0:T(8,128)(2,1)S(1)}, bf16[64,2048]{1,0:T(8,128)(2,1)S(1)}, u32[]{:S(2)}, u32[]{:S(2)}) collective-permute-start(bf16[64,2048]{1,0:T(8,128)(2,1)S(1)} %get-tuple-element.137), channel_id=1, source_target_pairs={{4,0},{5,1},{8,4},{9,5},{12,8},{13,9},{14,12},{15,13},{10,14},{11,... | collective-permute-start | bytes 786440 | tf_op jit(solution)/shard_map/ppermute | solution.py:475
  (12 other events, 104.7 us)
